TPU v7x, 32 devices: a whole 2x2x4 slice. The times are simulated.
32 devices in a mesh: tower: 2 (over x), grow: 4 (over y, core), gcol: 4 (over z).
Axes of the slice: x: 2, y: 2, z: 4, core: 2. Of those that a mesh axis runs over, the one named last changes fastest.
Arguments:
- hidden: bfloat16 [2, 4096, 768], P('tower', ('grow', 'gcol')), may hold values from -6 to 6
- preact: bfloat16 [2, 4096, 3072], P('tower', ('grow', 'gcol')), may hold values from -6 to 6
- w_down: bfloat16 [2, 768, 3072], P('tower', 'grow', 'gcol'), may hold values from -1 to 1
- projection: bfloat16 [2, 768, 768], P('tower', 'grow', 'gcol'), may hold values from -1 to 1
- log_scale: float32 [], replicated, may hold values from 4 to 6
Outputs:
- d_hidden: bfloat16 [2, 4096, 768], P('tower', ('grow', 'gcol'))
- d_preact: bfloat16 [2, 4096, 3072], P('tower', ('grow', 'gcol'))
- grad_down: float32 [2, 768, 3072], P('tower', 'grow', 'gcol')
- grad_proj: float32 [2, 768, 768], P('tower', 'grow', 'gcol')
All inputs are finite; a program needn't handle non-finite values.
Results may differ from a plain program's by a relative error of at most 0.006.
The roundings to bfloat16 on the way count: a program that leaves them out, or rounds other values in their place, can miss the bound.
Values may be sent and summed in bfloat16 or wider, within the bound.
No kernel may reach another device: no remote copies, remote signals or barrier semaphores. Data moves between devices by JAX's collectives and lax.ppermute only.
A program may use at most 128 MiB of HBM per device.

v0:
```python
import jax
import jax.numpy as jnp
from jax import lax
from jax.sharding import PartitionSpec as P


def combined_all(part, axis, combine):
    gathered = jax.tree.map(lambda a: lax.all_gather(a, axis), part)

    def take(source):
        return jax.tree.map(lambda a: lax.dynamic_index_in_dim(a, source, 0, False), gathered)

    return lax.fori_loop(
        1, lax.axis_size(axis), lambda source, state: combine(state, take(source)), take(0)
    )


def quick_gelu(values):
    return values * jax.nn.sigmoid(1.702 * values)


def gelu_slope(values):
    sigmoid = jax.nn.sigmoid(1.702 * values)
    return sigmoid + 1.702 * values * sigmoid * (1.0 - sigmoid)


def combine_totals(earlier, later):
    joint_max = jnp.maximum(earlier[0], later[0])
    return (
        joint_max,
        earlier[1] * jnp.exp(earlier[0] - joint_max) + later[1] * jnp.exp(later[0] - joint_max),
    )


def tile_whole(blocks, grow_count, gcol_count):
    height = blocks.shape[1]
    breadth = blocks.shape[2]
    return (
        blocks.reshape(grow_count, gcol_count, height, breadth)
        .transpose(0, 2, 1, 3)
        .reshape(grow_count * height, gcol_count * breadth)
    )


def split_blocks(whole, grow_count, gcol_count):
    height = whole.shape[0] // grow_count
    breadth = whole.shape[1] // gcol_count
    return (
        whole.reshape(grow_count, height, gcol_count, breadth)
        .transpose(0, 2, 1, 3)
        .reshape(grow_count * gcol_count, height, breadth)
    )


def body(hidden, preact, w_down, projection, log_scale):
    grow_count = lax.axis_size("grow")
    gcol_count = lax.axis_size("gcol")
    down_all, proj_all = (
        lax.all_gather(w_down, ("grow", "gcol"), axis=0, tiled=True),
        lax.all_gather(projection, ("grow", "gcol"), axis=0, tiled=True),
    )
    down_full = tile_whole(down_all, grow_count, gcol_count)
    proj_full = tile_whole(proj_all, grow_count, gcol_count)
    preact_local = preact[0].astype(jnp.float32)
    active = quick_gelu(preact_local).astype(jnp.bfloat16)
    stream = hidden[0].astype(jnp.float32) + lax.dot_general(
        active, down_full, (((1,), (1,)), ((), ())), preferred_element_type=jnp.float32
    )
    stream_b = stream.astype(jnp.bfloat16)
    embed = jnp.dot(stream_b, proj_full, preferred_element_type=jnp.float32)
    inverse = lax.rsqrt(jnp.sum(embed * embed, axis=1, keepdims=True) + 1e-06)
    unit = embed * inverse
    halves = lax.all_to_all(
        unit.astype(jnp.bfloat16)[None], "tower", split_axis=1, concat_axis=0, tiled=True
    )
    image_rows = lax.all_gather(halves[0], "gcol", axis=0, tiled=True)
    text_rows = lax.all_gather(halves[1], ("tower", "grow"), axis=0, tiled=True)
    logit_scale = jnp.exp(log_scale)
    scores = logit_scale * lax.dot_general(
        image_rows, text_rows, (((1,), (1,)), ((), ())), preferred_element_type=jnp.float32
    )
    row_max = jnp.max(scores, axis=1)
    row_sum = jnp.sum(jnp.exp(scores - row_max[:, None]), axis=1)
    column_max = jnp.max(scores, axis=0)
    column_sum = jnp.sum(jnp.exp(scores - column_max[None, :]), axis=0)
    row_max, row_sum = combined_all((row_max, row_sum), "gcol", combine_totals)
    column_max, column_sum = combined_all(
        (column_max, column_sum), ("tower", "grow"), combine_totals
    )
    row_lse = row_max + jnp.log(row_sum)
    column_lse = column_max + jnp.log(column_sum)
    half_rows = unit.shape[0] // 2
    row_index = lax.broadcasted_iota(jnp.int32, scores.shape, 0)
    column_index = lax.broadcasted_iota(jnp.int32, scores.shape, 1)
    grid_row = lax.axis_index("tower") * grow_count + lax.axis_index("grow")
    diagonal = (
        (row_index // half_rows == lax.axis_index("gcol"))
        & (column_index // half_rows == grid_row)
        & (row_index % half_rows == column_index % half_rows)
    )
    grad = 0.5 * (
        jnp.exp(scores - row_lse[:, None]) + jnp.exp(scores - column_lse[None, :])
    ) - diagonal.astype(jnp.float32)
    grad_b = grad.astype(jnp.bfloat16)
    block = grad_b
    image_grad = lax.psum_scatter(
        logit_scale * jnp.dot(block, text_rows, preferred_element_type=jnp.float32),
        "gcol",
        scatter_dimension=0,
        tiled=True,
    )
    block = grad_b
    text_grad = lax.psum_scatter(
        logit_scale
        * lax.dot_general(
            block, image_rows, (((0,), (0,)), ((), ())), preferred_element_type=jnp.float32
        ),
        ("tower", "grow"),
        scatter_dimension=0,
        tiled=True,
    )
    d_unit = lax.all_to_all(
        jnp.stack([image_grad, text_grad]), "tower", split_axis=0, concat_axis=1, tiled=True
    )[0]
    inner = jnp.sum(unit * d_unit, axis=1, keepdims=True)
    d_embed = (inverse * (d_unit - unit * inner)).astype(jnp.bfloat16)
    d_stream = lax.dot_general(
        d_embed, proj_full, (((1,), (1,)), ((), ())), preferred_element_type=jnp.float32
    ).astype(jnp.bfloat16)
    d_active = jnp.dot(d_stream, down_full, preferred_element_type=jnp.float32)
    d_pre = (d_active * gelu_slope(preact_local)).astype(jnp.bfloat16)
    term_down = lax.dot_general(
        d_stream, active, (((0,), (0,)), ((), ())), preferred_element_type=jnp.float32
    )
    term_proj = lax.dot_general(
        stream_b, d_embed, (((0,), (0,)), ((), ())), preferred_element_type=jnp.float32
    )
    down_part, proj_part = (
        lax.psum_scatter(
            split_blocks(term_down, grow_count, gcol_count),
            ("grow", "gcol"),
            scatter_dimension=0,
            tiled=True,
        ),
        lax.psum_scatter(
            split_blocks(term_proj, grow_count, gcol_count),
            ("grow", "gcol"),
            scatter_dimension=0,
            tiled=True,
        ),
    )
    return (d_stream[None], d_pre[None], down_part, proj_part)


def solution(mesh):
    placed = (
        P("tower", ("grow", "gcol"), None),
        P("tower", ("grow", "gcol"), None),
        P("tower", "grow", "gcol"),
        P("tower", "grow", "gcol"),
        P(),
    )
    return jax.shard_map(
        body,
        mesh=mesh,
        in_specs=placed,
        out_specs=(
            P("tower", ("grow", "gcol"), None),
            P("tower", ("grow", "gcol"), None),
            P("tower", "grow", "gcol"),
            P("tower", "grow", "gcol"),
        ),
        check_vma=False,
    )
```

profile of v0, /device:TPU:9, one launch (start us, length us, event | category | flops | bytes accessed | tf_op | source)
XLA Modules:
  0.0 499.5 jit_solution(1786979404935225360)
XLA Ops:
  8.7 41.9 %all-gather.14.cloned.1.call-done = bf16[16,192,192]{2,1,0:T(8,128)(2,1)} async-done(((bf16[1,192,192]{2,1,0:T(8,128)(2,1)}), bf16[16,192,192]{2,1,0:T(8,128)(2,1)}) %all-gather.14.cloned.1.call-update) | async-done | bytes 1179664 | tf_op jit(solution)/shard_map/all_gather | solution.py:60
  50.6 2.6 copy.41
  53.2 1.4 reshape.62
  54.6 51.6 %all-gather.12.cloned.1.call-done = bf16[16,192,768]{2,1,0:T(8,128)(2,1)} async-done(((bf16[1,192,768]{2,1,0:T(8,128)(2,1)}), bf16[16,192,768]{2,1,0:T(8,128)(2,1)}) %all-gather.12.cloned.1.call-update) | async-done | bytes 4718608 | tf_op jit(solution)/shard_map/all_gather | solution.py:59
  106.3 6.0 %copy.23 = bf16[4,4,192,768]{3,1,2,0:T(4,128)(2,1)S(1)} copy(bf16[4,4,192,768]{3,2,1,0:T(8,128)(2,1)} %bitcast.147) | data formatting | bytes 9437184 | tf_op jit(solution)/shard_map/reshape | solution.py:39
  113.7 2.0 fusion.34
  117.5 3.0 reduce
  120.7 8.7 %all_to_all.21 = bf16[2,2,49152]{2,1,0:T(2,128)(2,1)S(1)} all-to-all(bf16[2,2,49152]{2,1,0:T(2,128)(2,1)S(1)} %reshape.92), channel_id=1, replica_groups=mesh['tower'=2,'grow'=4,'gcol'=4] {'tower'}, dimensions={0} | all-to-all | bytes 786432 | tf_op jit(solution)/shard_map/all_to_all | solution.py:73
  132.0 14.1 %all-gather = bf16[1,1,512,768]{3,2,1,0:T(8,128)(2,1)} all-gather(bf16[1,1,128,768]{3,2,1,0:T(8,128)(2,1)S(1)} %slice.20), channel_id=2, replica_groups=mesh['tower'=2,'grow'=4,'gcol'=4] {'gcol'}, dimensions={2}, use_global_device_ids=true | all-gather | bytes 983040 | tf_op jit(solution)/shard_map/all_gather | solution.py:76
  146.1 9.2 %all-gather.16.cloned.1.call-done = bf16[1,1024,768]{2,1,0:T(8,128)(2,1)} async-done(((bf16[1,128,768]{2,1,0:T(8,128)(2,1)}), bf16[1,1024,768]{2,1,0:T(8,128)(2,1)}) %all-gather.16.cloned.1.call-update) | async-done | bytes 1572880 | tf_op jit(solution)/shard_map/all_gather | solution.py:77
  155.3 2.8 fusion.57
  158.1 9.1 %all-gather.4 = f32[8192]{0:T(1024)S(1)} all-gather(f32[1024]{0:T(1024)S(1)} %get-tuple-element.277), channel_id=6, replica_groups=mesh['tower'=2,'grow'=4,'gcol'=4] {'tower','grow'}, dimensions={0}, use_global_device_ids=true | all-gather | bytes 36864 | tf_op jit(solution)/shard_map/all_gather | solution.py:8
  167.9 8.1 %all-gather.5 = f32[8192]{0:T(1024)S(1)} all-gather(f32[1024]{0:T(1024)S(1)} %get-tuple-element.275), channel_id=7, replica_groups=mesh['tower'=2,'grow'=4,'gcol'=4] {'tower','grow'}, dimensions={0}, use_global_device_ids=true | all-gather | bytes 36864 | tf_op jit(solution)/shard_map/all_gather | solution.py:8
  176.0 9.3 %all-gather.6 = f32[4,1,512]{2,1,0:T(1,128)S(1)} all-gather(f32[1,1,512]{2,1,0:T(1,128)S(1)} %bitcast.164), channel_id=4, replica_groups=mesh['tower'=2,'grow'=4,'gcol'=4] {'gcol'}, dimensions={0}, use_global_device_ids=true | all-gather | bytes 10240 | tf_op jit(solution)/shard_map/all_gather | solution.py:8
  185.4 8.3 %all-gather.7 = f32[4,1,512]{2,1,0:T(1,128)S(1)} all-gather(f32[1,1,512]{2,1,0:T(1,128)S(1)} %bitcast.165), channel_id=5, replica_groups=mesh['tower'=2,'grow'=4,'gcol'=4] {'gcol'}, dimensions={0}, use_global_device_ids=true | all-gather | bytes 10240 | tf_op jit(solution)/shard_map/all_gather | solution.py:8
  194.3 2.5 subtract_convert_fusion
  196.8 3.4 fusion.28
  200.3 3.9 convolution_multiply_fusion.1
  204.2 32.8 %reduce-scatter.5.cloned.1.call-done = f32[128,768]{1,0:T(8,128)} async-done(((f32[512,768]{1,0:T(8,128)}), f32[128,768]{1,0:T(8,128)}) %reduce-scatter.5.cloned.1.call-update) | async-done | bytes 393232 | tf_op jit(solution)/shard_map/reduce_scatter | solution.py:106
  237.0 50.4 %reduce-scatter.7.cloned.1.call-done = f32[128,768]{1,0:T(8,128)} async-done(((f32[1024,768]{1,0:T(8,128)}), f32[128,768]{1,0:T(8,128)}) %reduce-scatter.7.cloned.1.call-update) | async-done | bytes 393232 | tf_op jit(solution)/shard_map/reduce_scatter | solution.py:113
  287.4 1.2 pad_maximum_fusion
  288.5 12.6 %all_to_all.22 = f32[2,128,768]{2,1,0:T(8,128)S(1)} all-to-all(f32[2,128,768]{2,1,0:T(8,128)S(1)} %pad_maximum_fusion), channel_id=1, replica_groups=mesh['tower'=2,'grow'=4,'gcol'=4] {'tower'}, dimensions={0} | all-to-all | bytes 1572864 | tf_op jit(solution)/shard_map/all_to_all | solution.py:122
  302.1 1.9 fusion.59
  304.0 3.6 reshape.64
  307.7 2.2 copy.29
  310.2 2.3 fusion.22
  312.5 1.6 copy.31
  315.5 5.1 %fusion.58 = f32[4,192,4,768]{3,1,2,0:T(8,128)} fusion(bf16[4,192,256,1]{2,1,3,0:T(8,128)(2,1)S(1)} %bitcast.149, bf16[4,768,256,1]{2,1,0,3:T(8,128)(2,1)S(1)} %bitcast.142), kind=kOutput, calls=%fused_computation.90 | convolution fusion | flops 1207959552 | bytes 11403264 | tf_op jit(solution)/shard_map/dot_general | solution.py:132
  320.6 1.4 copy-done.6
  322.0 5.7 %fusion.5 = bf16[1,256,3072]{2,1,0:T(8,128)(2,1)} fusion(bf16[256,768]{1,0:T(8,128)(2,1)S(1)} %convolution_convert_fusion, bf16[768,3072]{1,0:T(8,128)(2,1)} %bitcast.146, bf16[1,256,3072]{2,1,0:T(8,128)(2,1)S(1)} %copy-done.6), kind=kOutput, calls=%fused_computation.15 | convolution fusion | flops 1216610304 | bytes 8257536 | tf_op jit(solution)/shard_map/dot_general | solution.py:130
  327.7 47.6 %reduce-scatter.11.cloned.1.call-done = f32[1,192,192]{2,1,0:T(8,128)} async-done(((f32[16,192,192]{2,1,0:T(8,128)}), f32[1,192,192]{2,1,0:T(8,128)}) %reduce-scatter.11.cloned.1.call-update) | async-done | bytes 147472 | tf_op jit(solution)/shard_map/reduce_scatter | solution.py:145
  375.4 117.3 %reduce-scatter.9.cloned.1.call-done = f32[1,192,768]{2,1,0:T(8,128)} async-done(((f32[16,192,768]{2,1,0:T(8,128)}), f32[1,192,768]{2,1,0:T(8,128)}) %reduce-scatter.9.cloned.1.call-update) | async-done | bytes 589840 | tf_op jit(solution)/shard_map/reduce_scatter | solution.py:139
  (92 shorter events, 11.0 us)
Async XLA Ops:
  7.2 43.4 %all-gather.14.cloned.1.call-start = ((), (), s32[]{:S(2)}) async-start(), calls=%async_computation.7 | async-start | bytes 1671168 | tf_op jit(solution)/shard_map/all_gather | solution.py:60
  7.9 98.4 %all-gather.12.cloned.1.call-start = ((), (), s32[]{:S(2)}) async-start(), calls=%async_computation.6 | async-start | bytes 5013504 | tf_op jit(solution)/shard_map/all_gather | solution.py:59
  8.6 146.7 %all-gather.16.cloned.1.call-start = ((), (), s32[]{:S(2)}) async-start(), calls=%async_computation.12 | async-start | bytes 1769472 | tf_op jit(solution)/shard_map/all_gather | solution.py:77
  54.6 61.1 %copy-start = (bf16[768,768]{1,0:T(8,128)(2,1)}, bf16[768,768]{1,0:T(8,128)(2,1)S(1)}, u32[]{:S(2)}) copy-start(bf16[768,768]{1,0:T(8,128)(2,1)S(1)} %reshape.62) | copy-start | bytes 3538948
  112.2 1.4 copy-start.5
  112.2 1.5 copy-start.11
  113.3 2.4 copy-start.3
  115.7 1.3 copy-start.7
  130.9 106.1 %reduce-scatter.5.cloned.1.call-start = ((), (), s32[]{:S(2)}) async-start(), calls=%async_computation.8 | async-start | bytes 1966080 | tf_op jit(solution)/shard_map/reduce_scatter | solution.py:106
  194.2 2.5 copy-start.10
  196.8 3.5 copy-start.4
  200.2 87.2 %reduce-scatter.7.cloned.1.call-start = ((), (), s32[]{:S(2)}) async-start(), calls=%async_computation.9 | async-start | bytes 3538944 | tf_op jit(solution)/shard_map/reduce_scatter | solution.py:113
  204.2 171.2 %reduce-scatter.11.cloned.1.call-start = ((), (), s32[]{:S(2)}) async-start(), calls=%async_computation.11 | async-start | bytes 3342336 | tf_op jit(solution)/shard_map/reduce_scatter | solution.py:145
  301.1 1.0 copy-start.8
  309.9 182.8 %reduce-scatter.9.cloned.1.call-start = ((), (), s32[]{:S(2)}) async-start(), calls=%async_computation.10 | async-start | bytes 10027008 | tf_op jit(solution)/shard_map/reduce_scatter | solution.py:139
  312.5 1.6 copy-start.1
  314.1 1.4 copy-start.2
  314.6 6.0 %copy-start.9 = (bf16[256,768]{1,0:T(8,128)(2,1)}, bf16[256,768]{1,0:T(8,128)(2,1)S(1)}, u32[]{:S(2)}) copy-start(bf16[256,768]{1,0:T(8,128)(2,1)S(1)} %convolution_convert_fusion) | copy-start | bytes 1179652
  320.6 1.5 copy-start.6
Sparse Core Ops, SparseCore 0:
  10.3 40.2 all-gather.13
  52.9 53.3 all-gather.11
  131.0 24.2 all-gather.15
  200.3 36.6 reduce-scatter.4
  240.2 47.0 reduce-scatter.6
  310.0 65.3 reduce-scatter.10
  380.6 112.0 reduce-scatter.8
where the time goes:
time: 502 us; the launch traced here: 500 us
  waiting for transfers between devices  352 us (70%)
  blocking collectives  70.2 us (14%)
  matrix products  25.8 us (5%)
  local copies, waits for them, and re-layouts  24.7 us (5%)
  between operations  15.1 us (3%)
  other arithmetic  10.4 us (2%)
    reduce_scatter x1, waiting for transfers between devices, body(): lax.psum_scatter(split_blocks(term_down, grow_count, gcol_count), ('grow'...  117 us
    all_gather x1, waiting for transfers between devices, body(): lax.all_gather(w_down, ('grow', 'gcol'), axis=0, tiled=True)  51.6 us
    reduce_scatter x1, waiting for transfers between devices, body(): lax.psum_scatter(logit_scale * lax.dot_general(block, image_rows, (((0,),...  50.4 us
    reduce_scatter x1, waiting for transfers between devices, body(): lax.psum_scatter(split_blocks(term_proj, grow_count, gcol_count), ('grow'...  47.6 us
    all_gather x1, waiting for transfers between devices, body(): lax.all_gather(projection, ('grow', 'gcol'), axis=0, tiled=True)  41.9 us
    all_gather x4, blocking collectives, combined_all(): gathered = jax.tree.map(lambda a: lax.all_gather(a, axis), part)  34.8 us
    reduce_scatter x1, waiting for transfers between devices, body(): lax.psum_scatter(logit_scale * jnp.dot(block, text_rows, preferred_elemen...  32.8 us
    all_gather x1, blocking collectives, body(): image_rows = lax.all_gather(halves[0], 'gcol', axis=0, tiled=True)  14.1 us
  transfers between devices with their start and end apart: 7, of which 7 were waited for; matrix products, arithmetic and copies ran while one was open for 5% of the time, Pallas kernels for 0%

commit v1 on v0

v1 whole, which is shorter than its diff:
```python
import jax
import jax.numpy as jnp
from jax import lax
from jax.sharding import PartitionSpec as P

F32 = jnp.float32
BF16 = jnp.bfloat16


def quick_gelu(values):
    return values * jax.nn.sigmoid(1.702 * values)


def gelu_slope(values):
    sigmoid = jax.nn.sigmoid(1.702 * values)
    return sigmoid + 1.702 * values * sigmoid * (1.0 - sigmoid)


def shift(value, axis, step):
    count = lax.axis_size(axis)
    return lax.ppermute(value, axis, [(i, (i + step) % count) for i in range(count)])


def swap(value, axis, bit):
    return lax.ppermute(value, axis, [(i, i ^ bit) for i in range(lax.axis_size(axis))])


def ring(value):
    blocks = [value]
    for _ in range(lax.axis_size("gcol") - 1):
        blocks.append(shift(blocks[-1], "gcol", 1))
    return blocks


def spread(blocks):
    table = {0: blocks}
    bit = lax.axis_size("grow") // 2
    while bit:
        for j in list(table):
            table[j ^ bit] = [swap(block, "grow", bit) for block in table[j]]
        bit //= 2
    return [table[j] for j in range(len(table))]


def gather_rows(value, chunks):
    parts = [spread(ring(part)) for part in jnp.split(value, chunks, 0)]
    grow_count, gcol_count = lax.axis_size("grow"), lax.axis_size("gcol")
    return [
        [[part[j][k] for part in parts] for k in range(gcol_count)] for j in range(grow_count)
    ]


def dot_tn(left, right):
    return lax.dot_general(left, right, (((0,), (0,)), ((), ())), preferred_element_type=F32)


def dot_nt(left, right):
    return lax.dot_general(left, right, (((1,), (1,)), ((), ())), preferred_element_type=F32)


def dot_nn(left, right):
    return jnp.dot(left, right, preferred_element_type=F32)


def body(hidden, preact, w_down, projection, log_scale):
    tower_count = lax.axis_size("tower")
    grow_count, gcol_count = lax.axis_size("grow"), lax.axis_size("gcol")
    tower, grow, gcol = (lax.axis_index(a) for a in ("tower", "grow", "gcol"))
    hidden, preact, w_down, projection = hidden[0], preact[0], w_down[0], projection[0]
    rows = hidden.shape[0]
    features, inner_block = w_down.shape
    columns = projection.shape[1]
    js, ks = range(grow_count), range(gcol_count)

    proj_pieces = gather_rows(projection, 1)
    down_pieces = gather_rows(w_down, 2)
    down = [jnp.concatenate([part for j in js for part in down_pieces[j][k]], 0) for k in ks]
    proj = jnp.concatenate(
        [jnp.concatenate([proj_pieces[j][k][0] for j in js], 0) for k in reversed(ks)], 1
    )
    proj = jnp.roll(proj, (gcol + 1) * columns, 1)

    place = [lax.rem(gcol - k + gcol_count, gcol_count) * inner_block for k in ks]
    pre = [lax.dynamic_slice_in_dim(preact, place[k], inner_block, 1).astype(F32) for k in ks]
    active = [quick_gelu(pre[k]).astype(BF16) for k in ks]
    hidden_rel = jnp.concatenate(
        [lax.dynamic_slice_in_dim(hidden, (grow ^ j) * features, features, 1) for j in js], 1
    )
    stream = hidden_rel.astype(F32) + sum(dot_nt(active[k], down[k]) for k in ks)
    stream_b = stream.astype(BF16)
    embed = dot_nn(stream_b, proj)
    inverse = lax.rsqrt(jnp.sum(embed * embed, axis=1, keepdims=True) + 1e-06)
    unit = embed * inverse
    unit_b = unit.astype(BF16)

    chunks = 2
    pieces = [
        spread(ring(swap(part, "tower", 1))) for part in jnp.split(unit_b, chunks, 0)
    ]
    order = [(j, k) for j in js for k in ks]
    others = jnp.concatenate([pieces[q][j][k] for j, k in order for q in range(chunks)], 0)
    logit_scale = jnp.exp(log_scale)
    scores = logit_scale * dot_nt(unit_b, others)
    row_max = jnp.max(scores, axis=1)
    row_lse = row_max + jnp.log(jnp.sum(jnp.exp(scores - row_max[:, None]), axis=1))

    active_all = spread([jnp.concatenate(active, 1)])
    stream_all = [
        swap(stream_b[:, j * features : (j + 1) * features], "grow", j) if j else stream_b[:, :features]
        for j in js
    ]

    device_count = tower_count * grow_count * gcol_count
    lse_all = lax.all_to_all(
        jnp.broadcast_to(row_lse[None], (device_count, rows)), ("tower", "grow", "gcol"), 0, 0
    )
    sources = jnp.stack(
        [
            ((1 - tower) * grow_count + (grow ^ j)) * gcol_count
            + lax.rem(gcol - k + gcol_count, gcol_count)
            for j, k in order
        ]
    )
    other_lse = jnp.take(lse_all, sources, axis=0).reshape(-1)

    row_index = lax.broadcasted_iota(jnp.int32, scores.shape, 0)
    column_index = lax.broadcasted_iota(jnp.int32, scores.shape, 1)
    grad = 0.5 * (
        jnp.exp(scores - row_lse[:, None]) + jnp.exp(scores - other_lse[None, :])
    ) - (row_index == column_index).astype(F32)
    d_unit = logit_scale * dot_nn(grad.astype(BF16), others)
    along = jnp.sum(unit * d_unit, axis=1, keepdims=True)
    d_embed = (inverse * (d_unit - unit * along)).astype(BF16)
    d_stream = dot_nt(d_embed, proj).astype(BF16)

    d_embed_all = [table[0] for table in spread([d_embed])]
    d_stream_all = [
        swap(d_stream[:, j * features : (j + 1) * features], "grow", j) if j else d_stream[:, :features]
        for j in js
    ]
    left = jnp.concatenate(d_stream_all, 0)
    active_rows = jnp.concatenate([table[0] for table in active_all], 0)
    term_proj = dot_tn(jnp.concatenate(stream_all, 0), jnp.concatenate(d_embed_all, 0))
    grad_down, grad_proj = None, None
    sent = []
    for k in ks:
        term = dot_tn(left, active_rows[:, k * inner_block : (k + 1) * inner_block])
        owner = lax.rem(gcol - k + gcol_count, gcol_count)
        term_p = lax.dynamic_slice_in_dim(term_proj, owner * columns, columns, 1)
        if k == 0:
            grad_down, grad_proj = term, term_p
        else:
            sent.append((shift(term.astype(BF16), "gcol", -k), shift(term_p.astype(BF16), "gcol", -k)))
    for term, term_p in sent:
        grad_down = grad_down + term.astype(F32)
        grad_proj = grad_proj + term_p.astype(F32)

    d_pre = jnp.zeros(preact.shape, BF16)
    for k in ks:
        part = (dot_nn(d_stream, down[k]) * gelu_slope(pre[k])).astype(BF16)
        d_pre = lax.dynamic_update_slice_in_dim(d_pre, part, place[k], 1)
    d_hidden = jnp.zeros(hidden.shape, BF16)
    for j in js:
        d_hidden = lax.dynamic_update_slice_in_dim(
            d_hidden, d_stream[:, j * features : (j + 1) * features], (grow ^ j) * features, 1
        )
    return (d_hidden[None], d_pre[None], grad_down[None], grad_proj[None])


def solution(mesh):
    placed = (
        P("tower", ("grow", "gcol"), None),
        P("tower", ("grow", "gcol"), None),
        P("tower", "grow", "gcol"),
        P("tower", "grow", "gcol"),
        P(),
    )
    return jax.shard_map(
        body, mesh=mesh, in_specs=placed, out_specs=placed[:4], check_vma=False
    )
```

time: 502 us -> 314 us (0.63)
  waiting for transfers between devices: 352 us -> 125 us
  starting transfers between devices: 0.68 us -> 91.9 us
  blocking collectives: 70.2 us -> 0 us
  other arithmetic: 10.4 us -> 24.5 us
  local copies, waits for them, and re-layouts: 24.7 us -> 38.1 us
  between operations: 15.1 us -> 2.5 us
    reduce_scatter x4 -> x0, waiting for transfers between devices: 248 us -> none  [the longest x1 117 us: body(): lax.psum_scatter(split_blocks(term_down, grow_count, gcol_count), ('grow'...]
    ppermute x0 -> x95, waiting for transfers between devices: none -> 124 us  [the longest x74 80.4 us: swap(): lax.ppermute(value, axis, [(i, i ^ bit) for i in range(lax.axis_size(axis...]
    all_gather x3 -> x0, waiting for transfers between devices: 103 us -> none  [the longest x1 51.6 us: body(): lax.all_gather(w_down, ('grow', 'gcol'), axis=0, tiled=True)]
    ppermute x0 -> x95, starting transfers between devices: none -> 85.2 us  [the longest x74 62 us: swap(): lax.ppermute(value, axis, [(i, i ^ bit) for i in range(lax.axis_size(axis...]
    all_gather x5 -> x0, blocking collectives: 49 us -> none  [the longest x4 34.8 us: combined_all(): gathered = jax.tree.map(lambda a: lax.all_gather(a, axis), part)]
    all_to_all x2 -> x0, blocking collectives: 21.3 us -> none  [the longest x1 12.6 us: body(): lax.all_to_all(jnp.stack([image_grad, text_grad]), 'tower', split_axis=0,...]
    concatenate x0 -> x6, other arithmetic: none -> 18.5 us  [the longest x1 13 us: body(): active_rows = jnp.concatenate([table[0] for table in active_all], 0)]
    reshape x4 -> x0, local copies, waits for them, and re-layouts: 13.7 us -> none  [the longest x2 8.6 us: tile_whole(): blocks.reshape(grow_count, gcol_count, height, breadth)]
  transfers between devices with their start and end apart: 7 -> 96, of which waited for: 7 -> 41; matrix products, arithmetic and copies ran while one was open for 5% -> 26% of each run, Pallas kernels for 0% -> 0%
where the time goes in v1:
time: 314 us; the launch traced here: 310 us
  waiting for transfers between devices  125 us (40%)
  starting transfers between devices  91.9 us (29%)
  local copies, waits for them, and re-layouts  38.1 us (12%)
  matrix products  27.7 us (9%)
  other arithmetic  24.5 us (8%)
    ppermute x74, waiting for transfers between devices, swap(): lax.ppermute(value, axis, [(i, i ^ bit) for i in range(lax.axis_size(axis...  80.4 us
    ppermute x74, starting transfers between devices, swap(): lax.ppermute(value, axis, [(i, i ^ bit) for i in range(lax.axis_size(axis...  62 us
    ppermute x21, waiting for transfers between devices, shift(): lax.ppermute(value, axis, [(i, (i + step) % count) for i in range(count)])  43.1 us
    ppermute x21, starting transfers between devices, shift(): lax.ppermute(value, axis, [(i, (i + step) % count) for i in range(count)])  23.2 us
    unnamed x137, local copies, waits for them, and re-layouts  18.8 us
    concatenate x1, other arithmetic, body(): active_rows = jnp.concatenate([table[0] for table in active_all], 0)  13 us
    dot_general x6, matrix products, dot_nn(): return jnp.dot(left, right, preferred_element_type=F32)  10.9 us
    dot_general x5, matrix products, dot_tn(): lax.dot_general(left, right, (((0,), (0,)), ((), ())), preferred_element_...  8.44 us
  transfers between devices with their start and end apart: 96, of which 41 were waited for; matrix products, arithmetic and copies ran while one was open for 26% of the time, Pallas kernels for 0%

profile of v1, /device:TPU:9, one launch (start us, length us, event | category | flops | bytes accessed | tf_op | source)
XLA Modules:
  0.0 310.1 jit_solution(2016007969452088777)
XLA Ops:
  8.7 2.4 fusion.90
  21.1 5.3 %collective-permute-done.30 = bf16[192,192]{1,0:T(8,128)(2,1)S(1)} collective-permute-done((bf16[192,192]{1,0:T(8,128)(2,1)}, bf16[192,192]{1,0:T(8,128)(2,1)S(1)}, u32[]{:S(2)}, u32[]{:S(2)}) %collective-permute-start.30) | collective-permute-done | bytes 73760 | tf_op jit(solution)/shard_map/ppermute | solution.py:21
  28.8 29.0 %collective-permute-done.40 = bf16[192,192]{1,0:T(8,128)(2,1)S(1)} collective-permute-done((bf16[192,192]{1,0:T(8,128)(2,1)S(1)}, bf16[192,192]{1,0:T(8,128)(2,1)S(1)}, u32[]{:S(2)}, u32[]{:S(2)}) %collective-permute-start.40) | collective-permute-done | bytes 73760 | tf_op jit(solution)/shard_map/ppermute | solution.py:25
  65.9 3.2 %collective-permute-done.37 = bf16[192,192]{1,0:T(8,128)(2,1)S(1)} collective-permute-done((bf16[192,192]{1,0:T(8,128)(2,1)S(1)}, bf16[192,192]{1,0:T(8,128)(2,1)S(1)}, u32[]{:S(2)}, u32[]{:S(2)}) %collective-permute-start.37) | collective-permute-done | bytes 73760 | tf_op jit(solution)/shard_map/ppermute | solution.py:25
  69.1 2.2 collective-permute-start.36
  78.6 2.8 collective-permute-done.32
  84.5 2.5 collective-permute-start.33
  92.2 4.2 %concatenate.81 = bf16[768,1536]{1,0:T(8,128)(2,1)S(1)} concatenate(bf16[768,192]{1,0:T(8,128)(2,1)} %pad_maximum_fusion.3, bf16[768,192]{1,0:T(8,128)(2,1)} %pad_maximum_fusion.4, bf16[768,192]{1,0:T(8,128)(2,1)} %pad_maximum_fusion.5, bf16[768,192]{1,0:T(8,128)(2,1)} %pad_maximum_fusion.6, bf16[768,192]{1,0:T(8,128)(2,1)} %pad_maximum_fusion.3, ...), dimensions={1} | concatenate | bytes 4718592 | tf_op jit(solution)/shard_map/jit(_roll_dynamic)/concatenate | solution.py:81
  112.3 2.3 collective-permute-start.21
  131.6 4.1 %collective-permute-done.45 = bf16[128,768]{1,0:T(8,128)(2,1)S(1)} collective-permute-done((bf16[128,768]{1,0:T(8,128)(2,1)S(1)}, bf16[128,768]{1,0:T(8,128)(2,1)S(1)}, u32[]{:S(2)}, u32[]{:S(2)}) %collective-permute-start.45) | collective-permute-done | bytes 196640 | tf_op jit(solution)/shard_map/ppermute | solution.py:25
  135.7 2.2 collective-permute-start.53
  143.7 3.6 %collective-permute-done.48 = bf16[128,768]{1,0:T(8,128)(2,1)S(1)} collective-permute-done((bf16[128,768]{1,0:T(8,128)(2,1)S(1)}, bf16[128,768]{1,0:T(8,128)(2,1)S(1)}, u32[]{:S(2)}, u32[]{:S(2)}) %collective-permute-start.48) | collective-permute-done | bytes 196640 | tf_op jit(solution)/shard_map/ppermute | solution.py:21
  148.0 3.4 %collective-permute-done.49 = bf16[128,768]{1,0:T(8,128)(2,1)S(1)} collective-permute-done((bf16[128,768]{1,0:T(8,128)(2,1)S(1)}, bf16[128,768]{1,0:T(8,128)(2,1)S(1)}, u32[]{:S(2)}, u32[]{:S(2)}) %collective-permute-start.49) | collective-permute-done | bytes 196640 | tf_op jit(solution)/shard_map/ppermute | solution.py:21
  152.2 2.6 collective-permute-done.50
  155.9 4.0 %collective-permute-done.51 = bf16[128,768]{1,0:T(8,128)(2,1)S(1)} collective-permute-done((bf16[128,768]{1,0:T(8,128)(2,1)S(1)}, bf16[128,768]{1,0:T(8,128)(2,1)S(1)}, u32[]{:S(2)}, u32[]{:S(2)}) %collective-permute-start.51) | collective-permute-done | bytes 196640 | tf_op jit(solution)/shard_map/ppermute | solution.py:21
  159.9 4.0 %collective-permute-start.54 = (bf16[128,768]{1,0:T(8,128)(2,1)S(1)}, bf16[128,768]{1,0:T(8,128)(2,1)S(1)}, u32[]{:S(2)}, u32[]{:S(2)}) collective-permute-start(bf16[128,768]{1,0:T(8,128)(2,1)S(1)} %collective-permute-done.46), channel_id=1, source_target_pairs={{0,4},{4,0},{8,12},{12,8},{1,5},{5,1},{9,13},{13,9},{2,6},{6,2},{1... | collective-permute-start | bytes 589832 | tf_op jit(solution)/shard_map/ppermute | solution.py:25
  165.1 3.4 %collective-permute-start.55 = (bf16[128,768]{1,0:T(8,128)(2,1)S(1)}, bf16[128,768]{1,0:T(8,128)(2,1)S(1)}, u32[]{:S(2)}, u32[]{:S(2)}) collective-permute-start(bf16[128,768]{1,0:T(8,128)(2,1)S(1)} %collective-permute-done.47), channel_id=1, source_target_pairs={{0,4},{4,0},{8,12},{12,8},{1,5},{5,1},{9,13},{13,9},{2,6},{6,2},{1... | collective-permute-start | bytes 589832 | tf_op jit(solution)/shard_map/ppermute | solution.py:25
  174.6 3.9 %collective-permute-done.62 = bf16[128,768]{1,0:T(8,128)(2,1)S(1)} collective-permute-done((bf16[128,768]{1,0:T(8,128)(2,1)S(1)}, bf16[128,768]{1,0:T(8,128)(2,1)S(1)}, u32[]{:S(2)}, u32[]{:S(2)}) %collective-permute-start.62) | collective-permute-done | bytes 196640 | tf_op jit(solution)/shard_map/ppermute | solution.py:25
  180.5 2.2 collective-permute-done.63
  183.2 3.7 %collective-permute-done.64 = bf16[128,768]{1,0:T(8,128)(2,1)S(1)} collective-permute-done((bf16[128,768]{1,0:T(8,128)(2,1)S(1)}, bf16[128,768]{1,0:T(8,128)(2,1)S(1)}, u32[]{:S(2)}, u32[]{:S(2)}) %collective-permute-start.64) | collective-permute-done | bytes 196640 | tf_op jit(solution)/shard_map/ppermute | solution.py:25
  187.5 3.7 %collective-permute-done.65 = bf16[128,768]{1,0:T(8,128)(2,1)S(1)} collective-permute-done((bf16[128,768]{1,0:T(8,128)(2,1)S(1)}, bf16[128,768]{1,0:T(8,128)(2,1)S(1)}, u32[]{:S(2)}, u32[]{:S(2)}) %collective-permute-start.65) | collective-permute-done | bytes 196640 | tf_op jit(solution)/shard_map/ppermute | solution.py:25
  191.7 3.7 %collective-permute-done.66 = bf16[128,768]{1,0:T(8,128)(2,1)S(1)} collective-permute-done((bf16[128,768]{1,0:T(8,128)(2,1)S(1)}, bf16[128,768]{1,0:T(8,128)(2,1)S(1)}, u32[]{:S(2)}, u32[]{:S(2)}) %collective-permute-start.66) | collective-permute-done | bytes 196640 | tf_op jit(solution)/shard_map/ppermute | solution.py:25
  195.9 3.7 %collective-permute-done.67 = bf16[128,768]{1,0:T(8,128)(2,1)S(1)} collective-permute-done((bf16[128,768]{1,0:T(8,128)(2,1)S(1)}, bf16[128,768]{1,0:T(8,128)(2,1)S(1)}, u32[]{:S(2)}, u32[]{:S(2)}) %collective-permute-start.67) | collective-permute-done | bytes 196640 | tf_op jit(solution)/shard_map/ppermute | solution.py:25
  201.6 2.2 collective-permute-done.68
  214.7 6.6 %all-to-all-start = ((f32[32,1,256]{2,1,0:T(1,128)}), f32[32,1,256]{2,1,0:T(1,128)}, u32[]{:S(2)}, u32[]{:S(2)}) async-start(f32[32,1,256]{2,1,0:T(1,128)} %broadcast_in_dim.52), calls=%async_computation | async-start | bytes 65536 | tf_op jit(solution)/shard_map/all_to_all | solution.py:114
  230.8 6.6 %multiply_reduce_fusion = (f32[256]{0:T(256)S(1)}, f32[256,768]{1,0:T(8,128)S(1)}) fusion(f32[256,768]{1,0:T(8,128)S(1)} %get-tuple-element.32, f32[256]{0:T(256)} %copy-done.31, bf16[4096,768]{1,0:T(8,128)(2,1)} %copy-done.33, f32[256,4096]{1,0:T(8,128)} %copy-done.5, f32[4096]{0:T(1024)S(1)} %bitcast.127, f32[256]{0:T(256)} %copy-done.34, f32[]{:T(128)S(6)} %exp.32), kind=kOutput, calls=%fused_computation.101 | convolution fusion | flops 1619787520 | bytes 12078084 | tf_op jit(solution)/shard_map/dot_general | solution.py:62
  241.6 6.5 %collective-permute-done.90 = bf16[256,768]{1,0:T(8,128)(2,1)S(1)} collective-permute-done((bf16[256,768]{1,0:T(8,128)(2,1)S(1)}, bf16[256,768]{1,0:T(8,128)(2,1)S(1)}, u32[]{:S(2)}, u32[]{:S(2)}) %collective-permute-start.90) | collective-permute-done | bytes 393248 | tf_op jit(solution)/shard_map/ppermute | solution.py:25
  251.6 4.7 %collective-permute-done.88 = bf16[256,192]{1,0:T(8,128)(2,1)S(1)} collective-permute-done((bf16[256,192]{1,0:T(8,128)(2,1)S(1)}, bf16[256,192]{1,0:T(8,128)(2,1)S(1)}, u32[]{:S(2)}, u32[]{:S(2)}) %collective-permute-start.88) | collective-permute-done | bytes 98336 | tf_op jit(solution)/shard_map/ppermute | solution.py:25
  262.1 13.0 %pad_maximum_fusion = bf16[1024,3072]{1,0:T(8,128)(2,1)S(1)} fusion(bf16[256,3072]{1,0:T(8,128)(2,1)} %collective-permute-done.82, bf16[256,3072]{1,0:T(8,128)(2,1)} %collective-permute-done.81, bf16[256,3072]{1,0:T(8,128)(2,1)} %collective-permute-done.80, bf16[256,768]{1,0:T(8,128)(2,1)S(1)} %copy-done.8, bf16[256,768]{1,0:T(8,128)(2,1)S(1)} %copy-done.3, ...), kind=kLoop, calls=%fused_computation.1 | loop fusion | flops 44040192 | bytes 12582912 | tf_op jit(solution)/shard_map/concatenate | solution.py:142
  290.9 9.7 %collective-permute-done.84 = bf16[192,768]{1,0:T(8,128)(2,1)} collective-permute-done((bf16[192,768]{1,0:T(8,128)(2,1)}, bf16[192,768]{1,0:T(8,128)(2,1)}, u32[]{:S(2)}, u32[]{:S(2)}) %collective-permute-start.84) | collective-permute-done | bytes 294944 | tf_op jit(solution)/shard_map/ppermute | solution.py:21
  300.6 6.3 %collective-permute-done.85 = bf16[192,768]{1,0:T(8,128)(2,1)} collective-permute-done((bf16[192,768]{1,0:T(8,128)(2,1)}, bf16[192,768]{1,0:T(8,128)(2,1)}, u32[]{:S(2)}, u32[]{:S(2)}) %collective-permute-start.85) | collective-permute-done | bytes 294944 | tf_op jit(solution)/shard_map/ppermute | solution.py:21
  306.9 3.1 %fusion.36 = f32[1,192,768]{2,1,0:T(8,128)} fusion(bf16[1024,3072]{1,0:T(8,128)(2,1)} %copy-done.4, bf16[192,768]{1,0:T(8,128)(2,1)} %collective-permute-done.85, bf16[192,768]{1,0:T(8,128)(2,1)} %collective-permute-done.84, bf16[192,768]{1,0:T(8,128)(2,1)} %collective-permute-done.83, bf16[256,192]{1,0:T(8,128)(2,1)} %copy-done.37, ...), kind=kOutput, calls=%fused_computation.44 | convolution fusion | flops 304447488 | bytes 3538944 | tf_op jit(solution)/shard_map/dot_general | solution.py:54
  (353 shorter events, 146.7 us)
Async XLA Ops:
  2.3 18.3 %collective-permute-start = (bf16[96,768]{1,0:T(8,128)(2,1)}, bf16[96,768]{1,0:T(8,128)(2,1)S(1)}, u32[]{:S(2)}, u32[]{:S(2)}) collective-permute-start(bf16[96,768]{1,0:T(8,128)(2,1)} %get-tuple-element.30), channel_id=1, source_target_pairs={{0,4},{4,0},{8,12},{12,8},{1,5},{5,1},{9,13},{13,9},{2,6},{6,2},{1... | collective-permute-start | bytes 442376 | tf_op jit(solution)/shard_map/ppermute | solution.py:25
  3.0 24.9 %collective-permute-start.2 = (bf16[96,768]{1,0:T(8,128)(2,1)}, bf16[96,768]{1,0:T(8,128)(2,1)S(1)}, u32[]{:S(2)}, u32[]{:S(2)}) collective-permute-start(bf16[96,768]{1,0:T(8,128)(2,1)} %get-tuple-element.30), channel_id=1, source_target_pairs={{0,8},{4,12},{8,0},{12,4},{1,9},{5,13},{9,1},{13,5},{2,10},{6,14},... | collective-permute-start | bytes 442376 | tf_op jit(solution)/shard_map/ppermute | solution.py:25
  4.3 15.1 %collective-permute-start.6 = (bf16[96,768]{1,0:T(8,128)(2,1)}, bf16[96,768]{1,0:T(8,128)(2,1)S(1)}, u32[]{:S(2)}, u32[]{:S(2)}) collective-permute-start(bf16[96,768]{1,0:T(8,128)(2,1)} %get-tuple-element.30), channel_id=1, source_target_pairs={{0,1},{1,2},{2,3},{3,0},{4,5},{5,6},{6,7},{7,4},{8,9},{9,10},{10,1... | collective-permute-start | bytes 442376 | tf_op jit(solution)/shard_map/ppermute | solution.py:21
  5.8 9.9 %collective-permute-start.42 = (bf16[192,192]{1,0:T(8,128)(2,1)}, bf16[192,192]{1,0:T(8,128)(2,1)S(1)}, u32[]{:S(2)}, u32[]{:S(2)}) collective-permute-start(bf16[192,192]{1,0:T(8,128)(2,1)} %bitcast.124), channel_id=1, source_target_pairs={{0,4},{4,0},{8,12},{12,8},{1,5},{5,1},{9,13},{13,9},{2,6},{6,2},{1... | collective-permute-start | bytes 221192 | tf_op jit(solution)/shard_map/ppermute | solution.py:25
  16.3 11.8 %collective-permute-start.3 = (bf16[96,768]{1,0:T(8,128)(2,1)}, bf16[96,768]{1,0:T(8,128)(2,1)S(1)}, u32[]{:S(2)}, u32[]{:S(2)}) collective-permute-start(bf16[96,768]{1,0:T(8,128)(2,1)} %get-tuple-element.29), channel_id=1, source_target_pairs={{0,8},{4,12},{8,0},{12,4},{1,9},{5,13},{9,1},{13,5},{2,10},{6,14},... | collective-permute-start | bytes 442376 | tf_op jit(solution)/shard_map/ppermute | solution.py:25
  20.8 204.1 %collective-permute-start.81 = (bf16[256,3072]{1,0:T(8,128)(2,1)}, bf16[256,3072]{1,0:T(8,128)(2,1)}, u32[]{:S(2)}, u32[]{:S(2)}) collective-permute-start(bf16[256,3072]{1,0:T(8,128)(2,1)} %pad_maximum_fusion.1), channel_id=1, source_target_pairs={{0,8},{4,12},{8,0},{12,4},{1,9},{5,13},{9,1},{13,5},{2,10},{6,14},... | collective-permute-start | bytes 4718600 | tf_op jit(solution)/shard_map/ppermute | solution.py:25
  26.4 234.5 %collective-permute-start.80 = (bf16[256,3072]{1,0:T(8,128)(2,1)}, bf16[256,3072]{1,0:T(8,128)(2,1)}, u32[]{:S(2)}, u32[]{:S(2)}) collective-permute-start(bf16[256,3072]{1,0:T(8,128)(2,1)} %pad_maximum_fusion.1), channel_id=1, source_target_pairs={{0,4},{4,0},{8,12},{12,8},{1,5},{5,1},{9,13},{13,9},{2,6},{6,2},{1... | collective-permute-start | bytes 4718600 | tf_op jit(solution)/shard_map/ppermute | solution.py:25
  27.9 30.0 %collective-permute-start.40 = (bf16[192,192]{1,0:T(8,128)(2,1)S(1)}, bf16[192,192]{1,0:T(8,128)(2,1)S(1)}, u32[]{:S(2)}, u32[]{:S(2)}) collective-permute-start(bf16[192,192]{1,0:T(8,128)(2,1)S(1)} %collective-permute-done.30), channel_id=1, source_target_pairs={{0,8},{4,12},{8,0},{12,4},{1,9},{5,13},{9,1},{13,5},{2,10},{6,14},... | collective-permute-start | bytes 221192 | tf_op jit(solution)/shard_map/ppermute | solution.py:25
  28.2 31.8 %collective-permute-start.39 = (bf16[192,192]{1,0:T(8,128)(2,1)S(1)}, bf16[192,192]{1,0:T(8,128)(2,1)S(1)}, u32[]{:S(2)}, u32[]{:S(2)}) collective-permute-start(bf16[192,192]{1,0:T(8,128)(2,1)S(1)} %collective-permute-done.30), channel_id=1, source_target_pairs={{0,4},{4,0},{8,12},{12,8},{1,5},{5,1},{9,13},{13,9},{2,6},{6,2},{1... | collective-permute-start | bytes 221192 | tf_op jit(solution)/shard_map/ppermute | solution.py:25
  28.6 37.1 %collective-permute-start.4 = (bf16[96,768]{1,0:T(8,128)(2,1)S(1)}, bf16[96,768]{1,0:T(8,128)(2,1)S(1)}, u32[]{:S(2)}, u32[]{:S(2)}) collective-permute-start(bf16[96,768]{1,0:T(8,128)(2,1)S(1)} %collective-permute-done.2), channel_id=1, source_target_pairs={{0,4},{4,0},{8,12},{12,8},{1,5},{5,1},{9,13},{13,9},{2,6},{6,2},{1... | collective-permute-start | bytes 442376 | tf_op jit(solution)/shard_map/ppermute | solution.py:25
  61.3 10.1 %collective-permute-start.5 = (bf16[96,768]{1,0:T(8,128)(2,1)S(1)}, bf16[96,768]{1,0:T(8,128)(2,1)S(1)}, u32[]{:S(2)}, u32[]{:S(2)}) collective-permute-start(bf16[96,768]{1,0:T(8,128)(2,1)S(1)} %collective-permute-done.3), channel_id=1, source_target_pairs={{0,4},{4,0},{8,12},{12,8},{1,5},{5,1},{9,13},{13,9},{2,6},{6,2},{1... | collective-permute-start | bytes 442376 | tf_op jit(solution)/shard_map/ppermute | solution.py:25
  91.1 11.0 %collective-permute-start.16 = (bf16[96,768]{1,0:T(8,128)(2,1)}, bf16[96,768]{1,0:T(8,128)(2,1)}, u32[]{:S(2)}, u32[]{:S(2)}) collective-permute-start(bf16[96,768]{1,0:T(8,128)(2,1)} %collective-permute-done.14), channel_id=1, source_target_pairs={{0,4},{4,0},{8,12},{12,8},{1,5},{5,1},{9,13},{13,9},{2,6},{6,2},{1... | collective-permute-start | bytes 442376 | tf_op jit(solution)/shard_map/ppermute | solution.py:25
  135.7 29.3 %collective-permute-start.53 = (bf16[128,768]{1,0:T(8,128)(2,1)S(1)}, bf16[128,768]{1,0:T(8,128)(2,1)S(1)}, u32[]{:S(2)}, u32[]{:S(2)}) collective-permute-start(bf16[128,768]{1,0:T(8,128)(2,1)S(1)} %collective-permute-done.45), channel_id=1, source_target_pairs={{0,4},{4,0},{8,12},{12,8},{1,5},{5,1},{9,13},{13,9},{2,6},{6,2},{1... | collective-permute-start | bytes 589832 | tf_op jit(solution)/shard_map/ppermute | solution.py:25
  164.0 9.9 %collective-permute-start.61 = (bf16[128,768]{1,0:T(8,128)(2,1)S(1)}, bf16[128,768]{1,0:T(8,128)(2,1)S(1)}, u32[]{:S(2)}, u32[]{:S(2)}) collective-permute-start(bf16[128,768]{1,0:T(8,128)(2,1)S(1)} %collective-permute-done.45), channel_id=1, source_target_pairs={{0,8},{4,12},{8,0},{12,4},{1,9},{5,13},{9,1},{13,5},{2,10},{6,14},... | collective-permute-start | bytes 589832 | tf_op jit(solution)/shard_map/ppermute | solution.py:25
  172.9 9.8 %collective-permute-start.63 = (bf16[128,768]{1,0:T(8,128)(2,1)S(1)}, bf16[128,768]{1,0:T(8,128)(2,1)S(1)}, u32[]{:S(2)}, u32[]{:S(2)}) collective-permute-start(bf16[128,768]{1,0:T(8,128)(2,1)S(1)} %collective-permute-done.47), channel_id=1, source_target_pairs={{0,8},{4,12},{8,0},{12,4},{1,9},{5,13},{9,1},{13,5},{2,10},{6,14},... | collective-permute-start | bytes 589832 | tf_op jit(solution)/shard_map/ppermute | solution.py:25
  174.0 13.0 %collective-permute-start.64 = (bf16[128,768]{1,0:T(8,128)(2,1)S(1)}, bf16[128,768]{1,0:T(8,128)(2,1)S(1)}, u32[]{:S(2)}, u32[]{:S(2)}) collective-permute-start(bf16[128,768]{1,0:T(8,128)(2,1)S(1)} %collective-permute-done.48), channel_id=1, source_target_pairs={{0,8},{4,12},{8,0},{12,4},{1,9},{5,13},{9,1},{13,5},{2,10},{6,14},... | collective-permute-start | bytes 589832 | tf_op jit(solution)/shard_map/ppermute | solution.py:25
  178.5 26.5 %collective-permute-start.69 = (bf16[128,768]{1,0:T(8,128)(2,1)S(1)}, bf16[128,768]{1,0:T(8,128)(2,1)S(1)}, u32[]{:S(2)}, u32[]{:S(2)}) collective-permute-start(bf16[128,768]{1,0:T(8,128)(2,1)S(1)} %collective-permute-done.61), channel_id=1, source_target_pairs={{0,4},{4,0},{8,12},{12,8},{1,5},{5,1},{9,13},{13,9},{2,6},{6,2},{1... | collective-permute-start | bytes 589832 | tf_op jit(solution)/shard_map/ppermute | solution.py:25
  214.7 12.6 %all-to-all-start = ((f32[32,1,256]{2,1,0:T(1,128)}), f32[32,1,256]{2,1,0:T(1,128)}, u32[]{:S(2)}, u32[]{:S(2)}) async-start(f32[32,1,256]{2,1,0:T(1,128)} %broadcast_in_dim.52), calls=%async_computation | async-start | bytes 65536 | tf_op jit(solution)/shard_map/all_to_all | solution.py:114
  223.3 17.8 %collective-permute-start.86 = (bf16[256,192]{1,0:T(8,128)(2,1)}, bf16[256,192]{1,0:T(8,128)(2,1)}, u32[]{:S(2)}, u32[]{:S(2)}) collective-permute-start(bf16[256,192]{1,0:T(8,128)(2,1)} %get-tuple-element.14), channel_id=1, source_target_pairs={{0,4},{4,0},{8,12},{12,8},{1,5},{5,1},{9,13},{13,9},{2,6},{6,2},{1... | collective-permute-start | bytes 294920 | tf_op jit(solution)/shard_map/ppermute | solution.py:25
  223.7 27.5 %collective-permute-start.87 = (bf16[256,192]{1,0:T(8,128)(2,1)}, bf16[256,192]{1,0:T(8,128)(2,1)}, u32[]{:S(2)}, u32[]{:S(2)}) collective-permute-start(bf16[256,192]{1,0:T(8,128)(2,1)} %get-tuple-element.13), channel_id=1, source_target_pairs={{0,8},{4,12},{8,0},{12,4},{1,9},{5,13},{9,1},{13,5},{2,10},{6,14},... | collective-permute-start | bytes 294920 | tf_op jit(solution)/shard_map/ppermute | solution.py:25
  224.9 36.8 %collective-permute-start.82 = (bf16[256,3072]{1,0:T(8,128)(2,1)}, bf16[256,3072]{1,0:T(8,128)(2,1)}, u32[]{:S(2)}, u32[]{:S(2)}) collective-permute-start(bf16[256,3072]{1,0:T(8,128)(2,1)} %collective-permute-done.81), channel_id=1, source_target_pairs={{0,4},{4,0},{8,12},{12,8},{1,5},{5,1},{9,13},{13,9},{2,6},{6,2},{1... | collective-permute-start | bytes 4718600 | tf_op jit(solution)/shard_map/ppermute | solution.py:25
  237.7 10.4 %collective-permute-start.90 = (bf16[256,768]{1,0:T(8,128)(2,1)S(1)}, bf16[256,768]{1,0:T(8,128)(2,1)S(1)}, u32[]{:S(2)}, u32[]{:S(2)}) collective-permute-start(bf16[256,768]{1,0:T(8,128)(2,1)S(1)} %multiply_convert_fusion), channel_id=1, source_target_pairs={{0,8},{4,12},{8,0},{12,4},{1,9},{5,13},{9,1},{13,5},{2,10},{6,14},... | collective-permute-start | bytes 1179656 | tf_op jit(solution)/shard_map/ppermute | solution.py:25
  241.1 15.3 %collective-permute-start.89 = (bf16[256,768]{1,0:T(8,128)(2,1)S(1)}, bf16[256,768]{1,0:T(8,128)(2,1)S(1)}, u32[]{:S(2)}, u32[]{:S(2)}) collective-permute-start(bf16[256,768]{1,0:T(8,128)(2,1)S(1)} %multiply_convert_fusion), channel_id=1, source_target_pairs={{0,4},{4,0},{8,12},{12,8},{1,5},{5,1},{9,13},{13,9},{2,6},{6,2},{1... | collective-permute-start | bytes 1179656 | tf_op jit(solution)/shard_map/ppermute | solution.py:25
  256.3 18.7 %collective-permute-start.77 = (bf16[256,192]{1,0:T(8,128)(2,1)S(1)}, bf16[256,192]{1,0:T(8,128)(2,1)S(1)}, u32[]{:S(2)}, u32[]{:S(2)}) collective-permute-start(bf16[256,192]{1,0:T(8,128)(2,1)S(1)} %get-tuple-element.22), channel_id=1, source_target_pairs={{0,4},{4,0},{8,12},{12,8},{1,5},{5,1},{9,13},{13,9},{2,6},{6,2},{1... | collective-permute-start | bytes 294920 | tf_op jit(solution)/shard_map/ppermute | solution.py:25
  256.4 20.3 %collective-permute-start.78 = (bf16[256,192]{1,0:T(8,128)(2,1)S(1)}, bf16[256,192]{1,0:T(8,128)(2,1)S(1)}, u32[]{:S(2)}, u32[]{:S(2)}) collective-permute-start(bf16[256,192]{1,0:T(8,128)(2,1)S(1)} %get-tuple-element.21), channel_id=1, source_target_pairs={{0,8},{4,12},{8,0},{12,4},{1,9},{5,13},{9,1},{13,5},{2,10},{6,14},... | collective-permute-start | bytes 294920 | tf_op jit(solution)/shard_map/ppermute | solution.py:25
  256.7 20.0 %collective-permute-start.79 = (bf16[256,192]{1,0:T(8,128)(2,1)S(1)}, bf16[256,192]{1,0:T(8,128)(2,1)S(1)}, u32[]{:S(2)}, u32[]{:S(2)}) collective-permute-start(bf16[256,192]{1,0:T(8,128)(2,1)S(1)} %get-tuple-element.20), channel_id=1, source_target_pairs={{0,12},{4,8},{8,4},{12,0},{1,13},{5,9},{9,5},{13,1},{2,14},{6,10},... | collective-permute-start | bytes 294920 | tf_op jit(solution)/shard_map/ppermute | solution.py:25
  260.9 22.0 %collective-permute-start.92 = (bf16[192,192]{1,0:T(8,128)(2,1)S(1)}, bf16[192,192]{1,0:T(8,128)(2,1)S(1)}, u32[]{:S(2)}, u32[]{:S(2)}) collective-permute-start(bf16[192,192]{1,0:T(8,128)(2,1)S(1)} %get-tuple-element.8), channel_id=1, source_target_pairs={{0,3},{1,0},{2,1},{3,2},{4,7},{5,4},{6,5},{7,6},{8,11},{9,8},{10,9... | collective-permute-start | bytes 221192 | tf_op jit(solution)/shard_map/ppermute | solution.py:21
  261.7 28.4 %collective-permute-start.93 = (bf16[192,192]{1,0:T(8,128)(2,1)}, bf16[192,192]{1,0:T(8,128)(2,1)S(1)}, u32[]{:S(2)}, u32[]{:S(2)}) collective-permute-start(bf16[192,192]{1,0:T(8,128)(2,1)} %get-tuple-element.10), channel_id=1, source_target_pairs={{0,2},{1,3},{2,0},{3,1},{4,6},{5,7},{6,4},{7,5},{8,10},{9,11},{10,... | collective-permute-start | bytes 221192 | tf_op jit(solution)/shard_map/ppermute | solution.py:21
  275.1 15.0 %collective-permute-start.94 = (bf16[192,192]{1,0:T(8,128)(2,1)}, bf16[192,192]{1,0:T(8,128)(2,1)S(1)}, u32[]{:S(2)}, u32[]{:S(2)}) collective-permute-start(bf16[192,192]{1,0:T(8,128)(2,1)} %get-tuple-element.9), channel_id=1, source_target_pairs={{0,1},{1,2},{2,3},{3,0},{4,5},{5,6},{6,7},{7,4},{8,9},{9,10},{10,1... | collective-permute-start | bytes 221192 | tf_op jit(solution)/shard_map/ppermute | solution.py:21
  278.0 12.9 %collective-permute-start.83 = (bf16[192,768]{1,0:T(8,128)(2,1)}, bf16[192,768]{1,0:T(8,128)(2,1)}, u32[]{:S(2)}, u32[]{:S(2)}) collective-permute-start(bf16[192,768]{1,0:T(8,128)(2,1)} %fusion.39), channel_id=1, source_target_pairs={{0,3},{1,0},{2,1},{3,2},{4,7},{5,4},{6,5},{7,6},{8,11},{9,8},{10,9... | collective-permute-start | bytes 884744 | tf_op jit(solution)/shard_map/ppermute | solution.py:21
  279.7 20.9 %collective-permute-start.84 = (bf16[192,768]{1,0:T(8,128)(2,1)}, bf16[192,768]{1,0:T(8,128)(2,1)}, u32[]{:S(2)}, u32[]{:S(2)}) collective-permute-start(bf16[192,768]{1,0:T(8,128)(2,1)} %fusion.42), channel_id=1, source_target_pairs={{0,2},{1,3},{2,0},{3,1},{4,6},{5,7},{6,4},{7,5},{8,10},{9,11},{10,... | collective-permute-start | bytes 884744 | tf_op jit(solution)/shard_map/ppermute | solution.py:21
  282.9 24.0 %collective-permute-start.85 = (bf16[192,768]{1,0:T(8,128)(2,1)}, bf16[192,768]{1,0:T(8,128)(2,1)}, u32[]{:S(2)}, u32[]{:S(2)}) collective-permute-start(bf16[192,768]{1,0:T(8,128)(2,1)} %fusion.45), channel_id=1, source_target_pairs={{0,1},{1,2},{2,3},{3,0},{4,5},{5,6},{6,7},{7,4},{8,9},{9,10},{10,1... | collective-permute-start | bytes 884744 | tf_op jit(solution)/shard_map/ppermute | solution.py:21
  (102 other events, 820.7 us)

commit v2 on v1

v2 whole, which is shorter than its diff:
```python
import jax
import jax.numpy as jnp
from jax import lax
from jax.experimental import pallas as pl
from jax.experimental.pallas import tpu as pltpu
from jax.sharding import PartitionSpec as P

F32 = jnp.float32
BF16 = jnp.bfloat16


def quick_gelu(values):
    return values * jax.nn.sigmoid(1.702 * values)


def gelu_slope(values):
    sigmoid = jax.nn.sigmoid(1.702 * values)
    return sigmoid + 1.702 * values * sigmoid * (1.0 - sigmoid)


def shift(value, axis, step):
    count = lax.axis_size(axis)
    return lax.ppermute(value, axis, [(i, (i + step) % count) for i in range(count)])


def swap(value, axis, bit):
    return lax.ppermute(value, axis, [(i, i ^ bit) for i in range(lax.axis_size(axis))])


def ring(value, *earlier):
    blocks = [value]
    for step in range(1, lax.axis_size("gcol")):
        part = after(blocks[-1], *earlier) if step == 2 and earlier else blocks[-1]
        blocks.append(shift(part, "gcol", 1))
    return blocks


def grow_bits(last):
    bits, bit = [], lax.axis_size("grow") // 2
    while bit >= last:
        bits.append(bit)
        bit //= 2
    return bits


class Lane:
    def __init__(self):
        self.last = None

    def __call__(self, value, bit, *earlier):
        if self.last is not None:
            earlier = (*earlier, self.last)
        if earlier:
            value = after(value, *earlier)
        self.last = swap(value, "grow", bit)
        return self.last


def spread(value, lane=None, *earlier):
    table = {0: value}
    for bit in grow_bits(2):
        for j in list(table):
            table[j ^ bit] = lane(table[j], bit, *earlier) if lane else swap(table[j], "grow", bit)
    return table


def after(value, *earlier):
    return lax.optimization_barrier((value, *earlier))[0]


def dot_tn(left, right):
    return lax.dot_general(left, right, (((0,), (0,)), ((), ())), preferred_element_type=F32)


def dot_nt(left, right):
    return lax.dot_general(left, right, (((1,), (1,)), ((), ())), preferred_element_type=F32)


def dot_nn(left, right):
    return jnp.dot(left, right, preferred_element_type=F32)


def call(kernel, outs, *operands, name, in_specs=None, scalars=0):
    vmem, smem = pl.BlockSpec(memory_space=pltpu.VMEM), pl.BlockSpec(memory_space=pltpu.SMEM)
    specs = [smem] * scalars + [vmem] * (len(operands) - scalars)
    for place, spec in (in_specs or {}).items():
        specs[place] = spec
    return pl.pallas_call(
        kernel,
        out_shape=[jax.ShapeDtypeStruct(shape, dtype) for shape, dtype in outs],
        in_specs=specs,
        out_specs=[vmem] * len(outs),
        compiler_params=pltpu.CompilerParams(vmem_limit_bytes=56 * 1024 * 1024),
        cost_estimate=pl.CostEstimate(flops=1, bytes_accessed=1, transcendentals=0),
        name=name,
    )(*operands)


def activate(places, preact, block):
    rows, inner = preact.shape
    count = inner // block

    def kernel(places_ref, preact_ref, *outs):
        for k in range(count):
            start = pl.multiple_of(places_ref[k] * block, 128)
            outs[k][...] = quick_gelu(preact_ref[:, pl.ds(start, block)].astype(F32)).astype(BF16)

    outs = [((rows, block), BF16)] * count
    return call(kernel, outs, places, preact, name="activate", scalars=1)


def score_rows(log_scale, mine, mate, others, device_count):
    rows = mine.shape[0]
    width = others.shape[0]

    def kernel(scale_ref, mine_ref, mate_ref, others_ref, scores_mine, scores_mate, lse):
        halves = (scores_mine, scores_mate)
        logit_scale = scale_ref[0, 0]
        for half, ref in enumerate((mine_ref, mate_ref)):
            scores = halves[half]
            largest = None
            for place in range(0, width, 256):
                part = logit_scale * dot_nt(ref[...], others_ref[place : place + 256])
                scores[:, place : place + 256] = part
                here = jnp.max(part, axis=1, keepdims=True)
                largest = here if largest is None else jnp.maximum(largest, here)
            total = jnp.zeros_like(largest)
            for place in range(0, width, 256):
                part = scores[:, place : place + 256]
                total += jnp.sum(jnp.exp(part - largest), axis=1, keepdims=True)
            value = jnp.broadcast_to(largest + jnp.log(total), (rows, 128))
            row = value.T[:1]
            for device in range(device_count):
                lse[device, :, half * rows : (half + 1) * rows] = row

    outs = [((rows, width), F32)] * 2 + [((device_count, 1, 2 * rows), F32)]
    scale = jnp.exp(log_scale).reshape(1, 1)
    return call(kernel, outs, scale, mine, mate, others, name="scores", scalars=1)


def combine_lse(where, lse_all, count):
    rows = lse_all.shape[2] // 2

    def kernel(where_ref, lse_ref, column, row):
        def part(place, side):
            return lse_ref[where_ref[place]][:, side * rows : (side + 1) * rows]

        def log_add(left, right):
            top = jnp.maximum(left, right)
            return top + jnp.log(jnp.exp(left - top) + jnp.exp(right - top))

        for side in range(2):
            own = log_add(part(0, side), part(1, 1 - side))
            column[side * rows : (side + 1) * rows] = jnp.broadcast_to(own, (128, rows)).T[:, :1]
        for step in range(count):
            other = log_add(part(2 + 2 * step, 0), part(3 + 2 * step, 1))
            row[:, step * rows : (step + 1) * rows] = other

    outs = [((2 * rows, 1), F32), ((1, count * rows), F32)]
    return call(kernel, outs, where, lse_all, name="combine", scalars=1)


def all_terms(places, proj_own, rights, streams, embeds, columns):
    pieces, depth, width = len(embeds), proj_own.shape[0], rights[0][0].shape[1]
    rows, count = embeds[0].shape[0], len(rights) + 1

    def kernel(places_ref, proj_ref, *refs):
        embeds, refs = refs[:pieces], refs[pieces:]
        groups = [refs[pieces * i : pieces * (i + 1)] for i in range(len(rights))]
        streams, outs = refs[pieces * len(rights) :][: pieces // 2], refs[pieces * len(rights) + pieces // 2 :]
        left = outs[-1]
        for i, ref in enumerate(embeds):
            turned = dot_nt(proj_ref[...], ref[...]).astype(BF16)
            left[:, i * rows : (i + 1) * rows] = turned
        for i, group in enumerate(groups):
            total = None
            for j, ref in enumerate(group):
                part = dot_nn(left[:, j * rows : (j + 1) * rows], ref[...])
                total = part if total is None else total + part
            outs[i][:, :width] = total.astype(BF16)
        total = None
        for j, ref in enumerate(embeds):
            start = j % 2 * rows
            part = dot_nn(streams[j // 2][start : start + rows].T, ref[...])
            total = part if total is None else total + part
        for place in range(count):
            part = total[:, place * columns : (place + 1) * columns]
            for i in range(len(rights)):

                @pl.when(places_ref[i + 1] == place)
                def _():
                    outs[i][:, width:] = part.astype(BF16)

            @pl.when(places_ref[0] == place)
            def _():
                outs[-2][...] = part

    outs = [((depth, width + columns), BF16)] * len(rights)
    outs += [((depth, columns), F32), ((depth, rows * pieces), BF16)]
    flat = [piece for right in rights for piece in right]
    result = call(kernel, outs, places, proj_own, *embeds, *flat, *streams, name="terms", scalars=1)
    return result[:-2], result[-2], result[-1]


def weight_terms(left, right):
    depth, rows = left.shape[0], right[0].shape[0]

    def kernel(left_ref, *refs):
        out = refs[-1]
        total = None
        for j, ref in enumerate(refs[:-1]):
            part = dot_nn(left_ref[:, j * rows : (j + 1) * rows], ref[...])
            total = part if total is None else total + part
        out[...] = total

    return call(kernel, [((depth, right[0].shape[1]), F32)], left, *right, name="down_own")[0]


def own_gradients(places, found, preact, d_embed, d_stream, proj_mine, proj_rest, down_mine, down_rest):
    rows, inner = preact.shape
    blocks, features = len(d_stream), d_stream[0].shape[1]
    count, block = len(down_mine), down_mine[0].shape[1]
    depth, half = proj_mine.shape[0], blocks // 2

    def kernel(places_ref, found_ref, preact_ref, embed_ref, proj_a, proj_b, *refs):
        stream, refs = refs[:blocks], refs[blocks:]
        down_a, down_b, (d_hidden, d_pre) = refs[:count], refs[count : 2 * count], refs[2 * count :]
        for i in range(blocks):
            place = found_ref[i]
            near = place < half
            start = pl.multiple_of(jnp.where(near, place, place - half) * features, 16)
            rows_a, rows_b = proj_a[pl.ds(start, features)], proj_b[pl.ds(start, features)]
            part = dot_nt(embed_ref[...], jnp.where(near, rows_a, rows_b)).astype(BF16)
            d_hidden[:, i * features : (i + 1) * features] = part
        left = jnp.concatenate([r[...] for r in stream], 1)
        for k in range(count):
            start = pl.multiple_of(places_ref[k] * block, 128)
            d_active = dot_nn(left[:, :depth], down_a[k][...]) + dot_nn(left[:, depth:], down_b[k][...])
            slope = gelu_slope(preact_ref[:, pl.ds(start, block)].astype(F32))
            d_pre[:, pl.ds(start, block)] = (d_active * slope).astype(BF16)

    return call(
        kernel, [((rows, blocks * features), BF16), (preact.shape, BF16)], places, found, preact, d_embed,
        proj_mine, proj_rest, *d_stream, *down_mine, *down_rest, name="own_gradients", scalars=2,
    )


def body(hidden, preact, w_down, projection, log_scale):
    tower_count = lax.axis_size("tower")
    grow_count, gcol_count = lax.axis_size("grow"), lax.axis_size("gcol")
    tower, grow, gcol = (lax.axis_index(a) for a in ("tower", "grow", "gcol"))
    hidden, preact, w_down, projection = hidden[0], preact[0], w_down[0], projection[0]
    features, inner_block = w_down.shape
    columns = projection.shape[1]
    js, ks = range(grow_count), range(gcol_count)
    evens = range(0, grow_count, 2)
    last = evens[-1]
    order = [(j, k) for j in evens for k in ks]
    sources = [lax.rem(gcol - k + gcol_count, gcol_count) for k in ks]
    far, core = (Lane(), Lane()), Lane()
    places = jnp.stack(sources)
    found = [((grow ^ j) >> 1) + ((grow ^ j) & 1) * (grow_count // 2) for j in js]
    places, found = lax.optimization_barrier((places, jnp.stack(found)))
    chunks = range(2)

    active = activate(places, preact, inner_block)
    down_ring = ring(w_down)
    proj_ring = [projection]
    for k in ks[1:]:
        pace = () if k == 1 else (down_ring[k - 1],)
        proj_ring.append(shift(after(proj_ring[-1], *pace), "gcol", 1))
    down_tables = [spread(part, far[0]) for part in down_ring]
    active_even = {0: spread(active[0], None)}
    proj_own = jnp.roll(jnp.concatenate(proj_ring[::-1], 1), (gcol + 1) * columns, 1)
    proj_even = spread(proj_own)
    proj_pair = jnp.concatenate([proj_even[j] for j in evens], 0)
    proj_mate = swap(proj_pair, "grow", 1)
    proj_all = jnp.concatenate([proj_pair, proj_mate], 0)
    down_pair = [jnp.concatenate([table[j] for j in evens], 0) for table in down_tables]
    active_mate = [core(part, 1) for part in active]
    hidden_parts = [
        lax.dynamic_slice_in_dim(hidden, (grow ^ j) * features, features, 1) for j in js
    ]
    hidden_mine = jnp.concatenate([hidden_parts[j] for j in evens], 1)
    hidden_mate = core(jnp.concatenate([hidden_parts[j + 1] for j in evens], 1), 1)

    stream = jnp.concatenate([hidden_mine, hidden_mate], 0).astype(F32)
    stream = stream + sum(
        dot_nt(jnp.concatenate([active[k], active_mate[k]], 0), down_pair[k]) for k in ks
    )
    stream = stream.astype(BF16)
    own_rows = hidden.shape[0]
    stream_rest = swap(stream[own_rows:], "grow", 1)
    stream_b = jnp.concatenate([stream[:own_rows], stream_rest], 1)
    embed = after(dot_nn(stream_b, proj_all), active_even[0][last])
    inverse = lax.rsqrt(jnp.sum(embed * embed, axis=1, keepdims=True) + 1e-06)
    unit = embed * inverse
    unit_b = unit.astype(BF16)

    (
        unit, unit_b, inverse, stream, proj_pair, proj_mate, proj_all, down_pair, active, active_mate, preact, active_even
    ) = lax.optimization_barrier(
        (unit, unit_b, inverse, stream, proj_pair, proj_mate, proj_all, down_pair, active, active_mate, preact, active_even)
    )
    far, core = (Lane(), Lane()), Lane()
    active_even[1] = spread(active[1])

    unit_mate = swap(unit_b, "grow", 1)
    rings = [
        ring(after(swap(part, "tower", 1), active_even[1][last]))
        for part in jnp.split(unit_b, 2, 0)
    ]
    pieces = {(k, q): spread(rings[q][k], far[q]) for k in ks for q in chunks}
    others = jnp.concatenate([pieces[k, q][j] for j, k in order for q in chunks], 0)
    device_count = tower_count * grow_count * gcol_count
    others, unit_mate, unit_b, active_even, stream, active, log_scale = lax.optimization_barrier(
        (others, unit_mate, unit_b, active_even, stream, active, log_scale)
    )
    scores_own, scores_mate, lse = score_rows(log_scale, unit_b, unit_mate, others, device_count)
    lse_all = lax.all_to_all(lse, ("tower", "grow", "gcol"), 0, 0)

    far = (Lane(), Lane())
    for k in ks[2:]:
        active_even[k] = spread(active[k])
    stream_blocks = [stream[:, i * features : (i + 1) * features] for i in range(len(evens))]
    stream_even = {0: stream_blocks[0]}
    for i, j in enumerate(evens[1:], 1):
        stream_even[j] = swap(stream_blocks[i], "grow", j)
    core = Lane()
    active_odd = {k: {j: core(active_even[k][j], 1, others) for j in evens[1:]} for k in ks}

    def device(tower_of, j, k):
        return (tower_of * grow_count + (grow ^ j)) * gcol_count + sources[k]

    where = [device(tower, 0, 0), device(tower, 1, 0)]
    for j, k in order:
        where += [device(1 - tower, j, k), device(1 - tower, j ^ 1, k)]
    row_lse, other_lse = combine_lse(jnp.stack(where), lse_all, len(order))
    logit_scale = jnp.exp(log_scale)

    def embed_gradient(part, lse, diagonal):
        grad = 0.5 * (jnp.exp(part - lse) + jnp.exp(part - other_lse))
        return logit_scale * dot_nn((grad - diagonal).astype(BF16), others)

    row_index = lax.broadcasted_iota(jnp.int32, scores_own.shape, 0)
    column_index = lax.broadcasted_iota(jnp.int32, scores_own.shape, 1)
    diagonal = (row_index == column_index).astype(F32)
    arrived = [stream_even[last]] + [active_even[k][last] for k in ks[2:]]
    for_mate = embed_gradient(after(scores_mate, *arrived), row_lse[own_rows:], 0.0)
    for_own = embed_gradient(after(scores_own, for_mate), row_lse[:own_rows], diagonal)
    d_unit = for_own + swap(for_mate, "grow", 1)
    along = jnp.sum(unit * d_unit, axis=1, keepdims=True)
    d_embed = (inverse * (d_unit - unit * along)).astype(BF16)
    for_barrier = (d_embed, active_even, active_odd, stream_even, down_pair, proj_all, for_mate)
    for_barrier = lax.optimization_barrier(for_barrier)
    d_embed, active_even, active_odd, stream_even, down_pair, proj_all, for_mate = for_barrier
    rel = [*evens, *(j + 1 for j in evens)]
    d_stream = [
        dot_nt(d_embed, proj_all[i * features : (i + 1) * features]).astype(BF16) for i in js
    ]
    rights = []
    for k in ks:
        parts = {0: active[k], 1: active_mate[k]}
        for j in evens[1:]:
            parts[j], parts[j + 1] = active_even[k][j], active_odd[k][j]
        rights.append([parts[j] for j in js])
    embed_rows = {}
    for j, part in spread(d_embed).items():
        embed_rows[j], embed_rows[j + 1] = part, swap(part, "grow", 1)
    away = [*ks[1:]]
    terms, grad_proj, left = all_terms(
        places, proj_pair[:features], [rights[k] for k in away], [stream_even[j] for j in evens],
        [embed_rows[j] for j in js], columns,
    )
    sent = [shift(term, "gcol", -k) for k, term in zip(away, terms)]
    rights[0][0] = after(rights[0][0], *terms)
    grad_down = weight_terms(left, rights[0])

    down_mate = [swap(after(part, *terms), "grow", 1) for part in down_pair]
    d_hidden, d_pre = own_gradients(
        places, found, preact, after(d_embed, *terms), d_stream, proj_pair, proj_mate, down_pair, down_mate
    )
    grad_down, grad_proj = after(grad_down, d_pre, d_hidden), after(grad_proj, d_pre, d_hidden)
    for part in sent:
        grad_down = grad_down + part[:, :inner_block].astype(F32)
        grad_proj = grad_proj + part[:, inner_block:].astype(F32)
    return (d_hidden[None], d_pre[None], grad_down[None], grad_proj[None])


def solution(mesh):
    placed = (
        P("tower", ("grow", "gcol"), None),
        P("tower", ("grow", "gcol"), None),
        P("tower", "grow", "gcol"),
        P("tower", "grow", "gcol"),
        P(),
    )
    return jax.shard_map(
        body, mesh=mesh, in_specs=placed, out_specs=placed[:4], check_vma=False
    )
```

time: 314 us -> 209 us (0.67); the launches traced: 310 us -> 208 us
  waiting for transfers between devices: 125 us -> 75.9 us
  Pallas kernels: 0 us -> 26.3 us
  starting transfers between devices: 91.9 us -> 66 us
  local copies, waits for them, and re-layouts: 38.1 us -> 15.1 us
  other arithmetic: 24.5 us -> 7.66 us
  matrix products: 27.7 us -> 15.5 us
    ppermute x74 -> x40, waiting for transfers between devices: 80.4 us -> 34.9 us  [swap(): lax.ppermute(value, axis, [(i, i ^ bit) for i in range(lax.axis_size(axis...]
    pallas_call x0 -> x6, Pallas kernels: none -> 26.3 us  [call(): pl.pallas_call(kernel, out_shape=[jax.ShapeDtypeStruct(shape, dtype) for...]
    ppermute x74 -> x40, starting transfers between devices: 62 us -> 35.8 us  [swap(): lax.ppermute(value, axis, [(i, i ^ bit) for i in range(lax.axis_size(axis...]
    concatenate x6 -> x4, other arithmetic: 18.5 us -> 2.99 us  [the longest x1 1.17 us: body(): proj_all = jnp.concatenate([proj_pair, proj_mate], 0)]
    unnamed x137 -> x106, local copies, waits for them, and re-layouts: 18.8 us -> 5.26 us
    dot_general x5 -> x0, matrix products: 8.44 us -> none  [dot_tn(): lax.dot_general(left, right, (((0,), (0,)), ((), ())), preferred_element_...]
    all_to_all x1, starting transfers between devices: 6.61 us -> 13.7 us  [body(): lse_all = lax.all_to_all(lse, ('tower', 'grow', 'gcol'), 0, 0)]
    ppermute x21 -> x15, starting transfers between devices: 23.2 us -> 16.5 us  [shift(): lax.ppermute(value, axis, [(i, (i + step) % count) for i in range(count)])]
  transfers between devices with their start and end apart: 96 -> 56, of which waited for: 41 -> 25; matrix products, arithmetic and copies ran while one was open for 26% -> 15% of each run, Pallas kernels for 0% -> 9%
where the time goes in v2:
time: 209 us; the launch traced here: 208 us
  waiting for transfers between devices  75.9 us (36%)
  starting transfers between devices  66 us (32%)
  Pallas kernels  26.3 us (13%)
  matrix products  15.5 us (7%)
  local copies, waits for them, and re-layouts  15.1 us (7%)
  other arithmetic  7.66 us (4%)
    ppermute x15, waiting for transfers between devices, shift(): lax.ppermute(value, axis, [(i, (i + step) % count) for i in range(count)])  38.2 us
    ppermute x40, starting transfers between devices, swap(): lax.ppermute(value, axis, [(i, i ^ bit) for i in range(lax.axis_size(axis...  35.8 us
    ppermute x40, waiting for transfers between devices, swap(): lax.ppermute(value, axis, [(i, i ^ bit) for i in range(lax.axis_size(axis...  34.9 us
    pallas_call x6, Pallas kernels, call(): pl.pallas_call(kernel, out_shape=[jax.ShapeDtypeStruct(shape, dtype) for...  26.3 us
    ppermute x15, starting transfers between devices, shift(): lax.ppermute(value, axis, [(i, (i + step) % count) for i in range(count)])  16.5 us
    all_to_all x1, starting transfers between devices, body(): lse_all = lax.all_to_all(lse, ('tower', 'grow', 'gcol'), 0, 0)  13.7 us
    dot_general x8, matrix products, dot_nt(): lax.dot_general(left, right, (((1,), (1,)), ((), ())), preferred_element_...  9.56 us
    dot_general x3, matrix products, dot_nn(): return jnp.dot(left, right, preferred_element_type=F32)  5.93 us
  transfers between devices with their start and end apart: 56, of which 25 were waited for; matrix products, arithmetic and copies ran while one was open for 15% of the time, Pallas kernels for 9%

profile of v2, /device:TPU:9, one launch (start us, length us, event | category | flops | bytes accessed | tf_op | source)
XLA Modules:
  0.0 208.5 jit_solution(17683363654584823924)
XLA Ops:
  3.9 2.8 %activate.1 = (bf16[256,768]{1,0:T(8,128)(2,1)}, bf16[256,768]{1,0:T(8,128)(2,1)}, bf16[256,768]{1,0:T(8,128)(2,1)}, bf16[256,768]{1,0:T(8,128)(2,1)}) custom-call(s32[4]{0:T(128)} %get-tuple-element.102.places_ref, bf16[256,3072]{1,0:T(8,128)(2,1)} %bitcast.56), custom_call_target="tpu_custom_call" | custom-call | flops 1 | bytes 1 | tf_op jit(solution)/shard_map/activate/pallas_call | solution.py:88
  15.2 3.8 %collective-permute-start.1 = (bf16[256,768]{1,0:T(8,128)(2,1)}, bf16[256,768]{1,0:T(8,128)(2,1)}, u32[]{:S(2)}, u32[]{:S(2)}) collective-permute-start(bf16[256,768]{1,0:T(8,128)(2,1)} %get-tuple-element.163.refs_4_), channel_id=1, source_target_pairs={{0,4},{4,0},{8,12},{12,8},{1,5},{5,1},{9,13},{13,9},{2,6},{6,2},{1... | collective-permute-start | bytes 1179656 | tf_op jit(solution)/shard_map/ppermute | solution.py:27
  19.0 6.6 %collective-permute-done.7 = bf16[192,768]{1,0:T(8,128)(2,1)S(1)} collective-permute-done((bf16[192,768]{1,0:T(8,128)(2,1)S(1)}, bf16[192,768]{1,0:T(8,128)(2,1)S(1)}, u32[]{:S(2)}, u32[]{:S(2)}) %collective-permute-start.7) | collective-permute-done | bytes 294944 | tf_op jit(solution)/shard_map/ppermute | solution.py:27
  27.3 2.4 %collective-permute-done.15 = bf16[192,192]{1,0:T(8,128)(2,1)S(1)} collective-permute-done((bf16[192,192]{1,0:T(8,128)(2,1)S(1)}, bf16[192,192]{1,0:T(8,128)(2,1)S(1)}, u32[]{:S(2)}, u32[]{:S(2)}) %collective-permute-start.15) | collective-permute-done | bytes 73760 | tf_op jit(solution)/shard_map/ppermute | solution.py:23
  31.7 3.1 %collective-permute-start.2 = (bf16[256,768]{1,0:T(8,128)(2,1)S(1)}, bf16[256,768]{1,0:T(8,128)(2,1)S(1)}, u32[]{:S(2)}, u32[]{:S(2)}) collective-permute-start(bf16[256,768]{1,0:T(8,128)(2,1)S(1)} %copy-done.19), channel_id=1, source_target_pairs={{0,4},{4,0},{8,12},{12,8},{1,5},{5,1},{9,13},{13,9},{2,6},{6,2},{1... | collective-permute-start | bytes 1179656 | tf_op jit(solution)/shard_map/ppermute | solution.py:27
  39.8 1.6 collective-permute-start.3
  41.5 1.6 collective-permute-start.17
  43.1 2.7 %collective-permute-done.11 = bf16[192,768]{1,0:T(8,128)(2,1)S(1)} collective-permute-done((bf16[192,768]{1,0:T(8,128)(2,1)}, bf16[192,768]{1,0:T(8,128)(2,1)S(1)}, u32[]{:S(2)}, u32[]{:S(2)}) %collective-permute-start.11) | collective-permute-done | bytes 294944 | tf_op jit(solution)/shard_map/ppermute | solution.py:27
  46.5 2.0 collective-permute-start.4
  59.0 3.2 %collective-permute-done.19 = bf16[128,768]{1,0:T(8,128)(2,1)} collective-permute-done((bf16[128,768]{1,0:T(8,128)(2,1)}, bf16[128,768]{1,0:T(8,128)(2,1)}, u32[]{:S(2)}, u32[]{:S(2)}) %collective-permute-start.19) | collective-permute-done | bytes 196640 | tf_op jit(solution)/shard_map/ppermute | solution.py:27
  62.2 3.3 %collective-permute-done.20.refs_6_ = bf16[256,768]{1,0:T(8,128)(2,1)} collective-permute-done((bf16[256,768]{1,0:T(8,128)(2,1)S(1)}, bf16[256,768]{1,0:T(8,128)(2,1)}, u32[]{:S(2)}, u32[]{:S(2)}) %collective-permute-start.20) | collective-permute-done | bytes 393248 | tf_op jit(solution)/shard_map/ppermute | solution.py:27
  72.4 3.2 %collective-permute-done.23 = bf16[128,768]{1,0:T(8,128)(2,1)S(1)} collective-permute-done((bf16[128,768]{1,0:T(8,128)(2,1)}, bf16[128,768]{1,0:T(8,128)(2,1)S(1)}, u32[]{:S(2)}, u32[]{:S(2)}) %collective-permute-start.23) | collective-permute-done | bytes 196640 | tf_op jit(solution)/shard_map/ppermute | solution.py:23
  76.9 2.3 %collective-permute-start.25 = (bf16[128,768]{1,0:T(8,128)(2,1)S(1)}, bf16[128,768]{1,0:T(8,128)(2,1)S(1)}, u32[]{:S(2)}, u32[]{:S(2)}) collective-permute-start(bf16[128,768]{1,0:T(8,128)(2,1)S(1)} %collective-permute-done.23), channel_id=1, source_target_pairs={{0,1},{1,2},{2,3},{3,0},{4,5},{5,6},{6,7},{7,4},{8,9},{9,10},{10,1... | collective-permute-start | bytes 589832 | tf_op jit(solution)/shard_map/ppermute | solution.py:23
  79.3 3.0 %collective-permute-done.24 = bf16[128,768]{1,0:T(8,128)(2,1)S(1)} collective-permute-done((bf16[128,768]{1,0:T(8,128)(2,1)S(1)}, bf16[128,768]{1,0:T(8,128)(2,1)S(1)}, u32[]{:S(2)}, u32[]{:S(2)}) %collective-permute-start.24) | collective-permute-done | bytes 196640 | tf_op jit(solution)/shard_map/ppermute | solution.py:23
  86.1 2.8 %collective-permute-start.27 = (bf16[128,768]{1,0:T(8,128)(2,1)S(1)}, bf16[128,768]{1,0:T(8,128)(2,1)S(1)}, u32[]{:S(2)}, u32[]{:S(2)}) collective-permute-start(bf16[128,768]{1,0:T(8,128)(2,1)S(1)} %collective-permute-done.25), channel_id=1, source_target_pairs={{0,1},{1,2},{2,3},{3,0},{4,5},{5,6},{6,7},{7,4},{8,9},{9,10},{10,1... | collective-permute-start | bytes 589832 | tf_op jit(solution)/shard_map/ppermute | solution.py:23
  88.9 4.9 %collective-permute-done.26 = bf16[128,768]{1,0:T(8,128)(2,1)S(1)} collective-permute-done((bf16[128,768]{1,0:T(8,128)(2,1)S(1)}, bf16[128,768]{1,0:T(8,128)(2,1)S(1)}, u32[]{:S(2)}, u32[]{:S(2)}) %collective-permute-start.26) | collective-permute-done | bytes 196640 | tf_op jit(solution)/shard_map/ppermute | solution.py:23
  94.0 2.5 %collective-permute-done.27 = bf16[128,768]{1,0:T(8,128)(2,1)S(1)} collective-permute-done((bf16[128,768]{1,0:T(8,128)(2,1)S(1)}, bf16[128,768]{1,0:T(8,128)(2,1)S(1)}, u32[]{:S(2)}, u32[]{:S(2)}) %collective-permute-start.27) | collective-permute-done | bytes 196640 | tf_op jit(solution)/shard_map/ppermute | solution.py:23
  97.0 1.7 collective-permute-done.34
  98.7 2.4 %collective-permute-done.35 = bf16[128,768]{1,0:T(8,128)(2,1)S(1)} collective-permute-done((bf16[128,768]{1,0:T(8,128)(2,1)S(1)}, bf16[128,768]{1,0:T(8,128)(2,1)S(1)}, u32[]{:S(2)}, u32[]{:S(2)}) %collective-permute-start.35) | collective-permute-done | bytes 196640 | tf_op jit(solution)/shard_map/ppermute | solution.py:27
  102.9 5.4 %scores.1 = (f32[256,2048]{1,0:T(8,128)}, f32[256,2048]{1,0:T(8,128)}, f32[32,1,512]{2,1,0:T(1,128)}) custom-call(f32[1,1]{1,0:T(1,128)} %bitcast.17.scale_ref, bf16[256,768]{1,0:T(8,128)(2,1)} %copy-done.5, bf16[256,768]{1,0:T(8,128)(2,1)} %copy-done.34, bf16[2048,768]{1,0:T(8,128)(2,1)} %copy-done.1), custom_call_target="tpu_custom_call" | custom-call | flops 1 | bytes 1 | tf_op jit(solution)/shard_map/scores/pallas_call | solution.py:88
  108.3 13.7 %all-to-all-start = ((f32[32,1,512]{2,1,0:T(1,128)}), f32[32,1,512]{2,1,0:T(1,128)}, u32[]{:S(2)}, u32[]{:S(2)}) async-start(f32[32,1,512]{2,1,0:T(1,128)} %get-tuple-element.145), calls=%async_computation | async-start | bytes 131072 | tf_op jit(solution)/shard_map/all_to_all | solution.py:320
  125.1 2.9 %all-to-all-done.lse_ref = f32[32,1,512]{2,1,0:T(1,128)} async-done(((f32[32,1,512]{2,1,0:T(1,128)}), f32[32,1,512]{2,1,0:T(1,128)}, u32[]{:S(2)}, u32[]{:S(2)}) %all-to-all-start) | async-done | bytes 65568 | tf_op jit(solution)/shard_map/all_to_all | solution.py:320
  128.0 1.7 combine.1
  132.6 4.0 %convolution_multiply_fusion.1 = f32[256,768]{1,0:T(8,128)S(1)} fusion(bf16[2048,768]{1,0:T(8,128)(2,1)} %copy-done.1, f32[256,2048]{1,0:T(8,128)} %get-tuple-element.144, f32[2048]{0:T(1024)} %bitcast.67, f32[256]{0:T(256)S(1)} %get-tuple-element.201, f32[]{:T(128)} %exp.16), kind=kOutput, calls=%fused_computation.4 | convolution fusion | flops 808124416 | bytes 6038532 | tf_op jit(solution)/shard_map/dot_general | solution.py:80
  137.3 2.3 %collective-permute-done.43.refs_11_ = bf16[256,768]{1,0:T(8,128)(2,1)S(1)} collective-permute-done((bf16[256,768]{1,0:T(8,128)(2,1)S(1)}, bf16[256,768]{1,0:T(8,128)(2,1)S(1)}, u32[]{:S(2)}, u32[]{:S(2)}) %collective-permute-start.43) | collective-permute-done | bytes 393248 | tf_op jit(solution)/shard_map/ppermute | solution.py:27
  143.1 8.7 %collective-permute-done.46.refs_2_ = bf16[256,768]{1,0:T(8,128)(2,1)S(1)} collective-permute-done((bf16[256,768]{1,0:T(8,128)(2,1)S(1)}, bf16[256,768]{1,0:T(8,128)(2,1)S(1)}, u32[]{:S(2)}, u32[]{:S(2)}) %collective-permute-start.46) | collective-permute-done | bytes 393248 | tf_op jit(solution)/shard_map/ppermute | solution.py:27
  155.3 6.7 %terms.1 = (bf16[192,960]{1,0:T(8,128)(2,1)}, bf16[192,960]{1,0:T(8,128)(2,1)}, bf16[192,960]{1,0:T(8,128)(2,1)}, f32[192,192]{1,0:T(8,128)}, bf16[192,1024]{1,0:T(8,128)(2,1)}) custom-call(s32[4]{0:T(128)} %get-tuple-element.102.places_ref, bf16[192,768]{1,0:T(8,128)(2,1)} %slice.57.proj_ref, bf16[256,768]{1,0:T(8,128)(2,1)} %copy-done.3, ...), custom_call_target="tpu_custom_call" | custom-call | flops 1 | bytes 1 | tf_op jit(solution)/shard_map/terms/pallas_call | solution.py:88
  174.9 2.8 %down_own.1 = f32[192,768]{1,0:T(8,128)} custom-call(bf16[192,1024]{1,0:T(8,128)(2,1)} %get-tuple-element.191.left_ref, bf16[256,768]{1,0:T(8,128)(2,1)} %get-tuple-element.193.refs_0_, bf16[256,768]{1,0:T(8,128)(2,1)} %copy-done.32, bf16[256,768]{1,0:T(8,128)(2,1)} %collective-permute-done.18.refs_2_, bf16[256,768]{1,0:T(8,128)(2,1)} %collective-permute-done.41.refs_3_), custom_call_target="tpu_custom_call" | custom-call | flops 1 | bytes 1 | tf_op jit(solution)/shard_map/down_own/pallas_call | solution.py:88
  177.7 6.9 %own_gradients.1 = (bf16[256,768]{1,0:T(8,128)(2,1)}, bf16[256,3072]{1,0:T(8,128)(2,1)}) custom-call(s32[4]{0:T(128)} %get-tuple-element.102.places_ref, s32[4]{0:T(128)} %get-tuple-element.103.found_ref, bf16[256,3072]{1,0:T(8,128)(2,1)} %bitcast.57, bf16[256,768]{1,0:T(8,128)(2,1)} %copy-done.3, bf16[384,768]{1,0:T(8,128)(2,1)} %copy-done, ...), custom_call_target="tpu_custom_call" | custom-call | flops 1 | bytes 1 | tf_op jit(solution)/shard_map/own_gradients/pallas_call | solution.py:88
  184.7 17.7 %collective-permute-done.53 = bf16[192,960]{1,0:T(8,128)(2,1)S(1)} collective-permute-done((bf16[192,960]{1,0:T(8,128)(2,1)}, bf16[192,960]{1,0:T(8,128)(2,1)S(1)}, u32[]{:S(2)}, u32[]{:S(2)}) %collective-permute-start.53) | collective-permute-done | bytes 368672 | tf_op jit(solution)/shard_map/ppermute | solution.py:23
  202.3 2.6 %collective-permute-done.52 = bf16[192,960]{1,0:T(8,128)(2,1)S(1)} collective-permute-done((bf16[192,960]{1,0:T(8,128)(2,1)}, bf16[192,960]{1,0:T(8,128)(2,1)S(1)}, u32[]{:S(2)}, u32[]{:S(2)}) %collective-permute-start.52) | collective-permute-done | bytes 368672 | tf_op jit(solution)/shard_map/ppermute | solution.py:23
  204.9 1.9 add_bitcast_fusion
  (231 shorter events, 73.2 us)
Async XLA Ops:
  0.6 8.8 %collective-permute-start.6 = (bf16[192,768]{1,0:T(8,128)(2,1)}, bf16[192,768]{1,0:T(8,128)(2,1)S(1)}, u32[]{:S(2)}, u32[]{:S(2)}) collective-permute-start(bf16[192,768]{1,0:T(8,128)(2,1)} %bitcast.61), channel_id=1, source_target_pairs={{0,1},{1,2},{2,3},{3,0},{4,5},{5,6},{6,7},{7,4},{8,9},{9,10},{10,1... | collective-permute-start | bytes 884744 | tf_op jit(solution)/shard_map/ppermute | solution.py:23
  7.9 46.5 %collective-permute-start.18 = (bf16[256,768]{1,0:T(8,128)(2,1)}, bf16[256,768]{1,0:T(8,128)(2,1)}, u32[]{:S(2)}, u32[]{:S(2)}) collective-permute-start(bf16[256,768]{1,0:T(8,128)(2,1)} %get-tuple-element.193.refs_0_), channel_id=1, source_target_pairs={{0,8},{4,12},{8,0},{12,4},{1,9},{5,13},{9,1},{13,5},{2,10},{6,14},... | collective-permute-start | bytes 1179656 | tf_op jit(solution)/shard_map/ppermute | solution.py:27
  9.9 15.8 %collective-permute-start.7 = (bf16[192,768]{1,0:T(8,128)(2,1)S(1)}, bf16[192,768]{1,0:T(8,128)(2,1)S(1)}, u32[]{:S(2)}, u32[]{:S(2)}) collective-permute-start(bf16[192,768]{1,0:T(8,128)(2,1)S(1)} %collective-permute-done.6), channel_id=1, source_target_pairs={{0,8},{4,12},{8,0},{12,4},{1,9},{5,13},{9,1},{13,5},{2,10},{6,14},... | collective-permute-start | bytes 884744 | tf_op jit(solution)/shard_map/ppermute | solution.py:27
  14.1 11.7 %collective-permute-start.14 = (bf16[192,192]{1,0:T(8,128)(2,1)S(1)}, bf16[192,192]{1,0:T(8,128)(2,1)S(1)}, u32[]{:S(2)}, u32[]{:S(2)}) collective-permute-start(bf16[192,192]{1,0:T(8,128)(2,1)S(1)} %collective-permute-done.13), channel_id=1, source_target_pairs={{0,1},{1,2},{2,3},{3,0},{4,5},{5,6},{6,7},{7,4},{8,9},{9,10},{10,1... | collective-permute-start | bytes 221192 | tf_op jit(solution)/shard_map/ppermute | solution.py:23
  15.2 16.5 %collective-permute-start.1 = (bf16[256,768]{1,0:T(8,128)(2,1)}, bf16[256,768]{1,0:T(8,128)(2,1)}, u32[]{:S(2)}, u32[]{:S(2)}) collective-permute-start(bf16[256,768]{1,0:T(8,128)(2,1)} %get-tuple-element.163.refs_4_), channel_id=1, source_target_pairs={{0,4},{4,0},{8,12},{12,8},{1,5},{5,1},{9,13},{13,9},{2,6},{6,2},{1... | collective-permute-start | bytes 1179656 | tf_op jit(solution)/shard_map/ppermute | solution.py:27
  25.6 10.7 %collective-permute-start.9 = (bf16[192,768]{1,0:T(8,128)(2,1)S(1)}, bf16[192,768]{1,0:T(8,128)(2,1)}, u32[]{:S(2)}, u32[]{:S(2)}) collective-permute-start(bf16[192,768]{1,0:T(8,128)(2,1)S(1)} %collective-permute-done.8), channel_id=1, source_target_pairs={{0,8},{4,12},{8,0},{12,4},{1,9},{5,13},{9,1},{13,5},{2,10},{6,14},... | collective-permute-start | bytes 884744 | tf_op jit(solution)/shard_map/ppermute | solution.py:27
  27.2 9.2 %collective-permute-start.10 = (bf16[192,768]{1,0:T(8,128)(2,1)S(1)}, bf16[192,768]{1,0:T(8,128)(2,1)}, u32[]{:S(2)}, u32[]{:S(2)}) collective-permute-start(bf16[192,768]{1,0:T(8,128)(2,1)S(1)} %collective-permute-done.8), channel_id=1, source_target_pairs={{0,1},{1,2},{2,3},{3,0},{4,5},{5,6},{6,7},{7,4},{8,9},{9,10},{10,1... | collective-permute-start | bytes 884744 | tf_op jit(solution)/shard_map/ppermute | solution.py:23
  30.4 11.0 %collective-permute-start.16 = (bf16[192,768]{1,0:T(8,128)(2,1)S(1)}, bf16[192,768]{1,0:T(8,128)(2,1)S(1)}, u32[]{:S(2)}, u32[]{:S(2)}) collective-permute-start(bf16[192,768]{1,0:T(8,128)(2,1)S(1)} %constant_dynamic-slice_fusion), channel_id=1, source_target_pairs={{0,8},{4,12},{8,0},{12,4},{1,9},{5,13},{9,1},{13,5},{2,10},{6,14},... | collective-permute-start | bytes 884744 | tf_op jit(solution)/shard_map/ppermute | solution.py:27
  36.4 9.4 %collective-permute-start.11 = (bf16[192,768]{1,0:T(8,128)(2,1)}, bf16[192,768]{1,0:T(8,128)(2,1)S(1)}, u32[]{:S(2)}, u32[]{:S(2)}) collective-permute-start(bf16[192,768]{1,0:T(8,128)(2,1)} %collective-permute-done.10), channel_id=1, source_target_pairs={{0,8},{4,12},{8,0},{12,4},{1,9},{5,13},{9,1},{13,5},{2,10},{6,14},... | collective-permute-start | bytes 884744 | tf_op jit(solution)/shard_map/ppermute | solution.py:27
  41.5 11.3 %collective-permute-start.17 = (bf16[384,768]{1,0:T(8,128)(2,1)S(1)}, bf16[384,768]{1,0:T(8,128)(2,1)S(1)}, u32[]{:S(2)}, u32[]{:S(2)}) collective-permute-start(bf16[384,768]{1,0:T(8,128)(2,1)S(1)} %pad_maximum_fusion.2.proj_a), channel_id=1, source_target_pairs={{0,4},{4,0},{8,12},{12,8},{1,5},{5,1},{9,13},{13,9},{2,6},{6,2},{1... | collective-permute-start | bytes 1769480 | tf_op jit(solution)/shard_map/ppermute | solution.py:27
  54.7 10.8 %collective-permute-start.20 = (bf16[256,768]{1,0:T(8,128)(2,1)S(1)}, bf16[256,768]{1,0:T(8,128)(2,1)}, u32[]{:S(2)}, u32[]{:S(2)}) collective-permute-start(bf16[256,768]{1,0:T(8,128)(2,1)S(1)} %copy-done.18), channel_id=1, source_target_pairs={{0,8},{4,12},{8,0},{12,4},{1,9},{5,13},{9,1},{13,5},{2,10},{6,14},... | collective-permute-start | bytes 1179656 | tf_op jit(solution)/shard_map/ppermute | solution.py:27
  57.0 10.0 %collective-permute-start.21 = (bf16[128,768]{1,0:T(8,128)(2,1)}, bf16[128,768]{1,0:T(8,128)(2,1)}, u32[]{:S(2)}, u32[]{:S(2)}) collective-permute-start(bf16[128,768]{1,0:T(8,128)(2,1)} %get-tuple-element.206), channel_id=1, source_target_pairs={{0,16},{16,0},{1,17},{17,1},{2,18},{18,2},{3,19},{19,3},{4,20},{20... | collective-permute-start | bytes 589832 | tf_op jit(solution)/shard_map/ppermute | solution.py:27
  58.0 43.1 %collective-permute-start.36 = (bf16[256,768]{1,0:T(8,128)(2,1)S(1)}, bf16[256,768]{1,0:T(8,128)(2,1)S(1)}, u32[]{:S(2)}, u32[]{:S(2)}) collective-permute-start(bf16[256,768]{1,0:T(8,128)(2,1)S(1)} %get-tuple-element.136.mine_ref), channel_id=1, source_target_pairs={{0,4},{4,0},{8,12},{12,8},{1,5},{5,1},{9,13},{13,9},{2,6},{6,2},{1... | collective-permute-start | bytes 1179656 | tf_op jit(solution)/shard_map/ppermute | solution.py:27
  67.0 8.6 %collective-permute-start.23 = (bf16[128,768]{1,0:T(8,128)(2,1)}, bf16[128,768]{1,0:T(8,128)(2,1)S(1)}, u32[]{:S(2)}, u32[]{:S(2)}) collective-permute-start(bf16[128,768]{1,0:T(8,128)(2,1)} %collective-permute-done.21), channel_id=1, source_target_pairs={{0,1},{1,2},{2,3},{3,0},{4,5},{5,6},{6,7},{7,4},{8,9},{9,10},{10,1... | collective-permute-start | bytes 589832 | tf_op jit(solution)/shard_map/ppermute | solution.py:23
  67.7 8.7 %collective-permute-start.29 = (bf16[128,768]{1,0:T(8,128)(2,1)}, bf16[128,768]{1,0:T(8,128)(2,1)S(1)}, u32[]{:S(2)}, u32[]{:S(2)}) collective-permute-start(bf16[128,768]{1,0:T(8,128)(2,1)} %collective-permute-done.21), channel_id=1, source_target_pairs={{0,8},{4,12},{8,0},{12,4},{1,9},{5,13},{9,1},{13,5},{2,10},{6,14},... | collective-permute-start | bytes 589832 | tf_op jit(solution)/shard_map/ppermute | solution.py:27
  72.2 10.1 %collective-permute-start.30 = (bf16[128,768]{1,0:T(8,128)(2,1)S(1)}, bf16[128,768]{1,0:T(8,128)(2,1)S(1)}, u32[]{:S(2)}, u32[]{:S(2)}) collective-permute-start(bf16[128,768]{1,0:T(8,128)(2,1)S(1)} %collective-permute-done.22), channel_id=1, source_target_pairs={{0,8},{4,12},{8,0},{12,4},{1,9},{5,13},{9,1},{13,5},{2,10},{6,14},... | collective-permute-start | bytes 589832 | tf_op jit(solution)/shard_map/ppermute | solution.py:27
  76.4 8.4 %collective-permute-start.31 = (bf16[128,768]{1,0:T(8,128)(2,1)S(1)}, bf16[128,768]{1,0:T(8,128)(2,1)S(1)}, u32[]{:S(2)}, u32[]{:S(2)}) collective-permute-start(bf16[128,768]{1,0:T(8,128)(2,1)S(1)} %collective-permute-done.23), channel_id=1, source_target_pairs={{0,8},{4,12},{8,0},{12,4},{1,9},{5,13},{9,1},{13,5},{2,10},{6,14},... | collective-permute-start | bytes 589832 | tf_op jit(solution)/shard_map/ppermute | solution.py:27
  82.3 11.5 %collective-permute-start.32 = (bf16[128,768]{1,0:T(8,128)(2,1)S(1)}, bf16[128,768]{1,0:T(8,128)(2,1)S(1)}, u32[]{:S(2)}, u32[]{:S(2)}) collective-permute-start(bf16[128,768]{1,0:T(8,128)(2,1)S(1)} %collective-permute-done.24), channel_id=1, source_target_pairs={{0,8},{4,12},{8,0},{12,4},{1,9},{5,13},{9,1},{13,5},{2,10},{6,14},... | collective-permute-start | bytes 589832 | tf_op jit(solution)/shard_map/ppermute | solution.py:27
  84.8 11.8 %collective-permute-start.33 = (bf16[128,768]{1,0:T(8,128)(2,1)S(1)}, bf16[128,768]{1,0:T(8,128)(2,1)S(1)}, u32[]{:S(2)}, u32[]{:S(2)}) collective-permute-start(bf16[128,768]{1,0:T(8,128)(2,1)S(1)} %collective-permute-done.25), channel_id=1, source_target_pairs={{0,8},{4,12},{8,0},{12,4},{1,9},{5,13},{9,1},{13,5},{2,10},{6,14},... | collective-permute-start | bytes 589832 | tf_op jit(solution)/shard_map/ppermute | solution.py:27
  86.1 10.5 %collective-permute-start.27 = (bf16[128,768]{1,0:T(8,128)(2,1)S(1)}, bf16[128,768]{1,0:T(8,128)(2,1)S(1)}, u32[]{:S(2)}, u32[]{:S(2)}) collective-permute-start(bf16[128,768]{1,0:T(8,128)(2,1)S(1)} %collective-permute-done.25), channel_id=1, source_target_pairs={{0,1},{1,2},{2,3},{3,0},{4,5},{5,6},{6,7},{7,4},{8,9},{9,10},{10,1... | collective-permute-start | bytes 589832 | tf_op jit(solution)/shard_map/ppermute | solution.py:23
  101.1 30.5 %collective-permute-start.38 = (bf16[256,768]{1,0:T(8,128)(2,1)S(1)}, bf16[256,768]{1,0:T(8,128)(2,1)S(1)}, u32[]{:S(2)}, u32[]{:S(2)}) collective-permute-start(bf16[256,768]{1,0:T(8,128)(2,1)S(1)} %copy-done.19), channel_id=1, source_target_pairs={{0,8},{4,12},{8,0},{12,4},{1,9},{5,13},{9,1},{13,5},{2,10},{6,14},... | collective-permute-start | bytes 1179656 | tf_op jit(solution)/shard_map/ppermute | solution.py:27
  101.4 30.3 %collective-permute-start.39 = (bf16[256,768]{1,0:T(8,128)(2,1)S(1)}, bf16[256,768]{1,0:T(8,128)(2,1)}, u32[]{:S(2)}, u32[]{:S(2)}) collective-permute-start(bf16[256,768]{1,0:T(8,128)(2,1)S(1)} %copy-done.21), channel_id=1, source_target_pairs={{0,8},{4,12},{8,0},{12,4},{1,9},{5,13},{9,1},{13,5},{2,10},{6,14},... | collective-permute-start | bytes 1179656 | tf_op jit(solution)/shard_map/ppermute | solution.py:27
  108.3 19.7 %all-to-all-start = ((f32[32,1,512]{2,1,0:T(1,128)}), f32[32,1,512]{2,1,0:T(1,128)}, u32[]{:S(2)}, u32[]{:S(2)}) async-start(f32[32,1,512]{2,1,0:T(1,128)} %get-tuple-element.145), calls=%async_computation | async-start | bytes 131072 | tf_op jit(solution)/shard_map/all_to_all | solution.py:320
  122.0 9.7 %collective-permute-start.41 = (bf16[256,768]{1,0:T(8,128)(2,1)}, bf16[256,768]{1,0:T(8,128)(2,1)}, u32[]{:S(2)}, u32[]{:S(2)}) collective-permute-start(bf16[256,768]{1,0:T(8,128)(2,1)} %collective-permute-done.18.refs_2_), channel_id=1, source_target_pairs={{0,4},{4,0},{8,12},{12,8},{1,5},{5,1},{9,13},{13,9},{2,6},{6,2},{1... | collective-permute-start | bytes 1179656 | tf_op jit(solution)/shard_map/ppermute | solution.py:27
  123.3 8.4 %collective-permute-start.37 = (bf16[512,192]{1,0:T(8,128)(2,1)}, bf16[512,192]{1,0:T(8,128)(2,1)S(1)}, u32[]{:S(2)}, u32[]{:S(2)}) collective-permute-start(bf16[512,192]{1,0:T(8,128)(2,1)} %get-tuple-element.205), channel_id=1, source_target_pairs={{0,8},{4,12},{8,0},{12,4},{1,9},{5,13},{9,1},{13,5},{2,10},{6,14},... | collective-permute-start | bytes 589832 | tf_op jit(solution)/shard_map/ppermute | solution.py:27
  141.5 10.4 %collective-permute-start.46 = (bf16[256,768]{1,0:T(8,128)(2,1)S(1)}, bf16[256,768]{1,0:T(8,128)(2,1)S(1)}, u32[]{:S(2)}, u32[]{:S(2)}) collective-permute-start(bf16[256,768]{1,0:T(8,128)(2,1)S(1)} %multiply_convert_fusion.2.refs_0_.embed_ref), channel_id=1, source_target_pairs={{0,8},{4,12},{8,0},{12,4},{1,9},{5,13},{9,1},{13,5},{2,10},{6,14},... | collective-permute-start | bytes 1179656 | tf_op jit(solution)/shard_map/ppermute | solution.py:27
  142.5 11.3 %collective-permute-start.45 = (bf16[256,768]{1,0:T(8,128)(2,1)S(1)}, bf16[256,768]{1,0:T(8,128)(2,1)S(1)}, u32[]{:S(2)}, u32[]{:S(2)}) collective-permute-start(bf16[256,768]{1,0:T(8,128)(2,1)S(1)} %multiply_convert_fusion.2.refs_0_.embed_ref), channel_id=1, source_target_pairs={{0,4},{4,0},{8,12},{12,8},{1,5},{5,1},{9,13},{13,9},{2,6},{6,2},{1... | collective-permute-start | bytes 1179656 | tf_op jit(solution)/shard_map/ppermute | solution.py:27
  164.0 13.8 %collective-permute-start.50 = (bf16[384,768]{1,0:T(8,128)(2,1)S(1)}, bf16[384,768]{1,0:T(8,128)(2,1)}, u32[]{:S(2)}, u32[]{:S(2)}) collective-permute-start(bf16[384,768]{1,0:T(8,128)(2,1)S(1)} %copy-done.10), channel_id=1, source_target_pairs={{0,4},{4,0},{8,12},{12,8},{1,5},{5,1},{9,13},{13,9},{2,6},{6,2},{1... | collective-permute-start | bytes 1769480 | tf_op jit(solution)/shard_map/ppermute | solution.py:27
  164.3 13.5 %collective-permute-start.51 = (bf16[384,768]{1,0:T(8,128)(2,1)S(1)}, bf16[384,768]{1,0:T(8,128)(2,1)}, u32[]{:S(2)}, u32[]{:S(2)}) collective-permute-start(bf16[384,768]{1,0:T(8,128)(2,1)S(1)} %copy-done.14), channel_id=1, source_target_pairs={{0,4},{4,0},{8,12},{12,8},{1,5},{5,1},{9,13},{13,9},{2,6},{6,2},{1... | collective-permute-start | bytes 1769480 | tf_op jit(solution)/shard_map/ppermute | solution.py:27
  167.3 17.3 %collective-permute-start.54 = (bf16[192,960]{1,0:T(8,128)(2,1)}, bf16[192,960]{1,0:T(8,128)(2,1)}, u32[]{:S(2)}, u32[]{:S(2)}) collective-permute-start(bf16[192,960]{1,0:T(8,128)(2,1)} %get-tuple-element.177), channel_id=1, source_target_pairs={{0,1},{1,2},{2,3},{3,0},{4,5},{5,6},{6,7},{7,4},{8,9},{9,10},{10,1... | collective-permute-start | bytes 1105928 | tf_op jit(solution)/shard_map/ppermute | solution.py:23
  168.4 33.9 %collective-permute-start.53 = (bf16[192,960]{1,0:T(8,128)(2,1)}, bf16[192,960]{1,0:T(8,128)(2,1)S(1)}, u32[]{:S(2)}, u32[]{:S(2)}) collective-permute-start(bf16[192,960]{1,0:T(8,128)(2,1)} %get-tuple-element.176), channel_id=1, source_target_pairs={{0,2},{1,3},{2,0},{3,1},{4,6},{5,7},{6,4},{7,5},{8,10},{9,11},{10,... | collective-permute-start | bytes 1105928 | tf_op jit(solution)/shard_map/ppermute | solution.py:23
  169.8 35.1 %collective-permute-start.52 = (bf16[192,960]{1,0:T(8,128)(2,1)}, bf16[192,960]{1,0:T(8,128)(2,1)S(1)}, u32[]{:S(2)}, u32[]{:S(2)}) collective-permute-start(bf16[192,960]{1,0:T(8,128)(2,1)} %get-tuple-element.175), channel_id=1, source_target_pairs={{0,3},{1,0},{2,1},{3,2},{4,7},{5,4},{6,5},{7,6},{8,11},{9,8},{10,9... | collective-permute-start | bytes 1105928 | tf_op jit(solution)/shard_map/ppermute | solution.py:23
  (68 other events, 729.3 us)

commit v3 on v2

--- a/solution.py
+++ b/solution.py
@@ -1,3 +1,5 @@
+import math
+
 import jax
 import jax.numpy as jnp
 from jax import lax
@@ -33,6 +35,21 @@
         part = after(blocks[-1], *earlier) if step == 2 and earlier else blocks[-1]
         blocks.append(shift(part, "gcol", 1))
     return blocks
+
+
+def shift_across(value):
+    towers, count = lax.axis_size("tower"), lax.axis_size("gcol")
+    pairs = [
+        (t * count + c, (towers - 1 - t) * count + (c + 1) % count)
+        for t in range(towers)
+        for c in range(count)
+    ]
+    return lax.ppermute(value, ("tower", "gcol"), pairs)
+
+
+def swap_across(value):
+    towers = lax.axis_size("tower")
+    return lax.ppermute(value, "tower", [(t, towers - 1 - t) for t in range(towers)])
 
 
 def grow_bits(last):
@@ -85,12 +102,14 @@
     specs = [smem] * scalars + [vmem] * (len(operands) - scalars)
     for place, spec in (in_specs or {}).items():
         specs[place] = spec
+    held = sum(math.prod(shape) * jnp.dtype(dtype).itemsize for shape, dtype in outs)
+    held += sum(value.size * value.dtype.itemsize for value in operands)
     return pl.pallas_call(
         kernel,
         out_shape=[jax.ShapeDtypeStruct(shape, dtype) for shape, dtype in outs],
         in_specs=specs,
         out_specs=[vmem] * len(outs),
-        compiler_params=pltpu.CompilerParams(vmem_limit_bytes=56 * 1024 * 1024),
+        compiler_params=pltpu.CompilerParams(vmem_limit_bytes=min(held + 12 * 2**20, 56 * 2**20)),
         cost_estimate=pl.CostEstimate(flops=1, bytes_accessed=1, transcendentals=0),
         name=name,
     )(*operands)
@@ -216,14 +235,14 @@
     return call(kernel, [((depth, right[0].shape[1]), F32)], left, *right, name="down_own")[0]
 
 
-def own_gradients(places, found, preact, d_embed, d_stream, proj_mine, proj_rest, down_mine, down_rest):
+def own_gradients(places, found, preact, d_embed, proj_mine, proj_rest, down_mine, down_rest):
     rows, inner = preact.shape
-    blocks, features = len(d_stream), d_stream[0].shape[1]
+    blocks = found.shape[0]
     count, block = len(down_mine), down_mine[0].shape[1]
     depth, half = proj_mine.shape[0], blocks // 2
+    features = depth // half
 
     def kernel(places_ref, found_ref, preact_ref, embed_ref, proj_a, proj_b, *refs):
-        stream, refs = refs[:blocks], refs[blocks:]
         down_a, down_b, (d_hidden, d_pre) = refs[:count], refs[count : 2 * count], refs[2 * count :]
         for i in range(blocks):
             place = found_ref[i]
@@ -232,16 +251,17 @@
             rows_a, rows_b = proj_a[pl.ds(start, features)], proj_b[pl.ds(start, features)]
             part = dot_nt(embed_ref[...], jnp.where(near, rows_a, rows_b)).astype(BF16)
             d_hidden[:, i * features : (i + 1) * features] = part
-        left = jnp.concatenate([r[...] for r in stream], 1)
+        left_a = dot_nt(embed_ref[...], proj_a[...]).astype(BF16)
+        left_b = dot_nt(embed_ref[...], proj_b[...]).astype(BF16)
         for k in range(count):
             start = pl.multiple_of(places_ref[k] * block, 128)
-            d_active = dot_nn(left[:, :depth], down_a[k][...]) + dot_nn(left[:, depth:], down_b[k][...])
+            d_active = dot_nn(left_a, down_a[k][...]) + dot_nn(left_b, down_b[k][...])
             slope = gelu_slope(preact_ref[:, pl.ds(start, block)].astype(F32))
             d_pre[:, pl.ds(start, block)] = (d_active * slope).astype(BF16)
 
     return call(
         kernel, [((rows, blocks * features), BF16), (preact.shape, BF16)], places, found, preact, d_embed,
-        proj_mine, proj_rest, *d_stream, *down_mine, *down_rest, name="own_gradients", scalars=2,
+        proj_mine, proj_rest, *down_mine, *down_rest, name="own_gradients", scalars=2,
     )
 
 
@@ -270,7 +290,7 @@
         pace = () if k == 1 else (down_ring[k - 1],)
         proj_ring.append(shift(after(proj_ring[-1], *pace), "gcol", 1))
     down_tables = [spread(part, far[0]) for part in down_ring]
-    active_even = {0: spread(active[0], None)}
+    active_even = {1: spread(active[1])}
     proj_own = jnp.roll(jnp.concatenate(proj_ring[::-1], 1), (gcol + 1) * columns, 1)
     proj_even = spread(proj_own)
     proj_pair = jnp.concatenate([proj_even[j] for j in evens], 0)
@@ -292,7 +312,7 @@
     own_rows = hidden.shape[0]
     stream_rest = swap(stream[own_rows:], "grow", 1)
     stream_b = jnp.concatenate([stream[:own_rows], stream_rest], 1)
-    embed = after(dot_nn(stream_b, proj_all), active_even[0][last])
+    embed = after(dot_nn(stream_b, proj_all), active_even[1][last])
     inverse = lax.rsqrt(jnp.sum(embed * embed, axis=1, keepdims=True) + 1e-06)
     unit = embed * inverse
     unit_b = unit.astype(BF16)
@@ -303,31 +323,40 @@
         (unit, unit_b, inverse, stream, proj_pair, proj_mate, proj_all, down_pair, active, active_mate, preact, active_even)
     )
     far, core = (Lane(), Lane()), Lane()
-    active_even[1] = spread(active[1])
-
-    unit_mate = swap(unit_b, "grow", 1)
-    rings = [
-        ring(after(swap(part, "tower", 1), active_even[1][last]))
-        for part in jnp.split(unit_b, 2, 0)
-    ]
-    pieces = {(k, q): spread(rings[q][k], far[q]) for k in ks for q in chunks}
-    others = jnp.concatenate([pieces[k, q][j] for j, k in order for q in chunks], 0)
-    device_count = tower_count * grow_count * gcol_count
-    others, unit_mate, unit_b, active_even, stream, active, log_scale = lax.optimization_barrier(
-        (others, unit_mate, unit_b, active_even, stream, active, log_scale)
-    )
-    scores_own, scores_mate, lse = score_rows(log_scale, unit_b, unit_mate, others, device_count)
-    lse_all = lax.all_to_all(lse, ("tower", "grow", "gcol"), 0, 0)
-
-    far = (Lane(), Lane())
-    for k in ks[2:]:
-        active_even[k] = spread(active[k])
+
     stream_blocks = [stream[:, i * features : (i + 1) * features] for i in range(len(evens))]
     stream_even = {0: stream_blocks[0]}
     for i, j in enumerate(evens[1:], 1):
         stream_even[j] = swap(stream_blocks[i], "grow", j)
+    across = swap_across(unit_b)
+    near = {j: swap_across(part) for j, part in spread(unit_b).items() if j}
+    near[0] = across
+    rings = []
+    for part in jnp.split(unit_b, 2, 0):
+        blocks = [None, shift_across(part)]
+        for k in ks[2:]:
+            pace = (across, stream_even[last]) if k == 3 else ()
+            blocks.append(shift(after(blocks[-1], *pace), "gcol", 1))
+        rings.append(blocks)
+    unit_mate = swap(after(unit_b, rings[0][-1]), "grow", 1)
+    pieces = [near] + [
+        spread(jnp.concatenate([rings[q][k] for q in chunks], 0)) for k in ks[1:-1]
+    ]
+    lasts = [spread(after(rings[q][-1], pieces[1][last], near[last])) for q in chunks]
+    pieces.append({j: jnp.concatenate([part[j] for part in lasts], 0) for j in evens})
+    others = jnp.concatenate([pieces[k][j] for j, k in order], 0)
+    device_count = tower_count * grow_count * gcol_count
+    others, unit_mate, unit_b, active_even, stream_even, active, log_scale = lax.optimization_barrier(
+        (others, unit_mate, unit_b, active_even, stream_even, active, log_scale)
+    )
+    scores_own, scores_mate, lse = score_rows(log_scale, unit_b, unit_mate, others, device_count)
+    lse_all = lax.all_to_all(lse, ("tower", "grow", "gcol"), 0, 0)
+
+    far = (Lane(), Lane())
+    for k in ks[2:]:
+        active_even[k] = spread(active[k])
     core = Lane()
-    active_odd = {k: {j: core(active_even[k][j], 1, others) for j in evens[1:]} for k in ks}
+    active_odd = {k: {j: core(active_even[k][j], 1, others) for j in evens[1:]} for k in ks[1:]}
 
     def device(tower_of, j, k):
         return (tower_of * grow_count + (grow ^ j)) * gcol_count + sources[k]
@@ -345,7 +374,8 @@
     row_index = lax.broadcasted_iota(jnp.int32, scores_own.shape, 0)
     column_index = lax.broadcasted_iota(jnp.int32, scores_own.shape, 1)
     diagonal = (row_index == column_index).astype(F32)
-    arrived = [stream_even[last]] + [active_even[k][last] for k in ks[2:]]
+    arrived = [active_even[k][last] for k in ks[2:]]
+    scores_mate, scores_own, row_lse = lax.optimization_barrier((scores_mate, scores_own, row_lse))
     for_mate = embed_gradient(after(scores_mate, *arrived), row_lse[own_rows:], 0.0)
     for_own = embed_gradient(after(scores_own, for_mate), row_lse[:own_rows], diagonal)
     d_unit = for_own + swap(for_mate, "grow", 1)
@@ -354,31 +384,30 @@
     for_barrier = (d_embed, active_even, active_odd, stream_even, down_pair, proj_all, for_mate)
     for_barrier = lax.optimization_barrier(for_barrier)
     d_embed, active_even, active_odd, stream_even, down_pair, proj_all, for_mate = for_barrier
-    rel = [*evens, *(j + 1 for j in evens)]
-    d_stream = [
-        dot_nt(d_embed, proj_all[i * features : (i + 1) * features]).astype(BF16) for i in js
-    ]
-    rights = []
-    for k in ks:
+
+    def right(k, even, odd):
         parts = {0: active[k], 1: active_mate[k]}
         for j in evens[1:]:
-            parts[j], parts[j + 1] = active_even[k][j], active_odd[k][j]
-        rights.append([parts[j] for j in js])
+            parts[j], parts[j + 1] = even[j], odd[j]
+        return [parts[j] for j in js]
+
+    rights = {k: right(k, active_even[k], active_odd[k]) for k in ks[1:]}
     embed_rows = {}
     for j, part in spread(d_embed).items():
         embed_rows[j], embed_rows[j + 1] = part, swap(part, "grow", 1)
+    down_mate = [swap(part, "grow", 1) for part in down_pair]
     away = [*ks[1:]]
     terms, grad_proj, left = all_terms(
-        places, proj_pair[:features], [rights[k] for k in away], [stream_even[j] for j in evens],
+        places, after(proj_pair[:features], *down_mate), [rights[k] for k in away], [stream_even[j] for j in evens],
         [embed_rows[j] for j in js], columns,
     )
     sent = [shift(term, "gcol", -k) for k, term in zip(away, terms)]
-    rights[0][0] = after(rights[0][0], *terms)
-    grad_down = weight_terms(left, rights[0])
-
-    down_mate = [swap(after(part, *terms), "grow", 1) for part in down_pair]
+    even = spread(after(active[0], *terms))
+    odd = {j: swap(even[j], "grow", 1) for j in evens[1:]}
+    grad_down = weight_terms(left, right(0, even, odd))
+
     d_hidden, d_pre = own_gradients(
-        places, found, preact, after(d_embed, *terms), d_stream, proj_pair, proj_mate, down_pair, down_mate
+        places, found, preact, after(d_embed, *terms), proj_pair, proj_mate, down_pair, down_mate
     )
     grad_down, grad_proj = after(grad_down, d_pre, d_hidden), after(grad_proj, d_pre, d_hidden)
     for part in sent:

time: 209 us -> 193 us (0.923)
  Pallas kernels: 26.3 us -> 14 us
  waiting for transfers between devices: 75.9 us -> 82.9 us
  matrix products: 15.5 us -> 9.66 us
  starting transfers between devices: 66 us -> 61.2 us
  other arithmetic: 7.66 us -> 4.93 us
    ppermute x15 -> x13, waiting for transfers between devices: 38.2 us -> 24.3 us  [shift(): lax.ppermute(value, axis, [(i, (i + step) % count) for i in range(count)])]
    pallas_call x6, Pallas kernels: 26.3 us -> 14 us  [call(): pl.pallas_call(kernel, out_shape=[jax.ShapeDtypeStruct(shape, dtype) for...]
    ppermute x0 -> x4, waiting for transfers between devices: none -> 10.9 us  [the longest x2 5.69 us: shift_across(): return lax.ppermute(value, ('tower', 'gcol'), pairs)]
    ppermute x40 -> x35, waiting for transfers between devices: 34.9 us -> 42.2 us  [swap(): lax.ppermute(value, axis, [(i, i ^ bit) for i in range(lax.axis_size(axis...]
    all_to_all x1, starting transfers between devices: 13.7 us -> 7.24 us  [body(): lse_all = lax.all_to_all(lse, ('tower', 'grow', 'gcol'), 0, 0)]
    dot_general x8 -> x4, matrix products: 9.56 us -> 4.61 us  [dot_nt(): lax.dot_general(left, right, (((1,), (1,)), ((), ())), preferred_element_...]
    ppermute x0 -> x4, starting transfers between devices: none -> 4.78 us  [the longest x2 2.48 us: swap_across(): lax.ppermute(value, 'tower', [(t, towers - 1 - t) for t in range(towers)])]
    ppermute x15 -> x13, starting transfers between devices: 16.5 us -> 12.4 us  [shift(): lax.ppermute(value, axis, [(i, (i + step) % count) for i in range(count)])]
  transfers between devices with their start and end apart: 56 -> 53, of which waited for: 25 -> 20; matrix products, arithmetic and copies ran while one was open for 15% -> 12% of each run, Pallas kernels for 9% -> 5%
where the time goes in v3:
time: 193 us; the launch traced here: 191 us
  waiting for transfers between devices  82.9 us (43%)
  starting transfers between devices  61.2 us (32%)
  local copies, waits for them, and re-layouts  16.4 us (8%)
  Pallas kernels  14 us (7%)
  matrix products  9.66 us (5%)
  other arithmetic  4.93 us (3%)
  between operations  2.23 us (1%)
    ppermute x35, waiting for transfers between devices, swap(): lax.ppermute(value, axis, [(i, i ^ bit) for i in range(lax.axis_size(axis...  42.2 us
    ppermute x35, starting transfers between devices, swap(): lax.ppermute(value, axis, [(i, i ^ bit) for i in range(lax.axis_size(axis...  36.8 us
    ppermute x13, waiting for transfers between devices, shift(): lax.ppermute(value, axis, [(i, (i + step) % count) for i in range(count)])  24.3 us
    pallas_call x6, Pallas kernels, call(): pl.pallas_call(kernel, out_shape=[jax.ShapeDtypeStruct(shape, dtype) for...  14 us
    ppermute x13, starting transfers between devices, shift(): lax.ppermute(value, axis, [(i, (i + step) % count) for i in range(count)])  12.4 us
    unnamed x104, local copies, waits for them, and re-layouts  8.84 us
    all_to_all x1, starting transfers between devices, body(): lse_all = lax.all_to_all(lse, ('tower', 'grow', 'gcol'), 0, 0)  7.24 us
    ppermute x2, waiting for transfers between devices, shift_across(): return lax.ppermute(value, ('tower', 'gcol'), pairs)  5.69 us
  transfers between devices with their start and end apart: 53, of which 20 were waited for; matrix products, arithmetic and copies ran while one was open for 12% of the time, Pallas kernels for 5%

profile of v3, /device:TPU:9, one launch (start us, length us, event | category | flops | bytes accessed | tf_op | source)
XLA Modules:
  0.0 191.3 jit_solution(10506829234877296883)
XLA Ops:
  3.3 1.4 copy-done
  4.7 1.6 activate.1
  12.3 2.1 %dynamic-slice_bitcast_fusion.3 = (bf16[256,192]{1,0:T(8,128)(2,1)}, bf16[256,192]{1,0:T(8,128)(2,1)}, bf16[256,192]{1,0:T(8,128)(2,1)S(1)}, bf16[256,192]{1,0:T(8,128)(2,1)S(1)}) fusion(bf16[1,256,768]{2,1,0:T(8,128)(2,1)} %param.5, s32[]{:T(128)S(6)} %select_n.25, s32[]{:T(128)S(6)} %select_n.26, s32[]{:T(128)S(6)} %select_n.28, s32[]{:T(128)S(6)} %select_n.27), kind=kLoop, calls=%fused_computation.52 | loop fusion | bytes 786448 | tf_op jit(solution)/shard_map/dynamic_slice | solution.py:302
  15.6 3.6 %collective-permute-start.1 = (bf16[256,768]{1,0:T(8,128)(2,1)S(1)}, bf16[256,768]{1,0:T(8,128)(2,1)S(1)}, u32[]{:S(2)}, u32[]{:S(2)}) collective-permute-start(bf16[256,768]{1,0:T(8,128)(2,1)S(1)} %get-tuple-element.158.refs_4_), channel_id=1, source_target_pairs={{0,4},{4,0},{8,12},{12,8},{1,5},{5,1},{9,13},{13,9},{2,6},{6,2},{1... | collective-permute-start | bytes 1179656 | tf_op jit(solution)/shard_map/ppermute | solution.py:29
  19.2 6.3 %collective-permute-done.7 = bf16[192,768]{1,0:T(8,128)(2,1)S(1)} collective-permute-done((bf16[192,768]{1,0:T(8,128)(2,1)S(1)}, bf16[192,768]{1,0:T(8,128)(2,1)S(1)}, u32[]{:S(2)}, u32[]{:S(2)}) %collective-permute-start.7) | collective-permute-done | bytes 294944 | tf_op jit(solution)/shard_map/ppermute | solution.py:29
  32.8 4.0 %collective-permute-start.2 = (bf16[256,768]{1,0:T(8,128)(2,1)}, bf16[256,768]{1,0:T(8,128)(2,1)S(1)}, u32[]{:S(2)}, u32[]{:S(2)}) collective-permute-start(bf16[256,768]{1,0:T(8,128)(2,1)} %get-tuple-element.134.refs_8_), channel_id=1, source_target_pairs={{0,4},{4,0},{8,12},{12,8},{1,5},{5,1},{9,13},{13,9},{2,6},{6,2},{1... | collective-permute-start | bytes 1179656 | tf_op jit(solution)/shard_map/ppermute | solution.py:29
  41.1 3.5 %collective-permute-start.17 = (bf16[384,768]{1,0:T(8,128)(2,1)S(1)}, bf16[384,768]{1,0:T(8,128)(2,1)S(1)}, u32[]{:S(2)}, u32[]{:S(2)}) collective-permute-start(bf16[384,768]{1,0:T(8,128)(2,1)S(1)} %pad_maximum_fusion.2.proj_a), channel_id=1, source_target_pairs={{0,4},{4,0},{8,12},{12,8},{1,5},{5,1},{9,13},{13,9},{2,6},{6,2},{1... | collective-permute-start | bytes 1769480 | tf_op jit(solution)/shard_map/ppermute | solution.py:29
  44.6 2.1 %collective-permute-done.11 = bf16[192,768]{1,0:T(8,128)(2,1)S(1)} collective-permute-done((bf16[192,768]{1,0:T(8,128)(2,1)}, bf16[192,768]{1,0:T(8,128)(2,1)S(1)}, u32[]{:S(2)}, u32[]{:S(2)}) %collective-permute-start.11) | collective-permute-done | bytes 294944 | tf_op jit(solution)/shard_map/ppermute | solution.py:29
  46.8 1.8 fusion.16
  48.7 2.3 %collective-permute-start.4 = (bf16[256,384]{1,0:T(8,128)(2,1)S(1)}, bf16[256,384]{1,0:T(8,128)(2,1)S(1)}, u32[]{:S(2)}, u32[]{:S(2)}) collective-permute-start(bf16[256,384]{1,0:T(8,128)(2,1)S(1)} %copy-done.42), channel_id=1, source_target_pairs={{0,4},{4,0},{8,12},{12,8},{1,5},{5,1},{9,13},{13,9},{2,6},{6,2},{1... | collective-permute-start | bytes 589832 | tf_op jit(solution)/shard_map/ppermute | solution.py:29
  51.0 1.6 fusion.20
  62.6 2.4 %collective-permute-done.20 = bf16[128,768]{1,0:T(8,128)(2,1)S(1)} collective-permute-done((bf16[128,768]{1,0:T(8,128)(2,1)S(1)}, bf16[128,768]{1,0:T(8,128)(2,1)S(1)}, u32[]{:S(2)}, u32[]{:S(2)}) %collective-permute-start.20) | collective-permute-done | bytes 196640 | tf_op jit(solution)/shard_map/ppermute | solution.py:47
  66.0 3.3 %collective-permute-done.21 = bf16[128,768]{1,0:T(8,128)(2,1)S(1)} collective-permute-done((bf16[128,768]{1,0:T(8,128)(2,1)S(1)}, bf16[128,768]{1,0:T(8,128)(2,1)S(1)}, u32[]{:S(2)}, u32[]{:S(2)}) %collective-permute-start.21) | collective-permute-done | bytes 196640 | tf_op jit(solution)/shard_map/ppermute | solution.py:47
  70.2 5.2 %collective-permute-done.19 = bf16[256,768]{1,0:T(8,128)(2,1)S(1)} collective-permute-done((bf16[256,768]{1,0:T(8,128)(2,1)S(1)}, bf16[256,768]{1,0:T(8,128)(2,1)S(1)}, u32[]{:S(2)}, u32[]{:S(2)}) %collective-permute-start.19) | collective-permute-done | bytes 393248 | tf_op jit(solution)/shard_map/ppermute | solution.py:52
  80.0 2.8 %collective-permute-done.25 = bf16[128,768]{1,0:T(8,128)(2,1)S(1)} collective-permute-done((bf16[128,768]{1,0:T(8,128)(2,1)S(1)}, bf16[128,768]{1,0:T(8,128)(2,1)S(1)}, u32[]{:S(2)}, u32[]{:S(2)}) %collective-permute-start.25) | collective-permute-done | bytes 196640 | tf_op jit(solution)/shard_map/ppermute | solution.py:25
  82.8 4.2 %collective-permute-start.33 = (bf16[256,768]{1,0:T(8,128)(2,1)S(1)}, bf16[256,768]{1,0:T(8,128)(2,1)S(1)}, u32[]{:S(2)}, u32[]{:S(2)}) collective-permute-start(bf16[256,768]{1,0:T(8,128)(2,1)S(1)} %get-tuple-element.125.mine_ref), channel_id=1, source_target_pairs={{0,4},{4,0},{8,12},{12,8},{1,5},{5,1},{9,13},{13,9},{2,6},{6,2},{1... | collective-permute-start | bytes 1179656 | tf_op jit(solution)/shard_map/ppermute | solution.py:29
  88.7 4.6 %collective-permute-done.30 = bf16[256,768]{1,0:T(8,128)(2,1)S(1)} collective-permute-done((bf16[256,768]{1,0:T(8,128)(2,1)S(1)}, bf16[256,768]{1,0:T(8,128)(2,1)S(1)}, u32[]{:S(2)}, u32[]{:S(2)}) %collective-permute-start.30) | collective-permute-done | bytes 393248 | tf_op jit(solution)/shard_map/ppermute | solution.py:29
  93.4 4.2 %collective-permute-done.31 = bf16[128,768]{1,0:T(8,128)(2,1)S(1)} collective-permute-done((bf16[128,768]{1,0:T(8,128)(2,1)S(1)}, bf16[128,768]{1,0:T(8,128)(2,1)S(1)}, u32[]{:S(2)}, u32[]{:S(2)}) %collective-permute-start.31) | collective-permute-done | bytes 196640 | tf_op jit(solution)/shard_map/ppermute | solution.py:29
  97.6 4.2 %collective-permute-done.32 = bf16[128,768]{1,0:T(8,128)(2,1)S(1)} collective-permute-done((bf16[128,768]{1,0:T(8,128)(2,1)S(1)}, bf16[128,768]{1,0:T(8,128)(2,1)S(1)}, u32[]{:S(2)}, u32[]{:S(2)}) %collective-permute-start.32) | collective-permute-done | bytes 196640 | tf_op jit(solution)/shard_map/ppermute | solution.py:29
  105.7 2.5 %scores.1 = (f32[256,2048]{1,0:T(8,128)S(1)}, f32[256,2048]{1,0:T(8,128)S(1)}, f32[32,1,512]{2,1,0:T(1,128)S(1)}) custom-call(f32[1,1]{1,0:T(1,128)} %bitcast.17.scale_ref, bf16[256,768]{1,0:T(8,128)(2,1)S(1)} %get-tuple-element.125.mine_ref, bf16[256,768]{1,0:T(8,128)(2,1)S(1)} %copy-done.29, ...), custom_call_target="tpu_custom_call" | custom-call | flops 1 | bytes 1 | tf_op jit(solution)/shard_map/scores/pallas_call | solution.py:107
  111.4 7.2 %all-to-all-start = ((f32[32,1,512]{2,1,0:T(1,128)}), f32[32,1,512]{2,1,0:T(1,128)}, u32[]{:S(2)}, u32[]{:S(2)}) async-start(f32[32,1,512]{2,1,0:T(1,128)} %copy-done.32), calls=%async_computation | async-start | bytes 131072 | tf_op jit(solution)/shard_map/all_to_all | solution.py:353
  119.3 5.5 %all-to-all-done.lse_ref = f32[32,1,512]{2,1,0:T(1,128)} async-done(((f32[32,1,512]{2,1,0:T(1,128)}), f32[32,1,512]{2,1,0:T(1,128)}, u32[]{:S(2)}, u32[]{:S(2)}) %all-to-all-start) | async-done | bytes 65568 | tf_op jit(solution)/shard_map/all_to_all | solution.py:353
  125.9 3.1 %convolution_multiply_fusion.1 = f32[256,768]{1,0:T(8,128)S(1)} fusion(bf16[2048,768]{1,0:T(8,128)(2,1)S(1)} %constant_dynamic-update-slice_fusion.6.others_ref, f32[256,2048]{1,0:T(8,128)} %copy-done.35, f32[2048]{0:T(1024)S(1)} %bitcast.54, f32[256]{0:T(256)S(1)} %get-tuple-element.185, f32[]{:T(128)} %exp.16), kind=kOutput, calls=%fused_computation.4 | convolution fusion | flops 808124416 | bytes 6038532 | tf_op jit(solution)/shard_map/dot_general | solution.py:97
  129.6 2.6 %collective-permute-done.38.refs_11_ = bf16[256,768]{1,0:T(8,128)(2,1)S(1)} collective-permute-done((bf16[256,768]{1,0:T(8,128)(2,1)}, bf16[256,768]{1,0:T(8,128)(2,1)S(1)}, u32[]{:S(2)}, u32[]{:S(2)}) %collective-permute-start.38) | collective-permute-done | bytes 393248 | tf_op jit(solution)/shard_map/ppermute | solution.py:29
  132.6 1.5 multiply_reduce_fusion
  136.1 8.8 %collective-permute-done.45.refs_2_ = bf16[256,768]{1,0:T(8,128)(2,1)S(1)} collective-permute-done((bf16[256,768]{1,0:T(8,128)(2,1)S(1)}, bf16[256,768]{1,0:T(8,128)(2,1)S(1)}, u32[]{:S(2)}, u32[]{:S(2)}) %collective-permute-start.45) | collective-permute-done | bytes 393248 | tf_op jit(solution)/shard_map/ppermute | solution.py:29
  148.1 3.9 %terms.1 = (bf16[192,960]{1,0:T(8,128)(2,1)S(1)}, bf16[192,960]{1,0:T(8,128)(2,1)S(1)}, bf16[192,960]{1,0:T(8,128)(2,1)S(1)}, f32[192,192]{1,0:T(8,128)S(1)}, bf16[192,1024]{1,0:T(8,128)(2,1)S(1)}) custom-call(s32[4]{0:T(128)S(1)} %get-tuple-element.94.places_ref, bf16[192,768]{1,0:T(8,128)(2,1)S(1)} %slice.45.proj_ref, ...), custom_call_target="tpu_custom_call" | custom-call | flops 1 | bytes 1 | tf_op jit(solution)/shard_map/terms/pallas_call | solution.py:107
  152.9 3.1 %collective-permute-start.50 = (bf16[192,960]{1,0:T(8,128)(2,1)S(1)}, bf16[192,960]{1,0:T(8,128)(2,1)S(1)}, u32[]{:S(2)}, u32[]{:S(2)}) collective-permute-start(bf16[192,960]{1,0:T(8,128)(2,1)S(1)} %get-tuple-element.171), channel_id=1, source_target_pairs={{0,2},{1,3},{2,0},{3,1},{4,6},{5,7},{6,4},{7,5},{8,10},{9,11},{10,... | collective-permute-start | bytes 1105928 | tf_op jit(solution)/shard_map/ppermute | solution.py:25
  156.0 6.4 %collective-permute-done.47.refs_2_ = bf16[256,768]{1,0:T(8,128)(2,1)S(1)} collective-permute-done((bf16[256,768]{1,0:T(8,128)(2,1)S(1)}, bf16[256,768]{1,0:T(8,128)(2,1)S(1)}, u32[]{:S(2)}, u32[]{:S(2)}) %collective-permute-start.47) | collective-permute-done | bytes 393248 | tf_op jit(solution)/shard_map/ppermute | solution.py:29
  163.6 4.6 %own_gradients.1 = (bf16[256,768]{1,0:T(8,128)(2,1)}, bf16[256,3072]{1,0:T(8,128)(2,1)}) custom-call(s32[4]{0:T(128)S(1)} %get-tuple-element.94.places_ref, s32[4]{0:T(128)S(1)} %get-tuple-element.95.found_ref, bf16[256,3072]{1,0:T(8,128)(2,1)S(1)} %bitcast.53, bf16[256,768]{1,0:T(8,128)(2,1)S(1)} %multiply_convert_fusion.2.refs_0_.embed_ref, ...), custom_call_target="tpu_custom_call" | custom-call | flops 1 | bytes 1 | tf_op jit(solution)/shard_map/own_gradients/pallas_call | solution.py:107
  168.2 17.8 %collective-permute-done.50 = bf16[192,960]{1,0:T(8,128)(2,1)S(1)} collective-permute-done((bf16[192,960]{1,0:T(8,128)(2,1)S(1)}, bf16[192,960]{1,0:T(8,128)(2,1)S(1)}, u32[]{:S(2)}, u32[]{:S(2)}) %collective-permute-start.50) | collective-permute-done | bytes 368672 | tf_op jit(solution)/shard_map/ppermute | solution.py:25
  186.0 3.1 %collective-permute-done.49 = bf16[192,960]{1,0:T(8,128)(2,1)S(1)} collective-permute-done((bf16[192,960]{1,0:T(8,128)(2,1)S(1)}, bf16[192,960]{1,0:T(8,128)(2,1)S(1)}, u32[]{:S(2)}, u32[]{:S(2)}) %collective-permute-start.49) | collective-permute-done | bytes 368672 | tf_op jit(solution)/shard_map/ppermute | solution.py:25
  (216 shorter events, 57.8 us)
Async XLA Ops:
  8.9 46.5 %collective-permute-start.18 = (bf16[256,768]{1,0:T(8,128)(2,1)S(1)}, bf16[256,768]{1,0:T(8,128)(2,1)S(1)}, u32[]{:S(2)}, u32[]{:S(2)}) collective-permute-start(bf16[256,768]{1,0:T(8,128)(2,1)S(1)} %get-tuple-element.158.refs_4_), channel_id=1, source_target_pairs={{0,8},{4,12},{8,0},{12,4},{1,9},{5,13},{9,1},{13,5},{2,10},{6,14},... | collective-permute-start | bytes 1179656 | tf_op jit(solution)/shard_map/ppermute | solution.py:29
  9.8 15.8 %collective-permute-start.7 = (bf16[192,768]{1,0:T(8,128)(2,1)S(1)}, bf16[192,768]{1,0:T(8,128)(2,1)S(1)}, u32[]{:S(2)}, u32[]{:S(2)}) collective-permute-start(bf16[192,768]{1,0:T(8,128)(2,1)S(1)} %collective-permute-done.6), channel_id=1, source_target_pairs={{0,8},{4,12},{8,0},{12,4},{1,9},{5,13},{9,1},{13,5},{2,10},{6,14},... | collective-permute-start | bytes 884744 | tf_op jit(solution)/shard_map/ppermute | solution.py:29
  15.2 11.4 %collective-permute-start.14 = (bf16[192,192]{1,0:T(8,128)(2,1)S(1)}, bf16[192,192]{1,0:T(8,128)(2,1)S(1)}, u32[]{:S(2)}, u32[]{:S(2)}) collective-permute-start(bf16[192,192]{1,0:T(8,128)(2,1)S(1)} %collective-permute-done.13), channel_id=1, source_target_pairs={{0,1},{1,2},{2,3},{3,0},{4,5},{5,6},{6,7},{7,4},{8,9},{9,10},{10,1... | collective-permute-start | bytes 221192 | tf_op jit(solution)/shard_map/ppermute | solution.py:25
  15.6 17.3 %collective-permute-start.1 = (bf16[256,768]{1,0:T(8,128)(2,1)S(1)}, bf16[256,768]{1,0:T(8,128)(2,1)S(1)}, u32[]{:S(2)}, u32[]{:S(2)}) collective-permute-start(bf16[256,768]{1,0:T(8,128)(2,1)S(1)} %get-tuple-element.158.refs_4_), channel_id=1, source_target_pairs={{0,4},{4,0},{8,12},{12,8},{1,5},{5,1},{9,13},{13,9},{2,6},{6,2},{1... | collective-permute-start | bytes 1179656 | tf_op jit(solution)/shard_map/ppermute | solution.py:29
  25.5 11.9 %collective-permute-start.9 = (bf16[192,768]{1,0:T(8,128)(2,1)}, bf16[192,768]{1,0:T(8,128)(2,1)}, u32[]{:S(2)}, u32[]{:S(2)}) collective-permute-start(bf16[192,768]{1,0:T(8,128)(2,1)} %collective-permute-done.8), channel_id=1, source_target_pairs={{0,8},{4,12},{8,0},{12,4},{1,9},{5,13},{9,1},{13,5},{2,10},{6,14},... | collective-permute-start | bytes 884744 | tf_op jit(solution)/shard_map/ppermute | solution.py:29
  27.0 10.4 %collective-permute-start.10 = (bf16[192,768]{1,0:T(8,128)(2,1)}, bf16[192,768]{1,0:T(8,128)(2,1)}, u32[]{:S(2)}, u32[]{:S(2)}) collective-permute-start(bf16[192,768]{1,0:T(8,128)(2,1)} %collective-permute-done.8), channel_id=1, source_target_pairs={{0,1},{1,2},{2,3},{3,0},{4,5},{5,6},{6,7},{7,4},{8,9},{9,10},{10,1... | collective-permute-start | bytes 884744 | tf_op jit(solution)/shard_map/ppermute | solution.py:25
  41.1 13.3 %collective-permute-start.17 = (bf16[384,768]{1,0:T(8,128)(2,1)S(1)}, bf16[384,768]{1,0:T(8,128)(2,1)S(1)}, u32[]{:S(2)}, u32[]{:S(2)}) collective-permute-start(bf16[384,768]{1,0:T(8,128)(2,1)S(1)} %pad_maximum_fusion.2.proj_a), channel_id=1, source_target_pairs={{0,4},{4,0},{8,12},{12,8},{1,5},{5,1},{9,13},{13,9},{2,6},{6,2},{1... | collective-permute-start | bytes 1769480 | tf_op jit(solution)/shard_map/ppermute | solution.py:29
  56.6 18.8 %collective-permute-start.19 = (bf16[256,768]{1,0:T(8,128)(2,1)S(1)}, bf16[256,768]{1,0:T(8,128)(2,1)S(1)}, u32[]{:S(2)}, u32[]{:S(2)}) collective-permute-start(bf16[256,768]{1,0:T(8,128)(2,1)S(1)} %get-tuple-element.125.mine_ref), channel_id=1, source_target_pairs={{0,16},{16,0},{1,17},{17,1},{2,18},{18,2},{3,19},{19,3},{4,20},{20... | collective-permute-start | bytes 1179656 | tf_op jit(solution)/shard_map/ppermute | solution.py:52
  57.8 18.2 %collective-permute-start.27 = (bf16[256,768]{1,0:T(8,128)(2,1)S(1)}, bf16[256,768]{1,0:T(8,128)(2,1)S(1)}, u32[]{:S(2)}, u32[]{:S(2)}) collective-permute-start(bf16[256,768]{1,0:T(8,128)(2,1)S(1)} %get-tuple-element.125.mine_ref), channel_id=1, source_target_pairs={{0,8},{4,12},{8,0},{12,4},{1,9},{5,13},{9,1},{13,5},{2,10},{6,14},... | collective-permute-start | bytes 1179656 | tf_op jit(solution)/shard_map/ppermute | solution.py:29
  59.4 9.8 %collective-permute-start.21 = (bf16[128,768]{1,0:T(8,128)(2,1)S(1)}, bf16[128,768]{1,0:T(8,128)(2,1)S(1)}, u32[]{:S(2)}, u32[]{:S(2)}) collective-permute-start(bf16[128,768]{1,0:T(8,128)(2,1)S(1)} %get-tuple-element.190), channel_id=1, source_target_pairs={{0,17},{1,18},{2,19},{3,16},{16,1},{17,2},{18,3},{19,0},{4,21},{5,... | collective-permute-start | bytes 589832 | tf_op jit(solution)/shard_map/ppermute | solution.py:47
  61.5 15.8 %collective-permute-start.24 = (bf16[512,192]{1,0:T(8,128)(2,1)S(1)}, bf16[512,192]{1,0:T(8,128)(2,1)S(1)}, u32[]{:S(2)}, u32[]{:S(2)}) collective-permute-start(bf16[512,192]{1,0:T(8,128)(2,1)S(1)} %get-tuple-element.189), channel_id=1, source_target_pairs={{0,8},{4,12},{8,0},{12,4},{1,9},{5,13},{9,1},{13,5},{2,10},{6,14},... | collective-permute-start | bytes 589832 | tf_op jit(solution)/shard_map/ppermute | solution.py:29
  65.0 12.4 %collective-permute-start.22 = (bf16[128,768]{1,0:T(8,128)(2,1)S(1)}, bf16[128,768]{1,0:T(8,128)(2,1)S(1)}, u32[]{:S(2)}, u32[]{:S(2)}) collective-permute-start(bf16[128,768]{1,0:T(8,128)(2,1)S(1)} %collective-permute-done.20), channel_id=1, source_target_pairs={{0,1},{1,2},{2,3},{3,0},{4,5},{5,6},{6,7},{7,4},{8,9},{9,10},{10,1... | collective-permute-start | bytes 589832 | tf_op jit(solution)/shard_map/ppermute | solution.py:25
  75.4 11.6 %collective-permute-start.26 = (bf16[256,768]{1,0:T(8,128)(2,1)S(1)}, bf16[256,768]{1,0:T(8,128)(2,1)S(1)}, u32[]{:S(2)}, u32[]{:S(2)}) collective-permute-start(bf16[256,768]{1,0:T(8,128)(2,1)S(1)} %pad_maximum_fusion.3), channel_id=1, source_target_pairs={{0,8},{4,12},{8,0},{12,4},{1,9},{5,13},{9,1},{13,5},{2,10},{6,14},... | collective-permute-start | bytes 1179656 | tf_op jit(solution)/shard_map/ppermute | solution.py:29
  76.0 11.0 %collective-permute-start.28 = (bf16[256,768]{1,0:T(8,128)(2,1)S(1)}, bf16[256,768]{1,0:T(8,128)(2,1)S(1)}, u32[]{:S(2)}, u32[]{:S(2)}) collective-permute-start(bf16[256,768]{1,0:T(8,128)(2,1)S(1)} %collective-permute-done.27), channel_id=1, source_target_pairs={{0,16},{16,0},{1,17},{17,1},{2,18},{18,2},{3,19},{19,3},{4,20},{20... | collective-permute-start | bytes 1179656 | tf_op jit(solution)/shard_map/ppermute | solution.py:52
  78.9 14.5 %collective-permute-start.30 = (bf16[256,768]{1,0:T(8,128)(2,1)S(1)}, bf16[256,768]{1,0:T(8,128)(2,1)S(1)}, u32[]{:S(2)}, u32[]{:S(2)}) collective-permute-start(bf16[256,768]{1,0:T(8,128)(2,1)S(1)} %pad_maximum_fusion.4), channel_id=1, source_target_pairs={{0,8},{4,12},{8,0},{12,4},{1,9},{5,13},{9,1},{13,5},{2,10},{6,14},... | collective-permute-start | bytes 1179656 | tf_op jit(solution)/shard_map/ppermute | solution.py:29
  82.8 18.9 %collective-permute-start.33 = (bf16[256,768]{1,0:T(8,128)(2,1)S(1)}, bf16[256,768]{1,0:T(8,128)(2,1)S(1)}, u32[]{:S(2)}, u32[]{:S(2)}) collective-permute-start(bf16[256,768]{1,0:T(8,128)(2,1)S(1)} %get-tuple-element.125.mine_ref), channel_id=1, source_target_pairs={{0,4},{4,0},{8,12},{12,8},{1,5},{5,1},{9,13},{13,9},{2,6},{6,2},{1... | collective-permute-start | bytes 1179656 | tf_op jit(solution)/shard_map/ppermute | solution.py:29
  87.0 10.5 %collective-permute-start.31 = (bf16[128,768]{1,0:T(8,128)(2,1)S(1)}, bf16[128,768]{1,0:T(8,128)(2,1)S(1)}, u32[]{:S(2)}, u32[]{:S(2)}) collective-permute-start(bf16[128,768]{1,0:T(8,128)(2,1)S(1)} %collective-permute-done.25), channel_id=1, source_target_pairs={{0,8},{4,12},{8,0},{12,4},{1,9},{5,13},{9,1},{13,5},{2,10},{6,14},... | collective-permute-start | bytes 589832 | tf_op jit(solution)/shard_map/ppermute | solution.py:29
  88.0 13.7 %collective-permute-start.32 = (bf16[128,768]{1,0:T(8,128)(2,1)S(1)}, bf16[128,768]{1,0:T(8,128)(2,1)S(1)}, u32[]{:S(2)}, u32[]{:S(2)}) collective-permute-start(bf16[128,768]{1,0:T(8,128)(2,1)S(1)} %collective-permute-done.29), channel_id=1, source_target_pairs={{0,8},{4,12},{8,0},{12,4},{1,9},{5,13},{9,1},{13,5},{2,10},{6,14},... | collective-permute-start | bytes 589832 | tf_op jit(solution)/shard_map/ppermute | solution.py:29
  102.6 23.3 %collective-permute-start.34 = (bf16[256,768]{1,0:T(8,128)(2,1)}, bf16[256,768]{1,0:T(8,128)(2,1)}, u32[]{:S(2)}, u32[]{:S(2)}) collective-permute-start(bf16[256,768]{1,0:T(8,128)(2,1)} %get-tuple-element.134.refs_8_), channel_id=1, source_target_pairs={{0,8},{4,12},{8,0},{12,4},{1,9},{5,13},{9,1},{13,5},{2,10},{6,14},... | collective-permute-start | bytes 1179656 | tf_op jit(solution)/shard_map/ppermute | solution.py:29
  103.1 22.8 %collective-permute-start.35 = (bf16[256,768]{1,0:T(8,128)(2,1)}, bf16[256,768]{1,0:T(8,128)(2,1)}, u32[]{:S(2)}, u32[]{:S(2)}) collective-permute-start(bf16[256,768]{1,0:T(8,128)(2,1)} %get-tuple-element.135.refs_12_), channel_id=1, source_target_pairs={{0,8},{4,12},{8,0},{12,4},{1,9},{5,13},{9,1},{13,5},{2,10},{6,14},... | collective-permute-start | bytes 1179656 | tf_op jit(solution)/shard_map/ppermute | solution.py:29
  111.4 13.3 %all-to-all-start = ((f32[32,1,512]{2,1,0:T(1,128)}), f32[32,1,512]{2,1,0:T(1,128)}, u32[]{:S(2)}, u32[]{:S(2)}) async-start(f32[32,1,512]{2,1,0:T(1,128)} %copy-done.32), calls=%async_computation | async-start | bytes 131072 | tf_op jit(solution)/shard_map/all_to_all | solution.py:353
  118.8 10.7 %collective-permute-start.37 = (bf16[256,768]{1,0:T(8,128)(2,1)}, bf16[256,768]{1,0:T(8,128)(2,1)S(1)}, u32[]{:S(2)}, u32[]{:S(2)}) collective-permute-start(bf16[256,768]{1,0:T(8,128)(2,1)} %copy-done.16), channel_id=1, source_target_pairs={{0,4},{4,0},{8,12},{12,8},{1,5},{5,1},{9,13},{13,9},{2,6},{6,2},{1... | collective-permute-start | bytes 1179656 | tf_op jit(solution)/shard_map/ppermute | solution.py:29
  134.4 11.7 %collective-permute-start.40 = (bf16[384,768]{1,0:T(8,128)(2,1)S(1)}, bf16[384,768]{1,0:T(8,128)(2,1)S(1)}, u32[]{:S(2)}, u32[]{:S(2)}) collective-permute-start(bf16[384,768]{1,0:T(8,128)(2,1)S(1)} %copy-done.4), channel_id=1, source_target_pairs={{0,4},{4,0},{8,12},{12,8},{1,5},{5,1},{9,13},{13,9},{2,6},{6,2},{1... | collective-permute-start | bytes 1769480 | tf_op jit(solution)/shard_map/ppermute | solution.py:29
  134.6 10.3 %collective-permute-start.45 = (bf16[256,768]{1,0:T(8,128)(2,1)S(1)}, bf16[256,768]{1,0:T(8,128)(2,1)S(1)}, u32[]{:S(2)}, u32[]{:S(2)}) collective-permute-start(bf16[256,768]{1,0:T(8,128)(2,1)S(1)} %multiply_convert_fusion.2.refs_0_.embed_ref), channel_id=1, source_target_pairs={{0,8},{4,12},{8,0},{12,4},{1,9},{5,13},{9,1},{13,5},{2,10},{6,14},... | collective-permute-start | bytes 1179656 | tf_op jit(solution)/shard_map/ppermute | solution.py:29
  135.0 11.2 %collective-permute-start.41 = (bf16[384,768]{1,0:T(8,128)(2,1)S(1)}, bf16[384,768]{1,0:T(8,128)(2,1)S(1)}, u32[]{:S(2)}, u32[]{:S(2)}) collective-permute-start(bf16[384,768]{1,0:T(8,128)(2,1)S(1)} %copy-done.8), channel_id=1, source_target_pairs={{0,4},{4,0},{8,12},{12,8},{1,5},{5,1},{9,13},{13,9},{2,6},{6,2},{1... | collective-permute-start | bytes 1769480 | tf_op jit(solution)/shard_map/ppermute | solution.py:29
  135.6 10.6 %collective-permute-start.42 = (bf16[384,768]{1,0:T(8,128)(2,1)S(1)}, bf16[384,768]{1,0:T(8,128)(2,1)S(1)}, u32[]{:S(2)}, u32[]{:S(2)}) collective-permute-start(bf16[384,768]{1,0:T(8,128)(2,1)S(1)} %copy-done.6), channel_id=1, source_target_pairs={{0,4},{4,0},{8,12},{12,8},{1,5},{5,1},{9,13},{13,9},{2,6},{6,2},{1... | collective-permute-start | bytes 1769480 | tf_op jit(solution)/shard_map/ppermute | solution.py:29
  135.7 10.5 %collective-permute-start.43 = (bf16[384,768]{1,0:T(8,128)(2,1)S(1)}, bf16[384,768]{1,0:T(8,128)(2,1)S(1)}, u32[]{:S(2)}, u32[]{:S(2)}) collective-permute-start(bf16[384,768]{1,0:T(8,128)(2,1)S(1)} %copy-done.10), channel_id=1, source_target_pairs={{0,4},{4,0},{8,12},{12,8},{1,5},{5,1},{9,13},{13,9},{2,6},{6,2},{1... | collective-permute-start | bytes 1769480 | tf_op jit(solution)/shard_map/ppermute | solution.py:29
  152.0 10.4 %collective-permute-start.47 = (bf16[256,768]{1,0:T(8,128)(2,1)S(1)}, bf16[256,768]{1,0:T(8,128)(2,1)S(1)}, u32[]{:S(2)}, u32[]{:S(2)}) collective-permute-start(bf16[256,768]{1,0:T(8,128)(2,1)S(1)} %copy-done.25), channel_id=1, source_target_pairs={{0,8},{4,12},{8,0},{12,4},{1,9},{5,13},{9,1},{13,5},{2,10},{6,14},... | collective-permute-start | bytes 1179656 | tf_op jit(solution)/shard_map/ppermute | solution.py:29
  152.5 15.7 %collective-permute-start.51 = (bf16[192,960]{1,0:T(8,128)(2,1)S(1)}, bf16[192,960]{1,0:T(8,128)(2,1)S(1)}, u32[]{:S(2)}, u32[]{:S(2)}) collective-permute-start(bf16[192,960]{1,0:T(8,128)(2,1)S(1)} %get-tuple-element.172), channel_id=1, source_target_pairs={{0,1},{1,2},{2,3},{3,0},{4,5},{5,6},{6,7},{7,4},{8,9},{9,10},{10,1... | collective-permute-start | bytes 1105928 | tf_op jit(solution)/shard_map/ppermute | solution.py:25
  152.9 33.1 %collective-permute-start.50 = (bf16[192,960]{1,0:T(8,128)(2,1)S(1)}, bf16[192,960]{1,0:T(8,128)(2,1)S(1)}, u32[]{:S(2)}, u32[]{:S(2)}) collective-permute-start(bf16[192,960]{1,0:T(8,128)(2,1)S(1)} %get-tuple-element.171), channel_id=1, source_target_pairs={{0,2},{1,3},{2,0},{3,1},{4,6},{5,7},{6,4},{7,5},{8,10},{9,11},{10,... | collective-permute-start | bytes 1105928 | tf_op jit(solution)/shard_map/ppermute | solution.py:25
  156.0 33.0 %collective-permute-start.49 = (bf16[192,960]{1,0:T(8,128)(2,1)S(1)}, bf16[192,960]{1,0:T(8,128)(2,1)S(1)}, u32[]{:S(2)}, u32[]{:S(2)}) collective-permute-start(bf16[192,960]{1,0:T(8,128)(2,1)S(1)} %get-tuple-element.170), channel_id=1, source_target_pairs={{0,3},{1,0},{2,1},{3,2},{4,7},{5,4},{6,5},{7,6},{8,11},{9,8},{10,9... | collective-permute-start | bytes 1105928 | tf_op jit(solution)/shard_map/ppermute | solution.py:25
  162.4 27.4 %collective-permute-start.48 = (bf16[256,768]{1,0:T(8,128)(2,1)S(1)}, bf16[256,768]{1,0:T(8,128)(2,1)S(1)}, u32[]{:S(2)}, u32[]{:S(2)}) collective-permute-start(bf16[256,768]{1,0:T(8,128)(2,1)S(1)} %collective-permute-done.47.refs_2_), channel_id=1, source_target_pairs={{0,4},{4,0},{8,12},{12,8},{1,5},{5,1},{9,13},{13,9},{2,6},{6,2},{1... | collective-permute-start | bytes 1179656 | tf_op jit(solution)/shard_map/ppermute | solution.py:29
  (66 other events, 575.1 us)

commit v4 on v3

--- a/solution.py
+++ b/solution.py
@@ -97,18 +97,18 @@
     return jnp.dot(left, right, preferred_element_type=F32)
 
 
-def call(kernel, outs, *operands, name, in_specs=None, scalars=0):
+def call(kernel, outs, *operands, name, scalars=0, scratch=()):
     vmem, smem = pl.BlockSpec(memory_space=pltpu.VMEM), pl.BlockSpec(memory_space=pltpu.SMEM)
     specs = [smem] * scalars + [vmem] * (len(operands) - scalars)
-    for place, spec in (in_specs or {}).items():
-        specs[place] = spec
     held = sum(math.prod(shape) * jnp.dtype(dtype).itemsize for shape, dtype in outs)
     held += sum(value.size * value.dtype.itemsize for value in operands)
+    held += sum(math.prod(buffer.shape) * jnp.dtype(buffer.dtype).itemsize for buffer in scratch)
     return pl.pallas_call(
         kernel,
         out_shape=[jax.ShapeDtypeStruct(shape, dtype) for shape, dtype in outs],
         in_specs=specs,
         out_specs=[vmem] * len(outs),
+        scratch_shapes=scratch,
         compiler_params=pltpu.CompilerParams(vmem_limit_bytes=min(held + 12 * 2**20, 56 * 2**20)),
         cost_estimate=pl.CostEstimate(flops=1, bytes_accessed=1, transcendentals=0),
         name=name,
@@ -128,33 +128,42 @@
     return call(kernel, outs, places, preact, name="activate", scalars=1)
 
 
-def score_rows(log_scale, mine, mate, others, device_count):
-    rows = mine.shape[0]
-    width = others.shape[0]
-
-    def kernel(scale_ref, mine_ref, mate_ref, others_ref, scores_mine, scores_mate, lse):
-        halves = (scores_mine, scores_mate)
-        logit_scale = scale_ref[0, 0]
+def score_rows(scale, mine, mate, others, device_count):
+    rows, width, block = mine.shape[0], others.shape[0], 256
+
+    def kernel(scale_ref, mine_ref, mate_ref, others_ref, lse, held):
         for half, ref in enumerate((mine_ref, mate_ref)):
-            scores = halves[half]
             largest = None
-            for place in range(0, width, 256):
-                part = logit_scale * dot_nt(ref[...], others_ref[place : place + 256])
-                scores[:, place : place + 256] = part
+            for place in range(0, width, block):
+                part = scale_ref[0, 0] * dot_nt(ref[...], others_ref[place : place + block])
+                held[half, :, place : place + block] = part
                 here = jnp.max(part, axis=1, keepdims=True)
                 largest = here if largest is None else jnp.maximum(largest, here)
             total = jnp.zeros_like(largest)
-            for place in range(0, width, 256):
-                part = scores[:, place : place + 256]
+            for place in range(0, width, block):
+                part = held[half, :, place : place + block]
                 total += jnp.sum(jnp.exp(part - largest), axis=1, keepdims=True)
             value = jnp.broadcast_to(largest + jnp.log(total), (rows, 128))
             row = value.T[:1]
             for device in range(device_count):
                 lse[device, :, half * rows : (half + 1) * rows] = row
 
-    outs = [((rows, width), F32)] * 2 + [((device_count, 1, 2 * rows), F32)]
-    scale = jnp.exp(log_scale).reshape(1, 1)
-    return call(kernel, outs, scale, mine, mate, others, name="scores", scalars=1)
+    outs = [((device_count, 1, 2 * rows), F32)]
+    scratch = [pltpu.VMEM((2, rows, width), F32)]
+    return call(kernel, outs, scale, mine, mate, others, name="scores", scalars=1, scratch=scratch)[0]
+
+
+def score_values(scale, mine, mate, others):
+    rows, width, block = mine.shape[0], others.shape[0], 256
+
+    def kernel(scale_ref, mine_ref, mate_ref, others_ref, *outs):
+        for ref, out in zip((mine_ref, mate_ref), outs):
+            for place in range(0, width, block):
+                part = dot_nt(ref[...], others_ref[place : place + block])
+                out[:, place : place + block] = scale_ref[0, 0] * part
+
+    outs = [((rows, width), F32)] * 2
+    return call(kernel, outs, scale, mine, mate, others, name="values", scalars=1)
 
 
 def combine_lse(where, lse_all, count):
@@ -328,14 +337,15 @@
     stream_even = {0: stream_blocks[0]}
     for i, j in enumerate(evens[1:], 1):
         stream_even[j] = swap(stream_blocks[i], "grow", j)
-    across = swap_across(unit_b)
     near = {j: swap_across(part) for j, part in spread(unit_b).items() if j}
-    near[0] = across
+    halves = jnp.split(unit_b, 2, 0)
+    hops = [shift_across(part) for part in halves]
+    across = near[0] = swap_across(after(unit_b, hops[0], stream_even[last]))
     rings = []
-    for part in jnp.split(unit_b, 2, 0):
-        blocks = [None, shift_across(part)]
+    for hop in hops:
+        blocks = [None, hop]
         for k in ks[2:]:
-            pace = (across, stream_even[last]) if k == 3 else ()
+            pace = (across,) if k == 3 else ()
             blocks.append(shift(after(blocks[-1], *pace), "gcol", 1))
         rings.append(blocks)
     unit_mate = swap(after(unit_b, rings[0][-1]), "grow", 1)
@@ -349,7 +359,9 @@
     others, unit_mate, unit_b, active_even, stream_even, active, log_scale = lax.optimization_barrier(
         (others, unit_mate, unit_b, active_even, stream_even, active, log_scale)
     )
-    scores_own, scores_mate, lse = score_rows(log_scale, unit_b, unit_mate, others, device_count)
+    logit_scale = jnp.exp(log_scale)
+    lse = score_rows(logit_scale.reshape(1, 1), unit_b, unit_mate, others, device_count)
+    scores_own, scores_mate = score_values(logit_scale.reshape(1, 1), unit_b, after(unit_mate, lse), others)
     lse_all = lax.all_to_all(lse, ("tower", "grow", "gcol"), 0, 0)
 
     far = (Lane(), Lane())
@@ -365,8 +377,6 @@
     for j, k in order:
         where += [device(1 - tower, j, k), device(1 - tower, j ^ 1, k)]
     row_lse, other_lse = combine_lse(jnp.stack(where), lse_all, len(order))
-    logit_scale = jnp.exp(log_scale)
-
     def embed_gradient(part, lse, diagonal):
         grad = 0.5 * (jnp.exp(part - lse) + jnp.exp(part - other_lse))
         return logit_scale * dot_nn((grad - diagonal).astype(BF16), others)

time: 193 us -> 190 us (0.984)
  waiting for transfers between devices: 82.9 us -> 80.2 us
    ppermute x35, waiting for transfers between devices: 42.2 us -> 47.6 us  [swap(): lax.ppermute(value, axis, [(i, i ^ bit) for i in range(lax.axis_size(axis...]
    ppermute x2, waiting for transfers between devices: 5.22 us -> 1.28 us  [swap_across(): lax.ppermute(value, 'tower', [(t, towers - 1 - t) for t in range(towers)])]
    all_to_all x1, waiting for transfers between devices: 5.48 us -> 1.77 us  [body(): lse_all = lax.all_to_all(lse, ('tower', 'grow', 'gcol'), 0, 0)]
    ppermute x13, starting transfers between devices: 12.4 us -> 15.4 us  [shift(): lax.ppermute(value, axis, [(i, (i + step) % count) for i in range(count)])]
    ppermute x2, waiting for transfers between devices: 5.69 us -> 3.42 us  [shift_across(): return lax.ppermute(value, ('tower', 'gcol'), pairs)]
    ppermute x2, starting transfers between devices: 2.48 us -> 0.51 us  [swap_across(): lax.ppermute(value, 'tower', [(t, towers - 1 - t) for t in range(towers)])]
    pallas_call x6 -> x7, Pallas kernels: 14 us -> 15.9 us  [call(): pl.pallas_call(kernel, out_shape=[jax.ShapeDtypeStruct(shape, dtype) for...]
    unnamed x104 -> x102, local copies, waits for them, and re-layouts: 8.84 us -> 10.5 us
  transfers between devices with their start and end apart: 53 -> 53, of which waited for: 20 -> 22; matrix products, arithmetic and copies ran while one was open for 12% -> 11% of each run, Pallas kernels for 5% -> 6%
where the time goes in v4:
time: 190 us; the launch traced here: 189 us
  waiting for transfers between devices  80.2 us (42%)
  starting transfers between devices  59.8 us (31%)
  local copies, waits for them, and re-layouts  16.3 us (9%)
  Pallas kernels  15.9 us (8%)
  matrix products  9.66 us (5%)
  other arithmetic  4.93 us (3%)
  between operations  2.21 us (1%)
    ppermute x35, waiting for transfers between devices, swap(): lax.ppermute(value, axis, [(i, i ^ bit) for i in range(lax.axis_size(axis...  47.6 us
    ppermute x35, starting transfers between devices, swap(): lax.ppermute(value, axis, [(i, i ^ bit) for i in range(lax.axis_size(axis...  35 us
    ppermute x13, waiting for transfers between devices, shift(): lax.ppermute(value, axis, [(i, (i + step) % count) for i in range(count)])  26.1 us
    pallas_call x7, Pallas kernels, call(): pl.pallas_call(kernel, out_shape=[jax.ShapeDtypeStruct(shape, dtype) for...  15.9 us
    ppermute x13, starting transfers between devices, shift(): lax.ppermute(value, axis, [(i, (i + step) % count) for i in range(count)])  15.4 us
    unnamed x102, local copies, waits for them, and re-layouts  10.5 us
    all_to_all x1, starting transfers between devices, body(): lse_all = lax.all_to_all(lse, ('tower', 'grow', 'gcol'), 0, 0)  6.55 us
    dot_general x3, matrix products, dot_nn(): return jnp.dot(left, right, preferred_element_type=F32)  5.05 us
  transfers between devices with their start and end apart: 53, of which 22 were waited for; matrix products, arithmetic and copies ran while one was open for 11% of the time, Pallas kernels for 6%

profile of v4, /device:TPU:9, one launch (start us, length us, event | category | flops | bytes accessed | tf_op | source)
XLA Modules:
  0.0 189.0 jit_solution(16924832921968441736)
XLA Ops:
  4.7 1.6 activate.1
  12.3 2.2 %dynamic-slice_bitcast_fusion.3 = (bf16[256,192]{1,0:T(8,128)(2,1)}, bf16[256,192]{1,0:T(8,128)(2,1)}, bf16[256,192]{1,0:T(8,128)(2,1)S(1)}, bf16[256,192]{1,0:T(8,128)(2,1)S(1)}) fusion(bf16[1,256,768]{2,1,0:T(8,128)(2,1)} %param.5, s32[]{:T(128)S(6)} %select_n.25, s32[]{:T(128)S(6)} %select_n.26, s32[]{:T(128)S(6)} %select_n.28, s32[]{:T(128)S(6)} %select_n.27), kind=kLoop, calls=%fused_computation.52 | loop fusion | bytes 786448 | tf_op jit(solution)/shard_map/dynamic_slice | solution.py:311
  15.6 3.6 %collective-permute-start.1 = (bf16[256,768]{1,0:T(8,128)(2,1)S(1)}, bf16[256,768]{1,0:T(8,128)(2,1)S(1)}, u32[]{:S(2)}, u32[]{:S(2)}) collective-permute-start(bf16[256,768]{1,0:T(8,128)(2,1)S(1)} %get-tuple-element.160.refs_4_), channel_id=1, source_target_pairs={{0,4},{4,0},{8,12},{12,8},{1,5},{5,1},{9,13},{13,9},{2,6},{6,2},{1... | collective-permute-start | bytes 1179656 | tf_op jit(solution)/shard_map/ppermute | solution.py:29
  19.2 6.3 %collective-permute-done.7 = bf16[192,768]{1,0:T(8,128)(2,1)S(1)} collective-permute-done((bf16[192,768]{1,0:T(8,128)(2,1)S(1)}, bf16[192,768]{1,0:T(8,128)(2,1)S(1)}, u32[]{:S(2)}, u32[]{:S(2)}) %collective-permute-start.7) | collective-permute-done | bytes 294944 | tf_op jit(solution)/shard_map/ppermute | solution.py:29
  32.1 4.0 %collective-permute-start.2 = (bf16[256,768]{1,0:T(8,128)(2,1)}, bf16[256,768]{1,0:T(8,128)(2,1)S(1)}, u32[]{:S(2)}, u32[]{:S(2)}) collective-permute-start(bf16[256,768]{1,0:T(8,128)(2,1)} %get-tuple-element.136.refs_8_), channel_id=1, source_target_pairs={{0,4},{4,0},{8,12},{12,8},{1,5},{5,1},{9,13},{13,9},{2,6},{6,2},{1... | collective-permute-start | bytes 1179656 | tf_op jit(solution)/shard_map/ppermute | solution.py:29
  41.1 2.8 %collective-permute-start.17 = (bf16[384,768]{1,0:T(8,128)(2,1)S(1)}, bf16[384,768]{1,0:T(8,128)(2,1)S(1)}, u32[]{:S(2)}, u32[]{:S(2)}) collective-permute-start(bf16[384,768]{1,0:T(8,128)(2,1)S(1)} %pad_maximum_fusion.2.proj_a), channel_id=1, source_target_pairs={{0,4},{4,0},{8,12},{12,8},{1,5},{5,1},{9,13},{13,9},{2,6},{6,2},{1... | collective-permute-start | bytes 1769480 | tf_op jit(solution)/shard_map/ppermute | solution.py:29
  43.9 2.2 %collective-permute-done.11 = bf16[192,768]{1,0:T(8,128)(2,1)S(1)} collective-permute-done((bf16[192,768]{1,0:T(8,128)(2,1)}, bf16[192,768]{1,0:T(8,128)(2,1)S(1)}, u32[]{:S(2)}, u32[]{:S(2)}) %collective-permute-start.11) | collective-permute-done | bytes 294944 | tf_op jit(solution)/shard_map/ppermute | solution.py:29
  46.2 1.8 fusion.16
  48.0 2.3 %collective-permute-start.4 = (bf16[256,384]{1,0:T(8,128)(2,1)S(1)}, bf16[256,384]{1,0:T(8,128)(2,1)S(1)}, u32[]{:S(2)}, u32[]{:S(2)}) collective-permute-start(bf16[256,384]{1,0:T(8,128)(2,1)S(1)} %copy-done.41), channel_id=1, source_target_pairs={{0,4},{4,0},{8,12},{12,8},{1,5},{5,1},{9,13},{13,9},{2,6},{6,2},{1... | collective-permute-start | bytes 589832 | tf_op jit(solution)/shard_map/ppermute | solution.py:29
  55.9 2.3 %collective-permute-start.19 = (bf16[128,768]{1,0:T(8,128)(2,1)S(1)}, bf16[128,768]{1,0:T(8,128)(2,1)S(1)}, u32[]{:S(2)}, u32[]{:S(2)}) collective-permute-start(bf16[128,768]{1,0:T(8,128)(2,1)S(1)} %get-tuple-element.193), channel_id=1, source_target_pairs={{0,17},{1,18},{2,19},{3,16},{16,1},{17,2},{18,3},{19,0},{4,21},{5,... | collective-permute-start | bytes 589832 | tf_op jit(solution)/shard_map/ppermute | solution.py:47
  60.4 3.4 %collective-permute-done.19 = bf16[128,768]{1,0:T(8,128)(2,1)S(1)} collective-permute-done((bf16[128,768]{1,0:T(8,128)(2,1)S(1)}, bf16[128,768]{1,0:T(8,128)(2,1)S(1)}, u32[]{:S(2)}, u32[]{:S(2)}) %collective-permute-start.19) | collective-permute-done | bytes 196640 | tf_op jit(solution)/shard_map/ppermute | solution.py:47
  63.9 2.4 %collective-permute-done.20.refs_17_ = bf16[512,192]{1,0:T(8,128)(2,1)S(1)} collective-permute-done((bf16[512,192]{1,0:T(8,128)(2,1)S(1)}, bf16[512,192]{1,0:T(8,128)(2,1)S(1)}, u32[]{:S(2)}, u32[]{:S(2)}) %collective-permute-start.20) | collective-permute-done | bytes 196640 | tf_op jit(solution)/shard_map/ppermute | solution.py:29
  67.4 2.8 %collective-permute-start.24 = (bf16[128,768]{1,0:T(8,128)(2,1)S(1)}, bf16[128,768]{1,0:T(8,128)(2,1)S(1)}, u32[]{:S(2)}, u32[]{:S(2)}) collective-permute-start(bf16[128,768]{1,0:T(8,128)(2,1)S(1)} %collective-permute-done.22), channel_id=1, source_target_pairs={{0,1},{1,2},{2,3},{3,0},{4,5},{5,6},{6,7},{7,4},{8,9},{9,10},{10,1... | collective-permute-start | bytes 589832 | tf_op jit(solution)/shard_map/ppermute | solution.py:25
  70.8 3.9 %collective-permute-done.27 = bf16[256,768]{1,0:T(8,128)(2,1)S(1)} collective-permute-done((bf16[256,768]{1,0:T(8,128)(2,1)S(1)}, bf16[256,768]{1,0:T(8,128)(2,1)S(1)}, u32[]{:S(2)}, u32[]{:S(2)}) %collective-permute-start.27) | collective-permute-done | bytes 393248 | tf_op jit(solution)/shard_map/ppermute | solution.py:29
  78.8 4.2 %collective-permute-done.26 = bf16[256,768]{1,0:T(8,128)(2,1)S(1)} collective-permute-done((bf16[256,768]{1,0:T(8,128)(2,1)S(1)}, bf16[256,768]{1,0:T(8,128)(2,1)S(1)}, u32[]{:S(2)}, u32[]{:S(2)}) %collective-permute-start.26) | collective-permute-done | bytes 393248 | tf_op jit(solution)/shard_map/ppermute | solution.py:29
  84.5 1.8 collective-permute-done.29
  87.3 4.0 %collective-permute-start.33 = (bf16[256,768]{1,0:T(8,128)(2,1)S(1)}, bf16[256,768]{1,0:T(8,128)(2,1)S(1)}, u32[]{:S(2)}, u32[]{:S(2)}) collective-permute-start(bf16[256,768]{1,0:T(8,128)(2,1)S(1)} %get-tuple-element.127.mine_ref), channel_id=1, source_target_pairs={{0,4},{4,0},{8,12},{12,8},{1,5},{5,1},{9,13},{13,9},{2,6},{6,2},{1... | collective-permute-start | bytes 1179656 | tf_op jit(solution)/shard_map/ppermute | solution.py:29
  91.5 4.2 %collective-permute-done.31 = bf16[128,768]{1,0:T(8,128)(2,1)S(1)} collective-permute-done((bf16[128,768]{1,0:T(8,128)(2,1)S(1)}, bf16[128,768]{1,0:T(8,128)(2,1)S(1)}, u32[]{:S(2)}, u32[]{:S(2)}) %collective-permute-start.31) | collective-permute-done | bytes 196640 | tf_op jit(solution)/shard_map/ppermute | solution.py:29
  95.7 4.2 %collective-permute-done.32 = bf16[128,768]{1,0:T(8,128)(2,1)S(1)} collective-permute-done((bf16[128,768]{1,0:T(8,128)(2,1)S(1)}, bf16[128,768]{1,0:T(8,128)(2,1)S(1)}, u32[]{:S(2)}, u32[]{:S(2)}) %collective-permute-start.32) | collective-permute-done | bytes 196640 | tf_op jit(solution)/shard_map/ppermute | solution.py:29
  103.8 2.4 %scores.1 = f32[32,1,512]{2,1,0:T(1,128)S(1)} custom-call(f32[1,1]{1,0:T(1,128)} %bitcast.17.scale_ref, bf16[256,768]{1,0:T(8,128)(2,1)S(1)} %get-tuple-element.127.mine_ref, bf16[256,768]{1,0:T(8,128)(2,1)S(1)} %copy-done.6, bf16[2048,768]{1,0:T(8,128)(2,1)S(1)} %constant_dynamic-update-slice_fusion.6.others_ref), custom_call_target="tpu_custom_call" | custom-call | flops 1 | bytes 1 | tf_op jit(solution)/shard_map/scores/pallas_call | solution.py:106
  106.9 6.6 %all-to-all-start = ((f32[32,1,512]{2,1,0:T(1,128)}), f32[32,1,512]{2,1,0:T(1,128)}, u32[]{:S(2)}, u32[]{:S(2)}) async-start(f32[32,1,512]{2,1,0:T(1,128)} %copy-done.31), calls=%async_computation | async-start | bytes 131072 | tf_op jit(solution)/shard_map/all_to_all | solution.py:365
  114.6 1.8 values.1
  119.4 1.8 all-to-all-done.lse_ref
  122.4 3.1 %convolution_multiply_fusion.1 = f32[256,768]{1,0:T(8,128)S(1)} fusion(bf16[2048,768]{1,0:T(8,128)(2,1)S(1)} %constant_dynamic-update-slice_fusion.6.others_ref, f32[256,2048]{1,0:T(8,128)} %copy-done.34, f32[2048]{0:T(1024)S(1)} %bitcast.54, f32[256]{0:T(256)S(1)} %get-tuple-element.187, f32[]{:T(128)} %exp.15), kind=kOutput, calls=%fused_computation.4 | convolution fusion | flops 808124416 | bytes 6038532 | tf_op jit(solution)/shard_map/dot_general | solution.py:97
  126.1 2.6 %collective-permute-done.38.refs_11_ = bf16[256,768]{1,0:T(8,128)(2,1)S(1)} collective-permute-done((bf16[256,768]{1,0:T(8,128)(2,1)}, bf16[256,768]{1,0:T(8,128)(2,1)S(1)}, u32[]{:S(2)}, u32[]{:S(2)}) %collective-permute-start.38) | collective-permute-done | bytes 393248 | tf_op jit(solution)/shard_map/ppermute | solution.py:29
  132.2 9.2 %collective-permute-done.45.refs_2_ = bf16[256,768]{1,0:T(8,128)(2,1)S(1)} collective-permute-done((bf16[256,768]{1,0:T(8,128)(2,1)S(1)}, bf16[256,768]{1,0:T(8,128)(2,1)S(1)}, u32[]{:S(2)}, u32[]{:S(2)}) %collective-permute-start.45) | collective-permute-done | bytes 393248 | tf_op jit(solution)/shard_map/ppermute | solution.py:29
  144.5 4.0 %terms.1 = (bf16[192,960]{1,0:T(8,128)(2,1)S(1)}, bf16[192,960]{1,0:T(8,128)(2,1)S(1)}, bf16[192,960]{1,0:T(8,128)(2,1)S(1)}, f32[192,192]{1,0:T(8,128)S(1)}, bf16[192,1024]{1,0:T(8,128)(2,1)S(1)}) custom-call(s32[4]{0:T(128)S(1)} %get-tuple-element.95.places_ref, bf16[192,768]{1,0:T(8,128)(2,1)S(1)} %slice.45.proj_ref, ...), custom_call_target="tpu_custom_call" | custom-call | flops 1 | bytes 1 | tf_op jit(solution)/shard_map/terms/pallas_call | solution.py:106
  149.2 2.7 %collective-permute-start.50 = (bf16[192,960]{1,0:T(8,128)(2,1)S(1)}, bf16[192,960]{1,0:T(8,128)(2,1)S(1)}, u32[]{:S(2)}, u32[]{:S(2)}) collective-permute-start(bf16[192,960]{1,0:T(8,128)(2,1)S(1)} %get-tuple-element.173), channel_id=1, source_target_pairs={{0,2},{1,3},{2,0},{3,1},{4,6},{5,7},{6,4},{7,5},{8,10},{9,11},{10,... | collective-permute-start | bytes 1105928 | tf_op jit(solution)/shard_map/ppermute | solution.py:25
  153.4 5.6 %collective-permute-done.47.refs_2_ = bf16[256,768]{1,0:T(8,128)(2,1)S(1)} collective-permute-done((bf16[256,768]{1,0:T(8,128)(2,1)S(1)}, bf16[256,768]{1,0:T(8,128)(2,1)S(1)}, u32[]{:S(2)}, u32[]{:S(2)}) %collective-permute-start.47) | collective-permute-done | bytes 393248 | tf_op jit(solution)/shard_map/ppermute | solution.py:29
  160.2 4.5 %own_gradients.1 = (bf16[256,768]{1,0:T(8,128)(2,1)}, bf16[256,3072]{1,0:T(8,128)(2,1)}) custom-call(s32[4]{0:T(128)S(1)} %get-tuple-element.95.places_ref, s32[4]{0:T(128)S(1)} %get-tuple-element.96.found_ref, bf16[256,3072]{1,0:T(8,128)(2,1)S(1)} %bitcast.53, bf16[256,768]{1,0:T(8,128)(2,1)S(1)} %multiply_convert_fusion.2.refs_0_.embed_ref, ...), custom_call_target="tpu_custom_call" | custom-call | flops 1 | bytes 1 | tf_op jit(solution)/shard_map/own_gradients/pallas_call | solution.py:106
  164.7 17.6 %collective-permute-done.50 = bf16[192,960]{1,0:T(8,128)(2,1)S(1)} collective-permute-done((bf16[192,960]{1,0:T(8,128)(2,1)S(1)}, bf16[192,960]{1,0:T(8,128)(2,1)S(1)}, u32[]{:S(2)}, u32[]{:S(2)}) %collective-permute-start.50) | collective-permute-done | bytes 368672 | tf_op jit(solution)/shard_map/ppermute | solution.py:25
  182.3 4.5 %collective-permute-done.49 = bf16[192,960]{1,0:T(8,128)(2,1)S(1)} collective-permute-done((bf16[192,960]{1,0:T(8,128)(2,1)S(1)}, bf16[192,960]{1,0:T(8,128)(2,1)S(1)}, u32[]{:S(2)}, u32[]{:S(2)}) %collective-permute-start.49) | collective-permute-done | bytes 368672 | tf_op jit(solution)/shard_map/ppermute | solution.py:25
  (215 shorter events, 60.4 us)
Async XLA Ops:
  6.3 9.2 %collective-permute-start = (bf16[256,768]{1,0:T(8,128)(2,1)S(1)}, bf16[256,768]{1,0:T(8,128)(2,1)S(1)}, u32[]{:S(2)}, u32[]{:S(2)}) collective-permute-start(bf16[256,768]{1,0:T(8,128)(2,1)S(1)} %get-tuple-element.182.refs_0_), channel_id=1, source_target_pairs={{0,4},{4,0},{8,12},{12,8},{1,5},{5,1},{9,13},{13,9},{2,6},{6,2},{1... | collective-permute-start | bytes 1179656 | tf_op jit(solution)/shard_map/ppermute | solution.py:29
  8.9 45.8 %collective-permute-start.18 = (bf16[256,768]{1,0:T(8,128)(2,1)S(1)}, bf16[256,768]{1,0:T(8,128)(2,1)}, u32[]{:S(2)}, u32[]{:S(2)}) collective-permute-start(bf16[256,768]{1,0:T(8,128)(2,1)S(1)} %get-tuple-element.160.refs_4_), channel_id=1, source_target_pairs={{0,8},{4,12},{8,0},{12,4},{1,9},{5,13},{9,1},{13,5},{2,10},{6,14},... | collective-permute-start | bytes 1179656 | tf_op jit(solution)/shard_map/ppermute | solution.py:29
  9.8 15.8 %collective-permute-start.7 = (bf16[192,768]{1,0:T(8,128)(2,1)S(1)}, bf16[192,768]{1,0:T(8,128)(2,1)S(1)}, u32[]{:S(2)}, u32[]{:S(2)}) collective-permute-start(bf16[192,768]{1,0:T(8,128)(2,1)S(1)} %collective-permute-done.6), channel_id=1, source_target_pairs={{0,8},{4,12},{8,0},{12,4},{1,9},{5,13},{9,1},{13,5},{2,10},{6,14},... | collective-permute-start | bytes 884744 | tf_op jit(solution)/shard_map/ppermute | solution.py:29
  15.2 11.4 %collective-permute-start.14 = (bf16[192,192]{1,0:T(8,128)(2,1)S(1)}, bf16[192,192]{1,0:T(8,128)(2,1)S(1)}, u32[]{:S(2)}, u32[]{:S(2)}) collective-permute-start(bf16[192,192]{1,0:T(8,128)(2,1)S(1)} %collective-permute-done.13), channel_id=1, source_target_pairs={{0,1},{1,2},{2,3},{3,0},{4,5},{5,6},{6,7},{7,4},{8,9},{9,10},{10,1... | collective-permute-start | bytes 221192 | tf_op jit(solution)/shard_map/ppermute | solution.py:25
  15.6 16.6 %collective-permute-start.1 = (bf16[256,768]{1,0:T(8,128)(2,1)S(1)}, bf16[256,768]{1,0:T(8,128)(2,1)S(1)}, u32[]{:S(2)}, u32[]{:S(2)}) collective-permute-start(bf16[256,768]{1,0:T(8,128)(2,1)S(1)} %get-tuple-element.160.refs_4_), channel_id=1, source_target_pairs={{0,4},{4,0},{8,12},{12,8},{1,5},{5,1},{9,13},{13,9},{2,6},{6,2},{1... | collective-permute-start | bytes 1179656 | tf_op jit(solution)/shard_map/ppermute | solution.py:29
  25.5 11.2 %collective-permute-start.9 = (bf16[192,768]{1,0:T(8,128)(2,1)}, bf16[192,768]{1,0:T(8,128)(2,1)}, u32[]{:S(2)}, u32[]{:S(2)}) collective-permute-start(bf16[192,768]{1,0:T(8,128)(2,1)} %collective-permute-done.8), channel_id=1, source_target_pairs={{0,8},{4,12},{8,0},{12,4},{1,9},{5,13},{9,1},{13,5},{2,10},{6,14},... | collective-permute-start | bytes 884744 | tf_op jit(solution)/shard_map/ppermute | solution.py:29
  27.0 9.7 %collective-permute-start.10 = (bf16[192,768]{1,0:T(8,128)(2,1)}, bf16[192,768]{1,0:T(8,128)(2,1)}, u32[]{:S(2)}, u32[]{:S(2)}) collective-permute-start(bf16[192,768]{1,0:T(8,128)(2,1)} %collective-permute-done.8), channel_id=1, source_target_pairs={{0,1},{1,2},{2,3},{3,0},{4,5},{5,6},{6,7},{7,4},{8,9},{9,10},{10,1... | collective-permute-start | bytes 884744 | tf_op jit(solution)/shard_map/ppermute | solution.py:25
  31.9 9.1 %collective-permute-start.16 = (bf16[192,768]{1,0:T(8,128)(2,1)S(1)}, bf16[192,768]{1,0:T(8,128)(2,1)S(1)}, u32[]{:S(2)}, u32[]{:S(2)}) collective-permute-start(bf16[192,768]{1,0:T(8,128)(2,1)S(1)} %constant_dynamic-slice_fusion), channel_id=1, source_target_pairs={{0,8},{4,12},{8,0},{12,4},{1,9},{5,13},{9,1},{13,5},{2,10},{6,14},... | collective-permute-start | bytes 884744 | tf_op jit(solution)/shard_map/ppermute | solution.py:29
  36.7 9.3 %collective-permute-start.11 = (bf16[192,768]{1,0:T(8,128)(2,1)}, bf16[192,768]{1,0:T(8,128)(2,1)S(1)}, u32[]{:S(2)}, u32[]{:S(2)}) collective-permute-start(bf16[192,768]{1,0:T(8,128)(2,1)} %collective-permute-done.10), channel_id=1, source_target_pairs={{0,8},{4,12},{8,0},{12,4},{1,9},{5,13},{9,1},{13,5},{2,10},{6,14},... | collective-permute-start | bytes 884744 | tf_op jit(solution)/shard_map/ppermute | solution.py:29
  41.1 12.6 %collective-permute-start.17 = (bf16[384,768]{1,0:T(8,128)(2,1)S(1)}, bf16[384,768]{1,0:T(8,128)(2,1)S(1)}, u32[]{:S(2)}, u32[]{:S(2)}) collective-permute-start(bf16[384,768]{1,0:T(8,128)(2,1)S(1)} %pad_maximum_fusion.2.proj_a), channel_id=1, source_target_pairs={{0,4},{4,0},{8,12},{12,8},{1,5},{5,1},{9,13},{13,9},{2,6},{6,2},{1... | collective-permute-start | bytes 1769480 | tf_op jit(solution)/shard_map/ppermute | solution.py:29
  59.2 15.5 %collective-permute-start.27 = (bf16[256,768]{1,0:T(8,128)(2,1)S(1)}, bf16[256,768]{1,0:T(8,128)(2,1)S(1)}, u32[]{:S(2)}, u32[]{:S(2)}) collective-permute-start(bf16[256,768]{1,0:T(8,128)(2,1)S(1)} %get-tuple-element.127.mine_ref), channel_id=1, source_target_pairs={{0,8},{4,12},{8,0},{12,4},{1,9},{5,13},{9,1},{13,5},{2,10},{6,14},... | collective-permute-start | bytes 1179656 | tf_op jit(solution)/shard_map/ppermute | solution.py:29
  67.0 9.5 %collective-permute-start.21 = (bf16[256,768]{1,0:T(8,128)(2,1)S(1)}, bf16[256,768]{1,0:T(8,128)(2,1)S(1)}, u32[]{:S(2)}, u32[]{:S(2)}) collective-permute-start(bf16[256,768]{1,0:T(8,128)(2,1)S(1)} %get-tuple-element.127.mine_ref), channel_id=1, source_target_pairs={{0,16},{16,0},{1,17},{17,1},{2,18},{18,2},{3,19},{19,3},{4,20},{20... | collective-permute-start | bytes 1179656 | tf_op jit(solution)/shard_map/ppermute | solution.py:52
  70.2 12.8 %collective-permute-start.26 = (bf16[256,768]{1,0:T(8,128)(2,1)S(1)}, bf16[256,768]{1,0:T(8,128)(2,1)S(1)}, u32[]{:S(2)}, u32[]{:S(2)}) collective-permute-start(bf16[256,768]{1,0:T(8,128)(2,1)S(1)} %pad_maximum_fusion.3), channel_id=1, source_target_pairs={{0,8},{4,12},{8,0},{12,4},{1,9},{5,13},{9,1},{13,5},{2,10},{6,14},... | collective-permute-start | bytes 1179656 | tf_op jit(solution)/shard_map/ppermute | solution.py:29
  74.7 9.6 %collective-permute-start.28 = (bf16[256,768]{1,0:T(8,128)(2,1)S(1)}, bf16[256,768]{1,0:T(8,128)(2,1)S(1)}, u32[]{:S(2)}, u32[]{:S(2)}) collective-permute-start(bf16[256,768]{1,0:T(8,128)(2,1)S(1)} %collective-permute-done.27), channel_id=1, source_target_pairs={{0,16},{16,0},{1,17},{17,1},{2,18},{18,2},{3,19},{19,3},{4,20},{20... | collective-permute-start | bytes 1179656 | tf_op jit(solution)/shard_map/ppermute | solution.py:52
  75.6 15.9 %collective-permute-start.30 = (bf16[256,768]{1,0:T(8,128)(2,1)S(1)}, bf16[256,768]{1,0:T(8,128)(2,1)S(1)}, u32[]{:S(2)}, u32[]{:S(2)}) collective-permute-start(bf16[256,768]{1,0:T(8,128)(2,1)S(1)} %pad_maximum_fusion.4), channel_id=1, source_target_pairs={{0,8},{4,12},{8,0},{12,4},{1,9},{5,13},{9,1},{13,5},{2,10},{6,14},... | collective-permute-start | bytes 1179656 | tf_op jit(solution)/shard_map/ppermute | solution.py:29
  77.5 8.9 %collective-permute-start.29 = (bf16[128,768]{1,0:T(8,128)(2,1)S(1)}, bf16[128,768]{1,0:T(8,128)(2,1)S(1)}, u32[]{:S(2)}, u32[]{:S(2)}) collective-permute-start(bf16[128,768]{1,0:T(8,128)(2,1)S(1)} %collective-permute-done.24), channel_id=1, source_target_pairs={{0,1},{1,2},{2,3},{3,0},{4,5},{5,6},{6,7},{7,4},{8,9},{9,10},{10,1... | collective-permute-start | bytes 589832 | tf_op jit(solution)/shard_map/ppermute | solution.py:25
  84.3 11.4 %collective-permute-start.31 = (bf16[128,768]{1,0:T(8,128)(2,1)S(1)}, bf16[128,768]{1,0:T(8,128)(2,1)S(1)}, u32[]{:S(2)}, u32[]{:S(2)}) collective-permute-start(bf16[128,768]{1,0:T(8,128)(2,1)S(1)} %collective-permute-done.25), channel_id=1, source_target_pairs={{0,8},{4,12},{8,0},{12,4},{1,9},{5,13},{9,1},{13,5},{2,10},{6,14},... | collective-permute-start | bytes 589832 | tf_op jit(solution)/shard_map/ppermute | solution.py:29
  86.4 13.5 %collective-permute-start.32 = (bf16[128,768]{1,0:T(8,128)(2,1)S(1)}, bf16[128,768]{1,0:T(8,128)(2,1)S(1)}, u32[]{:S(2)}, u32[]{:S(2)}) collective-permute-start(bf16[128,768]{1,0:T(8,128)(2,1)S(1)} %collective-permute-done.29), channel_id=1, source_target_pairs={{0,8},{4,12},{8,0},{12,4},{1,9},{5,13},{9,1},{13,5},{2,10},{6,14},... | collective-permute-start | bytes 589832 | tf_op jit(solution)/shard_map/ppermute | solution.py:29
  87.3 12.5 %collective-permute-start.33 = (bf16[256,768]{1,0:T(8,128)(2,1)S(1)}, bf16[256,768]{1,0:T(8,128)(2,1)S(1)}, u32[]{:S(2)}, u32[]{:S(2)}) collective-permute-start(bf16[256,768]{1,0:T(8,128)(2,1)S(1)} %get-tuple-element.127.mine_ref), channel_id=1, source_target_pairs={{0,4},{4,0},{8,12},{12,8},{1,5},{5,1},{9,13},{13,9},{2,6},{6,2},{1... | collective-permute-start | bytes 1179656 | tf_op jit(solution)/shard_map/ppermute | solution.py:29
  100.6 21.7 %collective-permute-start.34 = (bf16[256,768]{1,0:T(8,128)(2,1)}, bf16[256,768]{1,0:T(8,128)(2,1)}, u32[]{:S(2)}, u32[]{:S(2)}) collective-permute-start(bf16[256,768]{1,0:T(8,128)(2,1)} %get-tuple-element.136.refs_8_), channel_id=1, source_target_pairs={{0,8},{4,12},{8,0},{12,4},{1,9},{5,13},{9,1},{13,5},{2,10},{6,14},... | collective-permute-start | bytes 1179656 | tf_op jit(solution)/shard_map/ppermute | solution.py:29
  100.6 21.7 %collective-permute-start.35 = (bf16[256,768]{1,0:T(8,128)(2,1)}, bf16[256,768]{1,0:T(8,128)(2,1)}, u32[]{:S(2)}, u32[]{:S(2)}) collective-permute-start(bf16[256,768]{1,0:T(8,128)(2,1)} %get-tuple-element.137.refs_12_), channel_id=1, source_target_pairs={{0,8},{4,12},{8,0},{12,4},{1,9},{5,13},{9,1},{13,5},{2,10},{6,14},... | collective-permute-start | bytes 1179656 | tf_op jit(solution)/shard_map/ppermute | solution.py:29
  106.9 14.3 %all-to-all-start = ((f32[32,1,512]{2,1,0:T(1,128)}), f32[32,1,512]{2,1,0:T(1,128)}, u32[]{:S(2)}, u32[]{:S(2)}) async-start(f32[32,1,512]{2,1,0:T(1,128)} %copy-done.31), calls=%async_computation | async-start | bytes 131072 | tf_op jit(solution)/shard_map/all_to_all | solution.py:365
  130.8 11.7 %collective-permute-start.40 = (bf16[384,768]{1,0:T(8,128)(2,1)S(1)}, bf16[384,768]{1,0:T(8,128)(2,1)S(1)}, u32[]{:S(2)}, u32[]{:S(2)}) collective-permute-start(bf16[384,768]{1,0:T(8,128)(2,1)S(1)} %copy-done.4), channel_id=1, source_target_pairs={{0,4},{4,0},{8,12},{12,8},{1,5},{5,1},{9,13},{13,9},{2,6},{6,2},{1... | collective-permute-start | bytes 1769480 | tf_op jit(solution)/shard_map/ppermute | solution.py:29
  131.0 10.3 %collective-permute-start.45 = (bf16[256,768]{1,0:T(8,128)(2,1)S(1)}, bf16[256,768]{1,0:T(8,128)(2,1)S(1)}, u32[]{:S(2)}, u32[]{:S(2)}) collective-permute-start(bf16[256,768]{1,0:T(8,128)(2,1)S(1)} %multiply_convert_fusion.2.refs_0_.embed_ref), channel_id=1, source_target_pairs={{0,8},{4,12},{8,0},{12,4},{1,9},{5,13},{9,1},{13,5},{2,10},{6,14},... | collective-permute-start | bytes 1179656 | tf_op jit(solution)/shard_map/ppermute | solution.py:29
  131.0 11.6 %collective-permute-start.41 = (bf16[384,768]{1,0:T(8,128)(2,1)S(1)}, bf16[384,768]{1,0:T(8,128)(2,1)S(1)}, u32[]{:S(2)}, u32[]{:S(2)}) collective-permute-start(bf16[384,768]{1,0:T(8,128)(2,1)S(1)} %copy-done.11), channel_id=1, source_target_pairs={{0,4},{4,0},{8,12},{12,8},{1,5},{5,1},{9,13},{13,9},{2,6},{6,2},{1... | collective-permute-start | bytes 1769480 | tf_op jit(solution)/shard_map/ppermute | solution.py:29
  131.7 11.0 %collective-permute-start.42 = (bf16[384,768]{1,0:T(8,128)(2,1)S(1)}, bf16[384,768]{1,0:T(8,128)(2,1)S(1)}, u32[]{:S(2)}, u32[]{:S(2)}) collective-permute-start(bf16[384,768]{1,0:T(8,128)(2,1)S(1)} %copy-done.9), channel_id=1, source_target_pairs={{0,4},{4,0},{8,12},{12,8},{1,5},{5,1},{9,13},{13,9},{2,6},{6,2},{1... | collective-permute-start | bytes 1769480 | tf_op jit(solution)/shard_map/ppermute | solution.py:29
  131.7 10.9 %collective-permute-start.43 = (bf16[384,768]{1,0:T(8,128)(2,1)S(1)}, bf16[384,768]{1,0:T(8,128)(2,1)S(1)}, u32[]{:S(2)}, u32[]{:S(2)}) collective-permute-start(bf16[384,768]{1,0:T(8,128)(2,1)S(1)} %copy-done.13), channel_id=1, source_target_pairs={{0,4},{4,0},{8,12},{12,8},{1,5},{5,1},{9,13},{13,9},{2,6},{6,2},{1... | collective-permute-start | bytes 1769480 | tf_op jit(solution)/shard_map/ppermute | solution.py:29
  148.6 10.4 %collective-permute-start.47 = (bf16[256,768]{1,0:T(8,128)(2,1)S(1)}, bf16[256,768]{1,0:T(8,128)(2,1)S(1)}, u32[]{:S(2)}, u32[]{:S(2)}) collective-permute-start(bf16[256,768]{1,0:T(8,128)(2,1)S(1)} %copy-done.26), channel_id=1, source_target_pairs={{0,8},{4,12},{8,0},{12,4},{1,9},{5,13},{9,1},{13,5},{2,10},{6,14},... | collective-permute-start | bytes 1179656 | tf_op jit(solution)/shard_map/ppermute | solution.py:29
  148.6 16.0 %collective-permute-start.51 = (bf16[192,960]{1,0:T(8,128)(2,1)S(1)}, bf16[192,960]{1,0:T(8,128)(2,1)S(1)}, u32[]{:S(2)}, u32[]{:S(2)}) collective-permute-start(bf16[192,960]{1,0:T(8,128)(2,1)S(1)} %get-tuple-element.174), channel_id=1, source_target_pairs={{0,1},{1,2},{2,3},{3,0},{4,5},{5,6},{6,7},{7,4},{8,9},{9,10},{10,1... | collective-permute-start | bytes 1105928 | tf_op jit(solution)/shard_map/ppermute | solution.py:25
  149.2 33.1 %collective-permute-start.50 = (bf16[192,960]{1,0:T(8,128)(2,1)S(1)}, bf16[192,960]{1,0:T(8,128)(2,1)S(1)}, u32[]{:S(2)}, u32[]{:S(2)}) collective-permute-start(bf16[192,960]{1,0:T(8,128)(2,1)S(1)} %get-tuple-element.173), channel_id=1, source_target_pairs={{0,2},{1,3},{2,0},{3,1},{4,6},{5,7},{6,4},{7,5},{8,10},{9,11},{10,... | collective-permute-start | bytes 1105928 | tf_op jit(solution)/shard_map/ppermute | solution.py:25
  151.9 34.9 %collective-permute-start.49 = (bf16[192,960]{1,0:T(8,128)(2,1)S(1)}, bf16[192,960]{1,0:T(8,128)(2,1)S(1)}, u32[]{:S(2)}, u32[]{:S(2)}) collective-permute-start(bf16[192,960]{1,0:T(8,128)(2,1)S(1)} %get-tuple-element.172), channel_id=1, source_target_pairs={{0,3},{1,0},{2,1},{3,2},{4,7},{5,4},{6,5},{7,6},{8,11},{9,8},{10,9... | collective-permute-start | bytes 1105928 | tf_op jit(solution)/shard_map/ppermute | solution.py:25
  159.0 28.6 %collective-permute-start.48 = (bf16[256,768]{1,0:T(8,128)(2,1)S(1)}, bf16[256,768]{1,0:T(8,128)(2,1)S(1)}, u32[]{:S(2)}, u32[]{:S(2)}) collective-permute-start(bf16[256,768]{1,0:T(8,128)(2,1)S(1)} %collective-permute-done.47.refs_2_), channel_id=1, source_target_pairs={{0,4},{4,0},{8,12},{12,8},{1,5},{5,1},{9,13},{13,9},{2,6},{6,2},{1... | collective-permute-start | bytes 1179656 | tf_op jit(solution)/shard_map/ppermute | solution.py:29
  (65 other events, 547.0 us)

commit v5 on v4

--- a/solution.py
+++ b/solution.py
@@ -299,7 +299,7 @@
         pace = () if k == 1 else (down_ring[k - 1],)
         proj_ring.append(shift(after(proj_ring[-1], *pace), "gcol", 1))
     down_tables = [spread(part, far[0]) for part in down_ring]
-    active_even = {1: spread(active[1])}
+    active_even = {1: spread(after(active[1], down_tables[0][last]))}
     proj_own = jnp.roll(jnp.concatenate(proj_ring[::-1], 1), (gcol + 1) * columns, 1)
     proj_even = spread(proj_own)
     proj_pair = jnp.concatenate([proj_even[j] for j in evens], 0)
@@ -326,14 +326,14 @@
     unit = embed * inverse
     unit_b = unit.astype(BF16)
 
+    stream_blocks = [stream[:, i * features : (i + 1) * features] for i in range(len(evens))]
     (
-        unit, unit_b, inverse, stream, proj_pair, proj_mate, proj_all, down_pair, active, active_mate, preact, active_even
+        unit, unit_b, inverse, stream_blocks, proj_pair, proj_mate, proj_all, down_pair, active, active_mate, preact, active_even
     ) = lax.optimization_barrier(
-        (unit, unit_b, inverse, stream, proj_pair, proj_mate, proj_all, down_pair, active, active_mate, preact, active_even)
+        (unit, unit_b, inverse, stream_blocks, proj_pair, proj_mate, proj_all, down_pair, active, active_mate, preact, active_even)
     )
     far, core = (Lane(), Lane()), Lane()
 
-    stream_blocks = [stream[:, i * features : (i + 1) * features] for i in range(len(evens))]
     stream_even = {0: stream_blocks[0]}
     for i, j in enumerate(evens[1:], 1):
         stream_even[j] = swap(stream_blocks[i], "grow", j)

time: 190 us -> 187 us (0.984)
  waiting for transfers between devices: 80.2 us -> 78.2 us
    ppermute x35, waiting for transfers between devices: 47.6 us -> 41.9 us  [swap(): lax.ppermute(value, axis, [(i, i ^ bit) for i in range(lax.axis_size(axis...]
    ppermute x13, starting transfers between devices: 15.4 us -> 11.7 us  [shift(): lax.ppermute(value, axis, [(i, (i + step) % count) for i in range(count)])]
    ppermute x35, starting transfers between devices: 35 us -> 38.5 us  [swap(): lax.ppermute(value, axis, [(i, i ^ bit) for i in range(lax.axis_size(axis...]
    unnamed x102 -> x104, local copies, waits for them, and re-layouts: 10.5 us -> 10.5 us
  transfers between devices with their start and end apart: 53 -> 53, of which waited for: 22 -> 25; matrix products, arithmetic and copies ran while one was open for 11% -> 11% of each run, Pallas kernels for 6% -> 6%
where the time goes in v5:
time: 187 us
  waiting for transfers between devices  78.2 us (42%)
  starting transfers between devices  59.6 us (32%)
  local copies, waits for them, and re-layouts  16.3 us (9%)
  Pallas kernels  15.9 us (9%)
  matrix products  9.66 us (5%)
  other arithmetic  4.88 us (3%)
  between operations  2.2 us (1%)
    ppermute x35, waiting for transfers between devices, swap(): lax.ppermute(value, axis, [(i, i ^ bit) for i in range(lax.axis_size(axis...  41.9 us
    ppermute x35, starting transfers between devices, swap(): lax.ppermute(value, axis, [(i, i ^ bit) for i in range(lax.axis_size(axis...  38.5 us
    ppermute x13, waiting for transfers between devices, shift(): lax.ppermute(value, axis, [(i, (i + step) % count) for i in range(count)])  27.9 us
    pallas_call x7, Pallas kernels, call(): pl.pallas_call(kernel, out_shape=[jax.ShapeDtypeStruct(shape, dtype) for...  15.9 us
    ppermute x13, starting transfers between devices, shift(): lax.ppermute(value, axis, [(i, (i + step) % count) for i in range(count)])  11.7 us
    unnamed x104, local copies, waits for them, and re-layouts  10.5 us
    all_to_all x1, starting transfers between devices, body(): lse_all = lax.all_to_all(lse, ('tower', 'grow', 'gcol'), 0, 0)  6.26 us
    dot_general x3, matrix products, dot_nn(): return jnp.dot(left, right, preferred_element_type=F32)  5.06 us
  transfers between devices with their start and end apart: 53, of which 25 were waited for; matrix products, arithmetic and copies ran while one was open for 11% of the time, Pallas kernels for 6%

profile of v5, /device:TPU:9, one launch (start us, length us, event | category | flops | bytes accessed | tf_op | source)
XLA Modules:
  0.0 186.8 jit_solution(6057959390404878920)
XLA Ops:
  4.7 1.6 activate.1
  8.9 2.1 %dynamic-slice_bitcast_fusion.3 = (bf16[256,192]{1,0:T(8,128)(2,1)}, bf16[256,192]{1,0:T(8,128)(2,1)}, bf16[256,192]{1,0:T(8,128)(2,1)S(1)}, bf16[256,192]{1,0:T(8,128)(2,1)S(1)}) fusion(bf16[1,256,768]{2,1,0:T(8,128)(2,1)} %param.5, s32[]{:T(128)S(6)} %select_n.25, s32[]{:T(128)S(6)} %select_n.26, s32[]{:T(128)S(6)} %select_n.28, s32[]{:T(128)S(6)} %select_n.27), kind=kLoop, calls=%fused_computation.52 | loop fusion | bytes 786448 | tf_op jit(solution)/shard_map/dynamic_slice | solution.py:311
  15.5 2.4 %collective-permute-start.1 = (bf16[256,768]{1,0:T(8,128)(2,1)S(1)}, bf16[256,768]{1,0:T(8,128)(2,1)S(1)}, u32[]{:S(2)}, u32[]{:S(2)}) collective-permute-start(bf16[256,768]{1,0:T(8,128)(2,1)S(1)} %get-tuple-element.164.refs_4_), channel_id=1, source_target_pairs={{0,4},{4,0},{8,12},{12,8},{1,5},{5,1},{9,13},{13,9},{2,6},{6,2},{1... | collective-permute-start | bytes 1179656 | tf_op jit(solution)/shard_map/ppermute | solution.py:29
  22.1 2.7 %collective-permute-done.15 = bf16[192,192]{1,0:T(8,128)(2,1)} collective-permute-done((bf16[192,192]{1,0:T(8,128)(2,1)S(1)}, bf16[192,192]{1,0:T(8,128)(2,1)}, u32[]{:S(2)}, u32[]{:S(2)}) %collective-permute-start.15) | collective-permute-done | bytes 73760 | tf_op jit(solution)/shard_map/ppermute | solution.py:25
  27.9 4.3 %collective-permute-start.2 = (bf16[256,768]{1,0:T(8,128)(2,1)}, bf16[256,768]{1,0:T(8,128)(2,1)S(1)}, u32[]{:S(2)}, u32[]{:S(2)}) collective-permute-start(bf16[256,768]{1,0:T(8,128)(2,1)} %get-tuple-element.140.refs_8_), channel_id=1, source_target_pairs={{0,4},{4,0},{8,12},{12,8},{1,5},{5,1},{9,13},{13,9},{2,6},{6,2},{1... | collective-permute-start | bytes 1179656 | tf_op jit(solution)/shard_map/ppermute | solution.py:29
  36.0 4.0 %collective-permute-start.3 = (bf16[256,768]{1,0:T(8,128)(2,1)}, bf16[256,768]{1,0:T(8,128)(2,1)S(1)}, u32[]{:S(2)}, u32[]{:S(2)}) collective-permute-start(bf16[256,768]{1,0:T(8,128)(2,1)} %get-tuple-element.141.refs_12_), channel_id=1, source_target_pairs={{0,4},{4,0},{8,12},{12,8},{1,5},{5,1},{9,13},{13,9},{2,6},{6,2},{1... | collective-permute-start | bytes 1179656 | tf_op jit(solution)/shard_map/ppermute | solution.py:29
  40.2 2.5 %collective-permute-start.17 = (bf16[384,768]{1,0:T(8,128)(2,1)S(1)}, bf16[384,768]{1,0:T(8,128)(2,1)S(1)}, u32[]{:S(2)}, u32[]{:S(2)}) collective-permute-start(bf16[384,768]{1,0:T(8,128)(2,1)S(1)} %pad_maximum_fusion.2.proj_a), channel_id=1, source_target_pairs={{0,4},{4,0},{8,12},{12,8},{1,5},{5,1},{9,13},{13,9},{2,6},{6,2},{1... | collective-permute-start | bytes 1769480 | tf_op jit(solution)/shard_map/ppermute | solution.py:29
  42.7 3.8 %collective-permute-done.11 = bf16[192,768]{1,0:T(8,128)(2,1)S(1)} collective-permute-done((bf16[192,768]{1,0:T(8,128)(2,1)}, bf16[192,768]{1,0:T(8,128)(2,1)S(1)}, u32[]{:S(2)}, u32[]{:S(2)}) %collective-permute-start.11) | collective-permute-done | bytes 294944 | tf_op jit(solution)/shard_map/ppermute | solution.py:29
  46.6 1.8 fusion.16
  49.9 1.6 fusion.20
  59.2 3.6 %collective-permute-done.19 = bf16[128,768]{1,0:T(8,128)(2,1)S(1)} collective-permute-done((bf16[128,768]{1,0:T(8,128)(2,1)S(1)}, bf16[128,768]{1,0:T(8,128)(2,1)S(1)}, u32[]{:S(2)}, u32[]{:S(2)}) %collective-permute-start.19) | collective-permute-done | bytes 196640 | tf_op jit(solution)/shard_map/ppermute | solution.py:47
  68.4 3.9 %collective-permute-done.27 = bf16[256,768]{1,0:T(8,128)(2,1)S(1)} collective-permute-done((bf16[256,768]{1,0:T(8,128)(2,1)S(1)}, bf16[256,768]{1,0:T(8,128)(2,1)S(1)}, u32[]{:S(2)}, u32[]{:S(2)}) %collective-permute-start.27) | collective-permute-done | bytes 393248 | tf_op jit(solution)/shard_map/ppermute | solution.py:29
  74.8 2.2 %collective-permute-start.29 = (bf16[128,768]{1,0:T(8,128)(2,1)S(1)}, bf16[128,768]{1,0:T(8,128)(2,1)S(1)}, u32[]{:S(2)}, u32[]{:S(2)}) collective-permute-start(bf16[128,768]{1,0:T(8,128)(2,1)S(1)} %collective-permute-done.24), channel_id=1, source_target_pairs={{0,1},{1,2},{2,3},{3,0},{4,5},{5,6},{6,7},{7,4},{8,9},{9,10},{10,1... | collective-permute-start | bytes 589832 | tf_op jit(solution)/shard_map/ppermute | solution.py:25
  77.1 3.6 %collective-permute-done.26 = bf16[256,768]{1,0:T(8,128)(2,1)S(1)} collective-permute-done((bf16[256,768]{1,0:T(8,128)(2,1)S(1)}, bf16[256,768]{1,0:T(8,128)(2,1)S(1)}, u32[]{:S(2)}, u32[]{:S(2)}) %collective-permute-start.26) | collective-permute-done | bytes 393248 | tf_op jit(solution)/shard_map/ppermute | solution.py:29
  80.8 1.9 %collective-permute-done.28 = bf16[256,768]{1,0:T(8,128)(2,1)S(1)} collective-permute-done((bf16[256,768]{1,0:T(8,128)(2,1)S(1)}, bf16[256,768]{1,0:T(8,128)(2,1)S(1)}, u32[]{:S(2)}, u32[]{:S(2)}) %collective-permute-start.28) | collective-permute-done | bytes 393248 | tf_op jit(solution)/shard_map/ppermute | solution.py:52
  83.4 1.9 collective-permute-done.29
  85.3 3.8 %collective-permute-start.33 = (bf16[256,768]{1,0:T(8,128)(2,1)S(1)}, bf16[256,768]{1,0:T(8,128)(2,1)S(1)}, u32[]{:S(2)}, u32[]{:S(2)}) collective-permute-start(bf16[256,768]{1,0:T(8,128)(2,1)S(1)} %get-tuple-element.131.mine_ref), channel_id=1, source_target_pairs={{0,4},{4,0},{8,12},{12,8},{1,5},{5,1},{9,13},{13,9},{2,6},{6,2},{1... | collective-permute-start | bytes 1179656 | tf_op jit(solution)/shard_map/ppermute | solution.py:29
  89.2 4.2 %collective-permute-done.31 = bf16[128,768]{1,0:T(8,128)(2,1)S(1)} collective-permute-done((bf16[128,768]{1,0:T(8,128)(2,1)S(1)}, bf16[128,768]{1,0:T(8,128)(2,1)S(1)}, u32[]{:S(2)}, u32[]{:S(2)}) %collective-permute-start.31) | collective-permute-done | bytes 196640 | tf_op jit(solution)/shard_map/ppermute | solution.py:29
  93.4 4.2 %collective-permute-done.32 = bf16[128,768]{1,0:T(8,128)(2,1)S(1)} collective-permute-done((bf16[128,768]{1,0:T(8,128)(2,1)S(1)}, bf16[128,768]{1,0:T(8,128)(2,1)S(1)}, u32[]{:S(2)}, u32[]{:S(2)}) %collective-permute-start.32) | collective-permute-done | bytes 196640 | tf_op jit(solution)/shard_map/ppermute | solution.py:29
  101.5 2.4 %scores.1 = f32[32,1,512]{2,1,0:T(1,128)S(1)} custom-call(f32[1,1]{1,0:T(1,128)} %bitcast.17.scale_ref, bf16[256,768]{1,0:T(8,128)(2,1)S(1)} %get-tuple-element.131.mine_ref, bf16[256,768]{1,0:T(8,128)(2,1)S(1)} %copy-done.6, bf16[2048,768]{1,0:T(8,128)(2,1)S(1)} %constant_dynamic-update-slice_fusion.6.others_ref), custom_call_target="tpu_custom_call" | custom-call | flops 1 | bytes 1 | tf_op jit(solution)/shard_map/scores/pallas_call | solution.py:106
  104.6 6.3 %all-to-all-start = ((f32[32,1,512]{2,1,0:T(1,128)}), f32[32,1,512]{2,1,0:T(1,128)}, u32[]{:S(2)}, u32[]{:S(2)}) async-start(f32[32,1,512]{2,1,0:T(1,128)} %copy-done.31), calls=%async_computation | async-start | bytes 131072 | tf_op jit(solution)/shard_map/all_to_all | solution.py:365
  112.0 1.8 values.1
  116.9 2.0 %all-to-all-done.lse_ref = f32[32,1,512]{2,1,0:T(1,128)} async-done(((f32[32,1,512]{2,1,0:T(1,128)}), f32[32,1,512]{2,1,0:T(1,128)}, u32[]{:S(2)}, u32[]{:S(2)}) %all-to-all-start) | async-done | bytes 65568 | tf_op jit(solution)/shard_map/all_to_all | solution.py:365
  120.1 3.1 %convolution_multiply_fusion.1 = f32[256,768]{1,0:T(8,128)S(1)} fusion(bf16[2048,768]{1,0:T(8,128)(2,1)S(1)} %constant_dynamic-update-slice_fusion.6.others_ref, f32[256,2048]{1,0:T(8,128)} %copy-done.34, f32[2048]{0:T(1024)S(1)} %bitcast.54, f32[256]{0:T(256)S(1)} %get-tuple-element.191, f32[]{:T(128)} %exp.15), kind=kOutput, calls=%fused_computation.4 | convolution fusion | flops 808124416 | bytes 6038532 | tf_op jit(solution)/shard_map/dot_general | solution.py:97
  123.8 2.6 %collective-permute-done.38.refs_11_ = bf16[256,768]{1,0:T(8,128)(2,1)S(1)} collective-permute-done((bf16[256,768]{1,0:T(8,128)(2,1)}, bf16[256,768]{1,0:T(8,128)(2,1)S(1)}, u32[]{:S(2)}, u32[]{:S(2)}) %collective-permute-start.38) | collective-permute-done | bytes 393248 | tf_op jit(solution)/shard_map/ppermute | solution.py:29
  131.2 7.9 %collective-permute-done.45.refs_2_ = bf16[256,768]{1,0:T(8,128)(2,1)S(1)} collective-permute-done((bf16[256,768]{1,0:T(8,128)(2,1)S(1)}, bf16[256,768]{1,0:T(8,128)(2,1)S(1)}, u32[]{:S(2)}, u32[]{:S(2)}) %collective-permute-start.45) | collective-permute-done | bytes 393248 | tf_op jit(solution)/shard_map/ppermute | solution.py:29
  142.2 4.0 %terms.1 = (bf16[192,960]{1,0:T(8,128)(2,1)S(1)}, bf16[192,960]{1,0:T(8,128)(2,1)S(1)}, bf16[192,960]{1,0:T(8,128)(2,1)S(1)}, f32[192,192]{1,0:T(8,128)S(1)}, bf16[192,1024]{1,0:T(8,128)(2,1)S(1)}) custom-call(s32[4]{0:T(128)S(1)} %get-tuple-element.97.places_ref, bf16[192,768]{1,0:T(8,128)(2,1)S(1)} %slice.45.proj_ref, ...), custom_call_target="tpu_custom_call" | custom-call | flops 1 | bytes 1 | tf_op jit(solution)/shard_map/terms/pallas_call | solution.py:106
  147.9 1.7 collective-permute-start.50
  151.0 5.7 %collective-permute-done.47.refs_2_ = bf16[256,768]{1,0:T(8,128)(2,1)S(1)} collective-permute-done((bf16[256,768]{1,0:T(8,128)(2,1)S(1)}, bf16[256,768]{1,0:T(8,128)(2,1)S(1)}, u32[]{:S(2)}, u32[]{:S(2)}) %collective-permute-start.47) | collective-permute-done | bytes 393248 | tf_op jit(solution)/shard_map/ppermute | solution.py:29
  157.9 4.5 %own_gradients.1 = (bf16[256,768]{1,0:T(8,128)(2,1)}, bf16[256,3072]{1,0:T(8,128)(2,1)}) custom-call(s32[4]{0:T(128)S(1)} %get-tuple-element.97.places_ref, s32[4]{0:T(128)S(1)} %get-tuple-element.98.found_ref, bf16[256,3072]{1,0:T(8,128)(2,1)S(1)} %bitcast.53, bf16[256,768]{1,0:T(8,128)(2,1)S(1)} %multiply_convert_fusion.2.refs_0_.embed_ref, ...), custom_call_target="tpu_custom_call" | custom-call | flops 1 | bytes 1 | tf_op jit(solution)/shard_map/own_gradients/pallas_call | solution.py:106
  162.4 18.6 %collective-permute-done.50 = bf16[192,960]{1,0:T(8,128)(2,1)S(1)} collective-permute-done((bf16[192,960]{1,0:T(8,128)(2,1)S(1)}, bf16[192,960]{1,0:T(8,128)(2,1)S(1)}, u32[]{:S(2)}, u32[]{:S(2)}) %collective-permute-start.50) | collective-permute-done | bytes 368672 | tf_op jit(solution)/shard_map/ppermute | solution.py:25
  181.0 3.6 %collective-permute-done.49 = bf16[192,960]{1,0:T(8,128)(2,1)S(1)} collective-permute-done((bf16[192,960]{1,0:T(8,128)(2,1)S(1)}, bf16[192,960]{1,0:T(8,128)(2,1)S(1)}, u32[]{:S(2)}, u32[]{:S(2)}) %collective-permute-start.49) | collective-permute-done | bytes 368672 | tf_op jit(solution)/shard_map/ppermute | solution.py:25
  (217 shorter events, 64.1 us)
Async XLA Ops:
  0.6 10.4 %collective-permute-start.6 = (bf16[192,768]{1,0:T(8,128)(2,1)}, bf16[192,768]{1,0:T(8,128)(2,1)S(1)}, u32[]{:S(2)}, u32[]{:S(2)}) collective-permute-start(bf16[192,768]{1,0:T(8,128)(2,1)} %bitcast.59), channel_id=1, source_target_pairs={{0,1},{1,2},{2,3},{3,0},{4,5},{5,6},{6,7},{7,4},{8,9},{9,10},{10,1... | collective-permute-start | bytes 884744 | tf_op jit(solution)/shard_map/ppermute | solution.py:25
  6.3 9.1 %collective-permute-start = (bf16[256,768]{1,0:T(8,128)(2,1)S(1)}, bf16[256,768]{1,0:T(8,128)(2,1)S(1)}, u32[]{:S(2)}, u32[]{:S(2)}) collective-permute-start(bf16[256,768]{1,0:T(8,128)(2,1)S(1)} %get-tuple-element.186.refs_0_), channel_id=1, source_target_pairs={{0,4},{4,0},{8,12},{12,8},{1,5},{5,1},{9,13},{13,9},{2,6},{6,2},{1... | collective-permute-start | bytes 1179656 | tf_op jit(solution)/shard_map/ppermute | solution.py:29
  13.4 40.9 %collective-permute-start.18 = (bf16[256,768]{1,0:T(8,128)(2,1)S(1)}, bf16[256,768]{1,0:T(8,128)(2,1)}, u32[]{:S(2)}, u32[]{:S(2)}) collective-permute-start(bf16[256,768]{1,0:T(8,128)(2,1)S(1)} %get-tuple-element.164.refs_4_), channel_id=1, source_target_pairs={{0,8},{4,12},{8,0},{12,4},{1,9},{5,13},{9,1},{13,5},{2,10},{6,14},... | collective-permute-start | bytes 1179656 | tf_op jit(solution)/shard_map/ppermute | solution.py:29
  15.5 12.5 %collective-permute-start.1 = (bf16[256,768]{1,0:T(8,128)(2,1)S(1)}, bf16[256,768]{1,0:T(8,128)(2,1)S(1)}, u32[]{:S(2)}, u32[]{:S(2)}) collective-permute-start(bf16[256,768]{1,0:T(8,128)(2,1)S(1)} %get-tuple-element.164.refs_4_), channel_id=1, source_target_pairs={{0,4},{4,0},{8,12},{12,8},{1,5},{5,1},{9,13},{13,9},{2,6},{6,2},{1... | collective-permute-start | bytes 1179656 | tf_op jit(solution)/shard_map/ppermute | solution.py:29
  19.2 14.7 %collective-permute-start.9 = (bf16[192,768]{1,0:T(8,128)(2,1)}, bf16[192,768]{1,0:T(8,128)(2,1)}, u32[]{:S(2)}, u32[]{:S(2)}) collective-permute-start(bf16[192,768]{1,0:T(8,128)(2,1)} %collective-permute-done.8), channel_id=1, source_target_pairs={{0,8},{4,12},{8,0},{12,4},{1,9},{5,13},{9,1},{13,5},{2,10},{6,14},... | collective-permute-start | bytes 884744 | tf_op jit(solution)/shard_map/ppermute | solution.py:29
  20.9 12.0 %collective-permute-start.10 = (bf16[192,768]{1,0:T(8,128)(2,1)}, bf16[192,768]{1,0:T(8,128)(2,1)}, u32[]{:S(2)}, u32[]{:S(2)}) collective-permute-start(bf16[192,768]{1,0:T(8,128)(2,1)} %collective-permute-done.8), channel_id=1, source_target_pairs={{0,1},{1,2},{2,3},{3,0},{4,5},{5,6},{6,7},{7,4},{8,9},{9,10},{10,1... | collective-permute-start | bytes 884744 | tf_op jit(solution)/shard_map/ppermute | solution.py:25
  26.4 13.8 %collective-permute-start.16 = (bf16[192,768]{1,0:T(8,128)(2,1)S(1)}, bf16[192,768]{1,0:T(8,128)(2,1)S(1)}, u32[]{:S(2)}, u32[]{:S(2)}) collective-permute-start(bf16[192,768]{1,0:T(8,128)(2,1)S(1)} %constant_dynamic-slice_fusion), channel_id=1, source_target_pairs={{0,8},{4,12},{8,0},{12,4},{1,9},{5,13},{9,1},{13,5},{2,10},{6,14},... | collective-permute-start | bytes 884744 | tf_op jit(solution)/shard_map/ppermute | solution.py:29
  34.0 12.5 %collective-permute-start.11 = (bf16[192,768]{1,0:T(8,128)(2,1)}, bf16[192,768]{1,0:T(8,128)(2,1)S(1)}, u32[]{:S(2)}, u32[]{:S(2)}) collective-permute-start(bf16[192,768]{1,0:T(8,128)(2,1)} %collective-permute-done.10), channel_id=1, source_target_pairs={{0,8},{4,12},{8,0},{12,4},{1,9},{5,13},{9,1},{13,5},{2,10},{6,14},... | collective-permute-start | bytes 884744 | tf_op jit(solution)/shard_map/ppermute | solution.py:29
  36.0 12.4 %collective-permute-start.3 = (bf16[256,768]{1,0:T(8,128)(2,1)}, bf16[256,768]{1,0:T(8,128)(2,1)S(1)}, u32[]{:S(2)}, u32[]{:S(2)}) collective-permute-start(bf16[256,768]{1,0:T(8,128)(2,1)} %get-tuple-element.141.refs_12_), channel_id=1, source_target_pairs={{0,4},{4,0},{8,12},{12,8},{1,5},{5,1},{9,13},{13,9},{2,6},{6,2},{1... | collective-permute-start | bytes 1179656 | tf_op jit(solution)/shard_map/ppermute | solution.py:29
  40.2 13.0 %collective-permute-start.17 = (bf16[384,768]{1,0:T(8,128)(2,1)S(1)}, bf16[384,768]{1,0:T(8,128)(2,1)S(1)}, u32[]{:S(2)}, u32[]{:S(2)}) collective-permute-start(bf16[384,768]{1,0:T(8,128)(2,1)S(1)} %pad_maximum_fusion.2.proj_a), channel_id=1, source_target_pairs={{0,4},{4,0},{8,12},{12,8},{1,5},{5,1},{9,13},{13,9},{2,6},{6,2},{1... | collective-permute-start | bytes 1769480 | tf_op jit(solution)/shard_map/ppermute | solution.py:29
  57.7 14.6 %collective-permute-start.27 = (bf16[256,768]{1,0:T(8,128)(2,1)S(1)}, bf16[256,768]{1,0:T(8,128)(2,1)S(1)}, u32[]{:S(2)}, u32[]{:S(2)}) collective-permute-start(bf16[256,768]{1,0:T(8,128)(2,1)S(1)} %get-tuple-element.131.mine_ref), channel_id=1, source_target_pairs={{0,8},{4,12},{8,0},{12,4},{1,9},{5,13},{9,1},{13,5},{2,10},{6,14},... | collective-permute-start | bytes 1179656 | tf_op jit(solution)/shard_map/ppermute | solution.py:29
  64.6 10.2 %collective-permute-start.21 = (bf16[256,768]{1,0:T(8,128)(2,1)S(1)}, bf16[256,768]{1,0:T(8,128)(2,1)S(1)}, u32[]{:S(2)}, u32[]{:S(2)}) collective-permute-start(bf16[256,768]{1,0:T(8,128)(2,1)S(1)} %get-tuple-element.131.mine_ref), channel_id=1, source_target_pairs={{0,16},{16,0},{1,17},{17,1},{2,18},{18,2},{3,19},{19,3},{4,20},{20... | collective-permute-start | bytes 1179656 | tf_op jit(solution)/shard_map/ppermute | solution.py:52
  67.4 13.3 %collective-permute-start.26 = (bf16[256,768]{1,0:T(8,128)(2,1)S(1)}, bf16[256,768]{1,0:T(8,128)(2,1)S(1)}, u32[]{:S(2)}, u32[]{:S(2)}) collective-permute-start(bf16[256,768]{1,0:T(8,128)(2,1)S(1)} %pad_maximum_fusion.3), channel_id=1, source_target_pairs={{0,8},{4,12},{8,0},{12,4},{1,9},{5,13},{9,1},{13,5},{2,10},{6,14},... | collective-permute-start | bytes 1179656 | tf_op jit(solution)/shard_map/ppermute | solution.py:29
  72.3 10.3 %collective-permute-start.28 = (bf16[256,768]{1,0:T(8,128)(2,1)S(1)}, bf16[256,768]{1,0:T(8,128)(2,1)S(1)}, u32[]{:S(2)}, u32[]{:S(2)}) collective-permute-start(bf16[256,768]{1,0:T(8,128)(2,1)S(1)} %collective-permute-done.27), channel_id=1, source_target_pairs={{0,16},{16,0},{1,17},{17,1},{2,18},{18,2},{3,19},{19,3},{4,20},{20... | collective-permute-start | bytes 1179656 | tf_op jit(solution)/shard_map/ppermute | solution.py:52
  73.7 15.4 %collective-permute-start.30 = (bf16[256,768]{1,0:T(8,128)(2,1)S(1)}, bf16[256,768]{1,0:T(8,128)(2,1)S(1)}, u32[]{:S(2)}, u32[]{:S(2)}) collective-permute-start(bf16[256,768]{1,0:T(8,128)(2,1)S(1)} %pad_maximum_fusion.4), channel_id=1, source_target_pairs={{0,8},{4,12},{8,0},{12,4},{1,9},{5,13},{9,1},{13,5},{2,10},{6,14},... | collective-permute-start | bytes 1179656 | tf_op jit(solution)/shard_map/ppermute | solution.py:29
  74.8 10.4 %collective-permute-start.29 = (bf16[128,768]{1,0:T(8,128)(2,1)S(1)}, bf16[128,768]{1,0:T(8,128)(2,1)S(1)}, u32[]{:S(2)}, u32[]{:S(2)}) collective-permute-start(bf16[128,768]{1,0:T(8,128)(2,1)S(1)} %collective-permute-done.24), channel_id=1, source_target_pairs={{0,1},{1,2},{2,3},{3,0},{4,5},{5,6},{6,7},{7,4},{8,9},{9,10},{10,1... | collective-permute-start | bytes 589832 | tf_op jit(solution)/shard_map/ppermute | solution.py:25
  82.7 10.7 %collective-permute-start.31 = (bf16[128,768]{1,0:T(8,128)(2,1)S(1)}, bf16[128,768]{1,0:T(8,128)(2,1)S(1)}, u32[]{:S(2)}, u32[]{:S(2)}) collective-permute-start(bf16[128,768]{1,0:T(8,128)(2,1)S(1)} %collective-permute-done.25), channel_id=1, source_target_pairs={{0,8},{4,12},{8,0},{12,4},{1,9},{5,13},{9,1},{13,5},{2,10},{6,14},... | collective-permute-start | bytes 589832 | tf_op jit(solution)/shard_map/ppermute | solution.py:29
  85.3 12.3 %collective-permute-start.32 = (bf16[128,768]{1,0:T(8,128)(2,1)S(1)}, bf16[128,768]{1,0:T(8,128)(2,1)S(1)}, u32[]{:S(2)}, u32[]{:S(2)}) collective-permute-start(bf16[128,768]{1,0:T(8,128)(2,1)S(1)} %collective-permute-done.29), channel_id=1, source_target_pairs={{0,8},{4,12},{8,0},{12,4},{1,9},{5,13},{9,1},{13,5},{2,10},{6,14},... | collective-permute-start | bytes 589832 | tf_op jit(solution)/shard_map/ppermute | solution.py:29
  85.3 12.4 %collective-permute-start.33 = (bf16[256,768]{1,0:T(8,128)(2,1)S(1)}, bf16[256,768]{1,0:T(8,128)(2,1)S(1)}, u32[]{:S(2)}, u32[]{:S(2)}) collective-permute-start(bf16[256,768]{1,0:T(8,128)(2,1)S(1)} %get-tuple-element.131.mine_ref), channel_id=1, source_target_pairs={{0,4},{4,0},{8,12},{12,8},{1,5},{5,1},{9,13},{13,9},{2,6},{6,2},{1... | collective-permute-start | bytes 1179656 | tf_op jit(solution)/shard_map/ppermute | solution.py:29
  98.4 21.7 %collective-permute-start.34 = (bf16[256,768]{1,0:T(8,128)(2,1)}, bf16[256,768]{1,0:T(8,128)(2,1)}, u32[]{:S(2)}, u32[]{:S(2)}) collective-permute-start(bf16[256,768]{1,0:T(8,128)(2,1)} %get-tuple-element.140.refs_8_), channel_id=1, source_target_pairs={{0,8},{4,12},{8,0},{12,4},{1,9},{5,13},{9,1},{13,5},{2,10},{6,14},... | collective-permute-start | bytes 1179656 | tf_op jit(solution)/shard_map/ppermute | solution.py:29
  99.6 20.5 %collective-permute-start.35 = (bf16[256,768]{1,0:T(8,128)(2,1)}, bf16[256,768]{1,0:T(8,128)(2,1)}, u32[]{:S(2)}, u32[]{:S(2)}) collective-permute-start(bf16[256,768]{1,0:T(8,128)(2,1)} %get-tuple-element.141.refs_12_), channel_id=1, source_target_pairs={{0,8},{4,12},{8,0},{12,4},{1,9},{5,13},{9,1},{13,5},{2,10},{6,14},... | collective-permute-start | bytes 1179656 | tf_op jit(solution)/shard_map/ppermute | solution.py:29
  104.6 14.3 %all-to-all-start = ((f32[32,1,512]{2,1,0:T(1,128)}), f32[32,1,512]{2,1,0:T(1,128)}, u32[]{:S(2)}, u32[]{:S(2)}) async-start(f32[32,1,512]{2,1,0:T(1,128)} %copy-done.31), calls=%async_computation | async-start | bytes 131072 | tf_op jit(solution)/shard_map/all_to_all | solution.py:365
  128.5 11.7 %collective-permute-start.40 = (bf16[384,768]{1,0:T(8,128)(2,1)S(1)}, bf16[384,768]{1,0:T(8,128)(2,1)S(1)}, u32[]{:S(2)}, u32[]{:S(2)}) collective-permute-start(bf16[384,768]{1,0:T(8,128)(2,1)S(1)} %copy-done.4), channel_id=1, source_target_pairs={{0,4},{4,0},{8,12},{12,8},{1,5},{5,1},{9,13},{13,9},{2,6},{6,2},{1... | collective-permute-start | bytes 1769480 | tf_op jit(solution)/shard_map/ppermute | solution.py:29
  128.8 10.3 %collective-permute-start.45 = (bf16[256,768]{1,0:T(8,128)(2,1)S(1)}, bf16[256,768]{1,0:T(8,128)(2,1)S(1)}, u32[]{:S(2)}, u32[]{:S(2)}) collective-permute-start(bf16[256,768]{1,0:T(8,128)(2,1)S(1)} %multiply_convert_fusion.2.refs_0_.embed_ref), channel_id=1, source_target_pairs={{0,8},{4,12},{8,0},{12,4},{1,9},{5,13},{9,1},{13,5},{2,10},{6,14},... | collective-permute-start | bytes 1179656 | tf_op jit(solution)/shard_map/ppermute | solution.py:29
  130.0 10.4 %collective-permute-start.41 = (bf16[384,768]{1,0:T(8,128)(2,1)S(1)}, bf16[384,768]{1,0:T(8,128)(2,1)S(1)}, u32[]{:S(2)}, u32[]{:S(2)}) collective-permute-start(bf16[384,768]{1,0:T(8,128)(2,1)S(1)} %copy-done.11), channel_id=1, source_target_pairs={{0,4},{4,0},{8,12},{12,8},{1,5},{5,1},{9,13},{13,9},{2,6},{6,2},{1... | collective-permute-start | bytes 1769480 | tf_op jit(solution)/shard_map/ppermute | solution.py:29
  130.7 9.7 %collective-permute-start.42 = (bf16[384,768]{1,0:T(8,128)(2,1)S(1)}, bf16[384,768]{1,0:T(8,128)(2,1)S(1)}, u32[]{:S(2)}, u32[]{:S(2)}) collective-permute-start(bf16[384,768]{1,0:T(8,128)(2,1)S(1)} %copy-done.9), channel_id=1, source_target_pairs={{0,4},{4,0},{8,12},{12,8},{1,5},{5,1},{9,13},{13,9},{2,6},{6,2},{1... | collective-permute-start | bytes 1769480 | tf_op jit(solution)/shard_map/ppermute | solution.py:29
  130.7 9.6 %collective-permute-start.43 = (bf16[384,768]{1,0:T(8,128)(2,1)S(1)}, bf16[384,768]{1,0:T(8,128)(2,1)S(1)}, u32[]{:S(2)}, u32[]{:S(2)}) collective-permute-start(bf16[384,768]{1,0:T(8,128)(2,1)S(1)} %copy-done.13), channel_id=1, source_target_pairs={{0,4},{4,0},{8,12},{12,8},{1,5},{5,1},{9,13},{13,9},{2,6},{6,2},{1... | collective-permute-start | bytes 1769480 | tf_op jit(solution)/shard_map/ppermute | solution.py:29
  146.3 10.4 %collective-permute-start.47 = (bf16[256,768]{1,0:T(8,128)(2,1)S(1)}, bf16[256,768]{1,0:T(8,128)(2,1)S(1)}, u32[]{:S(2)}, u32[]{:S(2)}) collective-permute-start(bf16[256,768]{1,0:T(8,128)(2,1)S(1)} %copy-done.26), channel_id=1, source_target_pairs={{0,8},{4,12},{8,0},{12,4},{1,9},{5,13},{9,1},{13,5},{2,10},{6,14},... | collective-permute-start | bytes 1179656 | tf_op jit(solution)/shard_map/ppermute | solution.py:29
  147.6 14.8 %collective-permute-start.51 = (bf16[192,960]{1,0:T(8,128)(2,1)S(1)}, bf16[192,960]{1,0:T(8,128)(2,1)S(1)}, u32[]{:S(2)}, u32[]{:S(2)}) collective-permute-start(bf16[192,960]{1,0:T(8,128)(2,1)S(1)} %get-tuple-element.178), channel_id=1, source_target_pairs={{0,1},{1,2},{2,3},{3,0},{4,5},{5,6},{6,7},{7,4},{8,9},{9,10},{10,1... | collective-permute-start | bytes 1105928 | tf_op jit(solution)/shard_map/ppermute | solution.py:25
  147.9 33.1 %collective-permute-start.50 = (bf16[192,960]{1,0:T(8,128)(2,1)S(1)}, bf16[192,960]{1,0:T(8,128)(2,1)S(1)}, u32[]{:S(2)}, u32[]{:S(2)}) collective-permute-start(bf16[192,960]{1,0:T(8,128)(2,1)S(1)} %get-tuple-element.177), channel_id=1, source_target_pairs={{0,2},{1,3},{2,0},{3,1},{4,6},{5,7},{6,4},{7,5},{8,10},{9,11},{10,... | collective-permute-start | bytes 1105928 | tf_op jit(solution)/shard_map/ppermute | solution.py:25
  149.6 34.9 %collective-permute-start.49 = (bf16[192,960]{1,0:T(8,128)(2,1)S(1)}, bf16[192,960]{1,0:T(8,128)(2,1)S(1)}, u32[]{:S(2)}, u32[]{:S(2)}) collective-permute-start(bf16[192,960]{1,0:T(8,128)(2,1)S(1)} %get-tuple-element.176), channel_id=1, source_target_pairs={{0,3},{1,0},{2,1},{3,2},{4,7},{5,4},{6,5},{7,6},{8,11},{9,8},{10,9... | collective-permute-start | bytes 1105928 | tf_op jit(solution)/shard_map/ppermute | solution.py:25
  156.7 28.6 %collective-permute-start.48 = (bf16[256,768]{1,0:T(8,128)(2,1)S(1)}, bf16[256,768]{1,0:T(8,128)(2,1)S(1)}, u32[]{:S(2)}, u32[]{:S(2)}) collective-permute-start(bf16[256,768]{1,0:T(8,128)(2,1)S(1)} %collective-permute-done.47.refs_2_), channel_id=1, source_target_pairs={{0,4},{4,0},{8,12},{12,8},{1,5},{5,1},{9,13},{13,9},{2,6},{6,2},{1... | collective-permute-start | bytes 1179656 | tf_op jit(solution)/shard_map/ppermute | solution.py:29
  (66 other events, 565.7 us)

commit v6 on v5

--- a/solution.py
+++ b/solution.py
@@ -345,7 +345,7 @@
     for hop in hops:
         blocks = [None, hop]
         for k in ks[2:]:
-            pace = (across,) if k == 3 else ()
+            pace = ()
             blocks.append(shift(after(blocks[-1], *pace), "gcol", 1))
         rings.append(blocks)
     unit_mate = swap(after(unit_b, rings[0][-1]), "grow", 1)

time: 187 us -> 187 us (level)
    ppermute x35, waiting for transfers between devices: 41.9 us -> 43.9 us  [swap(): lax.ppermute(value, axis, [(i, i ^ bit) for i in range(lax.axis_size(axis...]
    ppermute x2, waiting for transfers between devices: 1.92 us -> 0.01 us  [swap_across(): lax.ppermute(value, 'tower', [(t, towers - 1 - t) for t in range(towers)])]
  transfers between devices with their start and end apart: 53 -> 53, of which waited for: 25 -> 23; matrix products, arithmetic and copies ran while one was open for 11% -> 11% of each run, Pallas kernels for 6% -> 6%
where the time goes in v6:
time: 187 us
  waiting for transfers between devices  77.9 us (42%)
  starting transfers between devices  60 us (32%)
  local copies, waits for them, and re-layouts  16.3 us (9%)
  Pallas kernels  15.9 us (9%)
  matrix products  9.66 us (5%)
  other arithmetic  4.88 us (3%)
  between operations  2.21 us (1%)
    ppermute x35, waiting for transfers between devices, swap(): lax.ppermute(value, axis, [(i, i ^ bit) for i in range(lax.axis_size(axis...  43.9 us
    ppermute x35, starting transfers between devices, swap(): lax.ppermute(value, axis, [(i, i ^ bit) for i in range(lax.axis_size(axis...  40 us
    ppermute x13, waiting for transfers between devices, shift(): lax.ppermute(value, axis, [(i, (i + step) % count) for i in range(count)])  27.4 us
    pallas_call x7, Pallas kernels, call(): pl.pallas_call(kernel, out_shape=[jax.ShapeDtypeStruct(shape, dtype) for...  15.9 us
    unnamed x104, local copies, waits for them, and re-layouts  10.5 us
    ppermute x13, starting transfers between devices, shift(): lax.ppermute(value, axis, [(i, (i + step) % count) for i in range(count)])  10.5 us
    all_to_all x1, starting transfers between devices, body(): lse_all = lax.all_to_all(lse, ('tower', 'grow', 'gcol'), 0, 0)  6.3 us
    dot_general x3, matrix products, dot_nn(): return jnp.dot(left, right, preferred_element_type=F32)  5.06 us
  transfers between devices with their start and end apart: 53, of which 23 were waited for; matrix products, arithmetic and copies ran while one was open for 11% of the time, Pallas kernels for 6%

profile of v6, /device:TPU:9, one launch (start us, length us, event | category | flops | bytes accessed | tf_op | source)
XLA Modules:
  0.0 186.8 jit_solution(3976132375298742836)
XLA Ops:
  4.7 1.6 activate.1
  8.9 2.1 %dynamic-slice_bitcast_fusion.3 = (bf16[256,192]{1,0:T(8,128)(2,1)}, bf16[256,192]{1,0:T(8,128)(2,1)}, bf16[256,192]{1,0:T(8,128)(2,1)S(1)}, bf16[256,192]{1,0:T(8,128)(2,1)S(1)}) fusion(bf16[1,256,768]{2,1,0:T(8,128)(2,1)} %param.5, s32[]{:T(128)S(6)} %select_n.25, s32[]{:T(128)S(6)} %select_n.26, s32[]{:T(128)S(6)} %select_n.28, s32[]{:T(128)S(6)} %select_n.27), kind=kLoop, calls=%fused_computation.52 | loop fusion | bytes 786448 | tf_op jit(solution)/shard_map/dynamic_slice | solution.py:311
  15.5 2.4 %collective-permute-start.1 = (bf16[256,768]{1,0:T(8,128)(2,1)S(1)}, bf16[256,768]{1,0:T(8,128)(2,1)S(1)}, u32[]{:S(2)}, u32[]{:S(2)}) collective-permute-start(bf16[256,768]{1,0:T(8,128)(2,1)S(1)} %get-tuple-element.160.refs_4_), channel_id=1, source_target_pairs={{0,4},{4,0},{8,12},{12,8},{1,5},{5,1},{9,13},{13,9},{2,6},{6,2},{1... | collective-permute-start | bytes 1179656 | tf_op jit(solution)/shard_map/ppermute | solution.py:29
  22.1 2.7 %collective-permute-done.15 = bf16[192,192]{1,0:T(8,128)(2,1)} collective-permute-done((bf16[192,192]{1,0:T(8,128)(2,1)S(1)}, bf16[192,192]{1,0:T(8,128)(2,1)}, u32[]{:S(2)}, u32[]{:S(2)}) %collective-permute-start.15) | collective-permute-done | bytes 73760 | tf_op jit(solution)/shard_map/ppermute | solution.py:25
  26.4 1.6 collective-permute-start.16
  27.9 4.3 %collective-permute-start.2 = (bf16[256,768]{1,0:T(8,128)(2,1)}, bf16[256,768]{1,0:T(8,128)(2,1)S(1)}, u32[]{:S(2)}, u32[]{:S(2)}) collective-permute-start(bf16[256,768]{1,0:T(8,128)(2,1)} %get-tuple-element.136.refs_8_), channel_id=1, source_target_pairs={{0,4},{4,0},{8,12},{12,8},{1,5},{5,1},{9,13},{13,9},{2,6},{6,2},{1... | collective-permute-start | bytes 1179656 | tf_op jit(solution)/shard_map/ppermute | solution.py:29
  36.0 4.0 %collective-permute-start.3 = (bf16[256,768]{1,0:T(8,128)(2,1)}, bf16[256,768]{1,0:T(8,128)(2,1)S(1)}, u32[]{:S(2)}, u32[]{:S(2)}) collective-permute-start(bf16[256,768]{1,0:T(8,128)(2,1)} %get-tuple-element.137.refs_12_), channel_id=1, source_target_pairs={{0,4},{4,0},{8,12},{12,8},{1,5},{5,1},{9,13},{13,9},{2,6},{6,2},{1... | collective-permute-start | bytes 1179656 | tf_op jit(solution)/shard_map/ppermute | solution.py:29
  40.2 2.5 %collective-permute-start.17 = (bf16[384,768]{1,0:T(8,128)(2,1)S(1)}, bf16[384,768]{1,0:T(8,128)(2,1)S(1)}, u32[]{:S(2)}, u32[]{:S(2)}) collective-permute-start(bf16[384,768]{1,0:T(8,128)(2,1)S(1)} %pad_maximum_fusion.2.proj_a), channel_id=1, source_target_pairs={{0,4},{4,0},{8,12},{12,8},{1,5},{5,1},{9,13},{13,9},{2,6},{6,2},{1... | collective-permute-start | bytes 1769480 | tf_op jit(solution)/shard_map/ppermute | solution.py:29
  42.7 3.8 %collective-permute-done.11 = bf16[192,768]{1,0:T(8,128)(2,1)S(1)} collective-permute-done((bf16[192,768]{1,0:T(8,128)(2,1)}, bf16[192,768]{1,0:T(8,128)(2,1)S(1)}, u32[]{:S(2)}, u32[]{:S(2)}) %collective-permute-start.11) | collective-permute-done | bytes 294944 | tf_op jit(solution)/shard_map/ppermute | solution.py:29
  46.6 1.8 fusion.16
  49.9 1.6 fusion.20
  59.2 3.6 %collective-permute-done.19 = bf16[128,768]{1,0:T(8,128)(2,1)S(1)} collective-permute-done((bf16[128,768]{1,0:T(8,128)(2,1)S(1)}, bf16[128,768]{1,0:T(8,128)(2,1)S(1)}, u32[]{:S(2)}, u32[]{:S(2)}) %collective-permute-start.19) | collective-permute-done | bytes 196640 | tf_op jit(solution)/shard_map/ppermute | solution.py:47
  68.4 3.9 %collective-permute-done.27 = bf16[256,768]{1,0:T(8,128)(2,1)S(1)} collective-permute-done((bf16[256,768]{1,0:T(8,128)(2,1)S(1)}, bf16[256,768]{1,0:T(8,128)(2,1)S(1)}, u32[]{:S(2)}, u32[]{:S(2)}) %collective-permute-start.27) | collective-permute-done | bytes 393248 | tf_op jit(solution)/shard_map/ppermute | solution.py:29
  76.2 2.2 %collective-permute-done.25 = bf16[128,768]{1,0:T(8,128)(2,1)S(1)} collective-permute-done((bf16[128,768]{1,0:T(8,128)(2,1)S(1)}, bf16[128,768]{1,0:T(8,128)(2,1)S(1)}, u32[]{:S(2)}, u32[]{:S(2)}) %collective-permute-start.25) | collective-permute-done | bytes 196640 | tf_op jit(solution)/shard_map/ppermute | solution.py:25
  78.5 4.6 %collective-permute-start.33 = (bf16[256,768]{1,0:T(8,128)(2,1)S(1)}, bf16[256,768]{1,0:T(8,128)(2,1)S(1)}, u32[]{:S(2)}, u32[]{:S(2)}) collective-permute-start(bf16[256,768]{1,0:T(8,128)(2,1)S(1)} %get-tuple-element.127.mine_ref), channel_id=1, source_target_pairs={{0,4},{4,0},{8,12},{12,8},{1,5},{5,1},{9,13},{13,9},{2,6},{6,2},{1... | collective-permute-start | bytes 1179656 | tf_op jit(solution)/shard_map/ppermute | solution.py:29
  84.7 4.5 %collective-permute-done.30 = bf16[256,768]{1,0:T(8,128)(2,1)S(1)} collective-permute-done((bf16[256,768]{1,0:T(8,128)(2,1)S(1)}, bf16[256,768]{1,0:T(8,128)(2,1)S(1)}, u32[]{:S(2)}, u32[]{:S(2)}) %collective-permute-start.30) | collective-permute-done | bytes 393248 | tf_op jit(solution)/shard_map/ppermute | solution.py:29
  89.2 4.2 %collective-permute-done.31 = bf16[128,768]{1,0:T(8,128)(2,1)S(1)} collective-permute-done((bf16[128,768]{1,0:T(8,128)(2,1)S(1)}, bf16[128,768]{1,0:T(8,128)(2,1)S(1)}, u32[]{:S(2)}, u32[]{:S(2)}) %collective-permute-start.31) | collective-permute-done | bytes 196640 | tf_op jit(solution)/shard_map/ppermute | solution.py:29
  93.4 4.2 %collective-permute-done.32 = bf16[128,768]{1,0:T(8,128)(2,1)S(1)} collective-permute-done((bf16[128,768]{1,0:T(8,128)(2,1)S(1)}, bf16[128,768]{1,0:T(8,128)(2,1)S(1)}, u32[]{:S(2)}, u32[]{:S(2)}) %collective-permute-start.32) | collective-permute-done | bytes 196640 | tf_op jit(solution)/shard_map/ppermute | solution.py:29
  101.5 2.4 %scores.1 = f32[32,1,512]{2,1,0:T(1,128)S(1)} custom-call(f32[1,1]{1,0:T(1,128)} %bitcast.17.scale_ref, bf16[256,768]{1,0:T(8,128)(2,1)S(1)} %get-tuple-element.127.mine_ref, bf16[256,768]{1,0:T(8,128)(2,1)S(1)} %copy-done.6, bf16[2048,768]{1,0:T(8,128)(2,1)S(1)} %constant_dynamic-update-slice_fusion.6.others_ref), custom_call_target="tpu_custom_call" | custom-call | flops 1 | bytes 1 | tf_op jit(solution)/shard_map/scores/pallas_call | solution.py:106
  104.6 6.3 %all-to-all-start = ((f32[32,1,512]{2,1,0:T(1,128)}), f32[32,1,512]{2,1,0:T(1,128)}, u32[]{:S(2)}, u32[]{:S(2)}) async-start(f32[32,1,512]{2,1,0:T(1,128)} %copy-done.31), calls=%async_computation | async-start | bytes 131072 | tf_op jit(solution)/shard_map/all_to_all | solution.py:365
  112.1 1.8 values.1
  116.9 2.0 %all-to-all-done.lse_ref = f32[32,1,512]{2,1,0:T(1,128)} async-done(((f32[32,1,512]{2,1,0:T(1,128)}), f32[32,1,512]{2,1,0:T(1,128)}, u32[]{:S(2)}, u32[]{:S(2)}) %all-to-all-start) | async-done | bytes 65568 | tf_op jit(solution)/shard_map/all_to_all | solution.py:365
  120.1 3.1 %convolution_multiply_fusion.1 = f32[256,768]{1,0:T(8,128)S(1)} fusion(bf16[2048,768]{1,0:T(8,128)(2,1)S(1)} %constant_dynamic-update-slice_fusion.6.others_ref, f32[256,2048]{1,0:T(8,128)} %copy-done.34, f32[2048]{0:T(1024)S(1)} %bitcast.54, f32[256]{0:T(256)S(1)} %get-tuple-element.187, f32[]{:T(128)} %exp.15), kind=kOutput, calls=%fused_computation.4 | convolution fusion | flops 808124416 | bytes 6038532 | tf_op jit(solution)/shard_map/dot_general | solution.py:97
  123.8 2.6 %collective-permute-done.38.refs_11_ = bf16[256,768]{1,0:T(8,128)(2,1)S(1)} collective-permute-done((bf16[256,768]{1,0:T(8,128)(2,1)}, bf16[256,768]{1,0:T(8,128)(2,1)S(1)}, u32[]{:S(2)}, u32[]{:S(2)}) %collective-permute-start.38) | collective-permute-done | bytes 393248 | tf_op jit(solution)/shard_map/ppermute | solution.py:29
  126.8 1.5 multiply_reduce_fusion
  131.2 7.9 %collective-permute-done.45.refs_2_ = bf16[256,768]{1,0:T(8,128)(2,1)S(1)} collective-permute-done((bf16[256,768]{1,0:T(8,128)(2,1)S(1)}, bf16[256,768]{1,0:T(8,128)(2,1)S(1)}, u32[]{:S(2)}, u32[]{:S(2)}) %collective-permute-start.45) | collective-permute-done | bytes 393248 | tf_op jit(solution)/shard_map/ppermute | solution.py:29
  142.2 4.0 %terms.1 = (bf16[192,960]{1,0:T(8,128)(2,1)S(1)}, bf16[192,960]{1,0:T(8,128)(2,1)S(1)}, bf16[192,960]{1,0:T(8,128)(2,1)S(1)}, f32[192,192]{1,0:T(8,128)S(1)}, bf16[192,1024]{1,0:T(8,128)(2,1)S(1)}) custom-call(s32[4]{0:T(128)S(1)} %get-tuple-element.95.places_ref, bf16[192,768]{1,0:T(8,128)(2,1)S(1)} %slice.45.proj_ref, ...), custom_call_target="tpu_custom_call" | custom-call | flops 1 | bytes 1 | tf_op jit(solution)/shard_map/terms/pallas_call | solution.py:106
  147.6 2.1 %collective-permute-start.50 = (bf16[192,960]{1,0:T(8,128)(2,1)S(1)}, bf16[192,960]{1,0:T(8,128)(2,1)S(1)}, u32[]{:S(2)}, u32[]{:S(2)}) collective-permute-start(bf16[192,960]{1,0:T(8,128)(2,1)S(1)} %get-tuple-element.173), channel_id=1, source_target_pairs={{0,2},{1,3},{2,0},{3,1},{4,6},{5,7},{6,4},{7,5},{8,10},{9,11},{10,... | collective-permute-start | bytes 1105928 | tf_op jit(solution)/shard_map/ppermute | solution.py:25
  149.7 7.0 %collective-permute-done.47.refs_2_ = bf16[256,768]{1,0:T(8,128)(2,1)S(1)} collective-permute-done((bf16[256,768]{1,0:T(8,128)(2,1)S(1)}, bf16[256,768]{1,0:T(8,128)(2,1)S(1)}, u32[]{:S(2)}, u32[]{:S(2)}) %collective-permute-start.47) | collective-permute-done | bytes 393248 | tf_op jit(solution)/shard_map/ppermute | solution.py:29
  157.9 4.5 %own_gradients.1 = (bf16[256,768]{1,0:T(8,128)(2,1)}, bf16[256,3072]{1,0:T(8,128)(2,1)}) custom-call(s32[4]{0:T(128)S(1)} %get-tuple-element.95.places_ref, s32[4]{0:T(128)S(1)} %get-tuple-element.96.found_ref, bf16[256,3072]{1,0:T(8,128)(2,1)S(1)} %bitcast.53, bf16[256,768]{1,0:T(8,128)(2,1)S(1)} %multiply_convert_fusion.2.refs_0_.embed_ref, ...), custom_call_target="tpu_custom_call" | custom-call | flops 1 | bytes 1 | tf_op jit(solution)/shard_map/own_gradients/pallas_call | solution.py:106
  162.4 18.6 %collective-permute-done.50 = bf16[192,960]{1,0:T(8,128)(2,1)S(1)} collective-permute-done((bf16[192,960]{1,0:T(8,128)(2,1)S(1)}, bf16[192,960]{1,0:T(8,128)(2,1)S(1)}, u32[]{:S(2)}, u32[]{:S(2)}) %collective-permute-start.50) | collective-permute-done | bytes 368672 | tf_op jit(solution)/shard_map/ppermute | solution.py:25
  181.0 3.6 %collective-permute-done.49 = bf16[192,960]{1,0:T(8,128)(2,1)S(1)} collective-permute-done((bf16[192,960]{1,0:T(8,128)(2,1)S(1)}, bf16[192,960]{1,0:T(8,128)(2,1)S(1)}, u32[]{:S(2)}, u32[]{:S(2)}) %collective-permute-start.49) | collective-permute-done | bytes 368672 | tf_op jit(solution)/shard_map/ppermute | solution.py:25
  (217 shorter events, 61.5 us)
Async XLA Ops:
  0.6 10.4 %collective-permute-start.6 = (bf16[192,768]{1,0:T(8,128)(2,1)}, bf16[192,768]{1,0:T(8,128)(2,1)S(1)}, u32[]{:S(2)}, u32[]{:S(2)}) collective-permute-start(bf16[192,768]{1,0:T(8,128)(2,1)} %bitcast.59), channel_id=1, source_target_pairs={{0,1},{1,2},{2,3},{3,0},{4,5},{5,6},{6,7},{7,4},{8,9},{9,10},{10,1... | collective-permute-start | bytes 884744 | tf_op jit(solution)/shard_map/ppermute | solution.py:25
  6.3 9.1 %collective-permute-start = (bf16[256,768]{1,0:T(8,128)(2,1)S(1)}, bf16[256,768]{1,0:T(8,128)(2,1)S(1)}, u32[]{:S(2)}, u32[]{:S(2)}) collective-permute-start(bf16[256,768]{1,0:T(8,128)(2,1)S(1)} %get-tuple-element.182.refs_0_), channel_id=1, source_target_pairs={{0,4},{4,0},{8,12},{12,8},{1,5},{5,1},{9,13},{13,9},{2,6},{6,2},{1... | collective-permute-start | bytes 1179656 | tf_op jit(solution)/shard_map/ppermute | solution.py:29
  13.4 40.9 %collective-permute-start.18 = (bf16[256,768]{1,0:T(8,128)(2,1)S(1)}, bf16[256,768]{1,0:T(8,128)(2,1)}, u32[]{:S(2)}, u32[]{:S(2)}) collective-permute-start(bf16[256,768]{1,0:T(8,128)(2,1)S(1)} %get-tuple-element.160.refs_4_), channel_id=1, source_target_pairs={{0,8},{4,12},{8,0},{12,4},{1,9},{5,13},{9,1},{13,5},{2,10},{6,14},... | collective-permute-start | bytes 1179656 | tf_op jit(solution)/shard_map/ppermute | solution.py:29
  15.5 12.5 %collective-permute-start.1 = (bf16[256,768]{1,0:T(8,128)(2,1)S(1)}, bf16[256,768]{1,0:T(8,128)(2,1)S(1)}, u32[]{:S(2)}, u32[]{:S(2)}) collective-permute-start(bf16[256,768]{1,0:T(8,128)(2,1)S(1)} %get-tuple-element.160.refs_4_), channel_id=1, source_target_pairs={{0,4},{4,0},{8,12},{12,8},{1,5},{5,1},{9,13},{13,9},{2,6},{6,2},{1... | collective-permute-start | bytes 1179656 | tf_op jit(solution)/shard_map/ppermute | solution.py:29
  19.2 14.7 %collective-permute-start.9 = (bf16[192,768]{1,0:T(8,128)(2,1)}, bf16[192,768]{1,0:T(8,128)(2,1)}, u32[]{:S(2)}, u32[]{:S(2)}) collective-permute-start(bf16[192,768]{1,0:T(8,128)(2,1)} %collective-permute-done.8), channel_id=1, source_target_pairs={{0,8},{4,12},{8,0},{12,4},{1,9},{5,13},{9,1},{13,5},{2,10},{6,14},... | collective-permute-start | bytes 884744 | tf_op jit(solution)/shard_map/ppermute | solution.py:29
  20.9 12.0 %collective-permute-start.10 = (bf16[192,768]{1,0:T(8,128)(2,1)}, bf16[192,768]{1,0:T(8,128)(2,1)}, u32[]{:S(2)}, u32[]{:S(2)}) collective-permute-start(bf16[192,768]{1,0:T(8,128)(2,1)} %collective-permute-done.8), channel_id=1, source_target_pairs={{0,1},{1,2},{2,3},{3,0},{4,5},{5,6},{6,7},{7,4},{8,9},{9,10},{10,1... | collective-permute-start | bytes 884744 | tf_op jit(solution)/shard_map/ppermute | solution.py:25
  26.4 13.8 %collective-permute-start.16 = (bf16[192,768]{1,0:T(8,128)(2,1)S(1)}, bf16[192,768]{1,0:T(8,128)(2,1)S(1)}, u32[]{:S(2)}, u32[]{:S(2)}) collective-permute-start(bf16[192,768]{1,0:T(8,128)(2,1)S(1)} %constant_dynamic-slice_fusion), channel_id=1, source_target_pairs={{0,8},{4,12},{8,0},{12,4},{1,9},{5,13},{9,1},{13,5},{2,10},{6,14},... | collective-permute-start | bytes 884744 | tf_op jit(solution)/shard_map/ppermute | solution.py:29
  34.0 12.5 %collective-permute-start.11 = (bf16[192,768]{1,0:T(8,128)(2,1)}, bf16[192,768]{1,0:T(8,128)(2,1)S(1)}, u32[]{:S(2)}, u32[]{:S(2)}) collective-permute-start(bf16[192,768]{1,0:T(8,128)(2,1)} %collective-permute-done.10), channel_id=1, source_target_pairs={{0,8},{4,12},{8,0},{12,4},{1,9},{5,13},{9,1},{13,5},{2,10},{6,14},... | collective-permute-start | bytes 884744 | tf_op jit(solution)/shard_map/ppermute | solution.py:29
  36.0 12.4 %collective-permute-start.3 = (bf16[256,768]{1,0:T(8,128)(2,1)}, bf16[256,768]{1,0:T(8,128)(2,1)S(1)}, u32[]{:S(2)}, u32[]{:S(2)}) collective-permute-start(bf16[256,768]{1,0:T(8,128)(2,1)} %get-tuple-element.137.refs_12_), channel_id=1, source_target_pairs={{0,4},{4,0},{8,12},{12,8},{1,5},{5,1},{9,13},{13,9},{2,6},{6,2},{1... | collective-permute-start | bytes 1179656 | tf_op jit(solution)/shard_map/ppermute | solution.py:29
  40.2 13.0 %collective-permute-start.17 = (bf16[384,768]{1,0:T(8,128)(2,1)S(1)}, bf16[384,768]{1,0:T(8,128)(2,1)S(1)}, u32[]{:S(2)}, u32[]{:S(2)}) collective-permute-start(bf16[384,768]{1,0:T(8,128)(2,1)S(1)} %pad_maximum_fusion.2.proj_a), channel_id=1, source_target_pairs={{0,4},{4,0},{8,12},{12,8},{1,5},{5,1},{9,13},{13,9},{2,6},{6,2},{1... | collective-permute-start | bytes 1769480 | tf_op jit(solution)/shard_map/ppermute | solution.py:29
  57.7 14.6 %collective-permute-start.27 = (bf16[256,768]{1,0:T(8,128)(2,1)S(1)}, bf16[256,768]{1,0:T(8,128)(2,1)S(1)}, u32[]{:S(2)}, u32[]{:S(2)}) collective-permute-start(bf16[256,768]{1,0:T(8,128)(2,1)S(1)} %get-tuple-element.127.mine_ref), channel_id=1, source_target_pairs={{0,8},{4,12},{8,0},{12,4},{1,9},{5,13},{9,1},{13,5},{2,10},{6,14},... | collective-permute-start | bytes 1179656 | tf_op jit(solution)/shard_map/ppermute | solution.py:29
  64.6 10.5 %collective-permute-start.21 = (bf16[256,768]{1,0:T(8,128)(2,1)S(1)}, bf16[256,768]{1,0:T(8,128)(2,1)S(1)}, u32[]{:S(2)}, u32[]{:S(2)}) collective-permute-start(bf16[256,768]{1,0:T(8,128)(2,1)S(1)} %get-tuple-element.127.mine_ref), channel_id=1, source_target_pairs={{0,16},{16,0},{1,17},{17,1},{2,18},{18,2},{3,19},{19,3},{4,20},{20... | collective-permute-start | bytes 1179656 | tf_op jit(solution)/shard_map/ppermute | solution.py:52
  67.4 15.6 %collective-permute-start.26 = (bf16[256,768]{1,0:T(8,128)(2,1)S(1)}, bf16[256,768]{1,0:T(8,128)(2,1)S(1)}, u32[]{:S(2)}, u32[]{:S(2)}) collective-permute-start(bf16[256,768]{1,0:T(8,128)(2,1)S(1)} %pad_maximum_fusion.3), channel_id=1, source_target_pairs={{0,8},{4,12},{8,0},{12,4},{1,9},{5,13},{9,1},{13,5},{2,10},{6,14},... | collective-permute-start | bytes 1179656 | tf_op jit(solution)/shard_map/ppermute | solution.py:29
  72.3 10.8 %collective-permute-start.28 = (bf16[256,768]{1,0:T(8,128)(2,1)S(1)}, bf16[256,768]{1,0:T(8,128)(2,1)S(1)}, u32[]{:S(2)}, u32[]{:S(2)}) collective-permute-start(bf16[256,768]{1,0:T(8,128)(2,1)S(1)} %collective-permute-done.27), channel_id=1, source_target_pairs={{0,16},{16,0},{1,17},{17,1},{2,18},{18,2},{3,19},{19,3},{4,20},{20... | collective-permute-start | bytes 1179656 | tf_op jit(solution)/shard_map/ppermute | solution.py:52
  73.8 10.6 %collective-permute-start.29 = (bf16[128,768]{1,0:T(8,128)(2,1)S(1)}, bf16[128,768]{1,0:T(8,128)(2,1)S(1)}, u32[]{:S(2)}, u32[]{:S(2)}) collective-permute-start(bf16[128,768]{1,0:T(8,128)(2,1)S(1)} %collective-permute-done.24), channel_id=1, source_target_pairs={{0,1},{1,2},{2,3},{3,0},{4,5},{5,6},{6,7},{7,4},{8,9},{9,10},{10,1... | collective-permute-start | bytes 589832 | tf_op jit(solution)/shard_map/ppermute | solution.py:25
  75.2 14.0 %collective-permute-start.30 = (bf16[256,768]{1,0:T(8,128)(2,1)S(1)}, bf16[256,768]{1,0:T(8,128)(2,1)S(1)}, u32[]{:S(2)}, u32[]{:S(2)}) collective-permute-start(bf16[256,768]{1,0:T(8,128)(2,1)S(1)} %pad_maximum_fusion.4), channel_id=1, source_target_pairs={{0,8},{4,12},{8,0},{12,4},{1,9},{5,13},{9,1},{13,5},{2,10},{6,14},... | collective-permute-start | bytes 1179656 | tf_op jit(solution)/shard_map/ppermute | solution.py:29
  78.5 19.2 %collective-permute-start.33 = (bf16[256,768]{1,0:T(8,128)(2,1)S(1)}, bf16[256,768]{1,0:T(8,128)(2,1)S(1)}, u32[]{:S(2)}, u32[]{:S(2)}) collective-permute-start(bf16[256,768]{1,0:T(8,128)(2,1)S(1)} %get-tuple-element.127.mine_ref), channel_id=1, source_target_pairs={{0,4},{4,0},{8,12},{12,8},{1,5},{5,1},{9,13},{13,9},{2,6},{6,2},{1... | collective-permute-start | bytes 1179656 | tf_op jit(solution)/shard_map/ppermute | solution.py:29
  83.1 10.3 %collective-permute-start.31 = (bf16[128,768]{1,0:T(8,128)(2,1)S(1)}, bf16[128,768]{1,0:T(8,128)(2,1)S(1)}, u32[]{:S(2)}, u32[]{:S(2)}) collective-permute-start(bf16[128,768]{1,0:T(8,128)(2,1)S(1)} %collective-permute-done.25), channel_id=1, source_target_pairs={{0,8},{4,12},{8,0},{12,4},{1,9},{5,13},{9,1},{13,5},{2,10},{6,14},... | collective-permute-start | bytes 589832 | tf_op jit(solution)/shard_map/ppermute | solution.py:29
  84.4 13.2 %collective-permute-start.32 = (bf16[128,768]{1,0:T(8,128)(2,1)S(1)}, bf16[128,768]{1,0:T(8,128)(2,1)S(1)}, u32[]{:S(2)}, u32[]{:S(2)}) collective-permute-start(bf16[128,768]{1,0:T(8,128)(2,1)S(1)} %collective-permute-done.29), channel_id=1, source_target_pairs={{0,8},{4,12},{8,0},{12,4},{1,9},{5,13},{9,1},{13,5},{2,10},{6,14},... | collective-permute-start | bytes 589832 | tf_op jit(solution)/shard_map/ppermute | solution.py:29
  98.4 21.7 %collective-permute-start.34 = (bf16[256,768]{1,0:T(8,128)(2,1)}, bf16[256,768]{1,0:T(8,128)(2,1)}, u32[]{:S(2)}, u32[]{:S(2)}) collective-permute-start(bf16[256,768]{1,0:T(8,128)(2,1)} %get-tuple-element.136.refs_8_), channel_id=1, source_target_pairs={{0,8},{4,12},{8,0},{12,4},{1,9},{5,13},{9,1},{13,5},{2,10},{6,14},... | collective-permute-start | bytes 1179656 | tf_op jit(solution)/shard_map/ppermute | solution.py:29
  99.6 20.5 %collective-permute-start.35 = (bf16[256,768]{1,0:T(8,128)(2,1)}, bf16[256,768]{1,0:T(8,128)(2,1)}, u32[]{:S(2)}, u32[]{:S(2)}) collective-permute-start(bf16[256,768]{1,0:T(8,128)(2,1)} %get-tuple-element.137.refs_12_), channel_id=1, source_target_pairs={{0,8},{4,12},{8,0},{12,4},{1,9},{5,13},{9,1},{13,5},{2,10},{6,14},... | collective-permute-start | bytes 1179656 | tf_op jit(solution)/shard_map/ppermute | solution.py:29
  104.6 14.3 %all-to-all-start = ((f32[32,1,512]{2,1,0:T(1,128)}), f32[32,1,512]{2,1,0:T(1,128)}, u32[]{:S(2)}, u32[]{:S(2)}) async-start(f32[32,1,512]{2,1,0:T(1,128)} %copy-done.31), calls=%async_computation | async-start | bytes 131072 | tf_op jit(solution)/shard_map/all_to_all | solution.py:365
  128.5 11.7 %collective-permute-start.40 = (bf16[384,768]{1,0:T(8,128)(2,1)S(1)}, bf16[384,768]{1,0:T(8,128)(2,1)S(1)}, u32[]{:S(2)}, u32[]{:S(2)}) collective-permute-start(bf16[384,768]{1,0:T(8,128)(2,1)S(1)} %copy-done.4), channel_id=1, source_target_pairs={{0,4},{4,0},{8,12},{12,8},{1,5},{5,1},{9,13},{13,9},{2,6},{6,2},{1... | collective-permute-start | bytes 1769480 | tf_op jit(solution)/shard_map/ppermute | solution.py:29
  128.8 10.3 %collective-permute-start.45 = (bf16[256,768]{1,0:T(8,128)(2,1)S(1)}, bf16[256,768]{1,0:T(8,128)(2,1)S(1)}, u32[]{:S(2)}, u32[]{:S(2)}) collective-permute-start(bf16[256,768]{1,0:T(8,128)(2,1)S(1)} %multiply_convert_fusion.2.refs_0_.embed_ref), channel_id=1, source_target_pairs={{0,8},{4,12},{8,0},{12,4},{1,9},{5,13},{9,1},{13,5},{2,10},{6,14},... | collective-permute-start | bytes 1179656 | tf_op jit(solution)/shard_map/ppermute | solution.py:29
  130.0 10.4 %collective-permute-start.41 = (bf16[384,768]{1,0:T(8,128)(2,1)S(1)}, bf16[384,768]{1,0:T(8,128)(2,1)S(1)}, u32[]{:S(2)}, u32[]{:S(2)}) collective-permute-start(bf16[384,768]{1,0:T(8,128)(2,1)S(1)} %copy-done.11), channel_id=1, source_target_pairs={{0,4},{4,0},{8,12},{12,8},{1,5},{5,1},{9,13},{13,9},{2,6},{6,2},{1... | collective-permute-start | bytes 1769480 | tf_op jit(solution)/shard_map/ppermute | solution.py:29
  130.7 9.7 %collective-permute-start.42 = (bf16[384,768]{1,0:T(8,128)(2,1)S(1)}, bf16[384,768]{1,0:T(8,128)(2,1)S(1)}, u32[]{:S(2)}, u32[]{:S(2)}) collective-permute-start(bf16[384,768]{1,0:T(8,128)(2,1)S(1)} %copy-done.9), channel_id=1, source_target_pairs={{0,4},{4,0},{8,12},{12,8},{1,5},{5,1},{9,13},{13,9},{2,6},{6,2},{1... | collective-permute-start | bytes 1769480 | tf_op jit(solution)/shard_map/ppermute | solution.py:29
  130.7 9.6 %collective-permute-start.43 = (bf16[384,768]{1,0:T(8,128)(2,1)S(1)}, bf16[384,768]{1,0:T(8,128)(2,1)S(1)}, u32[]{:S(2)}, u32[]{:S(2)}) collective-permute-start(bf16[384,768]{1,0:T(8,128)(2,1)S(1)} %copy-done.13), channel_id=1, source_target_pairs={{0,4},{4,0},{8,12},{12,8},{1,5},{5,1},{9,13},{13,9},{2,6},{6,2},{1... | collective-permute-start | bytes 1769480 | tf_op jit(solution)/shard_map/ppermute | solution.py:29
  146.3 10.4 %collective-permute-start.47 = (bf16[256,768]{1,0:T(8,128)(2,1)S(1)}, bf16[256,768]{1,0:T(8,128)(2,1)S(1)}, u32[]{:S(2)}, u32[]{:S(2)}) collective-permute-start(bf16[256,768]{1,0:T(8,128)(2,1)S(1)} %copy-done.26), channel_id=1, source_target_pairs={{0,8},{4,12},{8,0},{12,4},{1,9},{5,13},{9,1},{13,5},{2,10},{6,14},... | collective-permute-start | bytes 1179656 | tf_op jit(solution)/shard_map/ppermute | solution.py:29
  147.6 14.8 %collective-permute-start.51 = (bf16[192,960]{1,0:T(8,128)(2,1)S(1)}, bf16[192,960]{1,0:T(8,128)(2,1)S(1)}, u32[]{:S(2)}, u32[]{:S(2)}) collective-permute-start(bf16[192,960]{1,0:T(8,128)(2,1)S(1)} %get-tuple-element.174), channel_id=1, source_target_pairs={{0,1},{1,2},{2,3},{3,0},{4,5},{5,6},{6,7},{7,4},{8,9},{9,10},{10,1... | collective-permute-start | bytes 1105928 | tf_op jit(solution)/shard_map/ppermute | solution.py:25
  147.6 33.4 %collective-permute-start.50 = (bf16[192,960]{1,0:T(8,128)(2,1)S(1)}, bf16[192,960]{1,0:T(8,128)(2,1)S(1)}, u32[]{:S(2)}, u32[]{:S(2)}) collective-permute-start(bf16[192,960]{1,0:T(8,128)(2,1)S(1)} %get-tuple-element.173), channel_id=1, source_target_pairs={{0,2},{1,3},{2,0},{3,1},{4,6},{5,7},{6,4},{7,5},{8,10},{9,11},{10,... | collective-permute-start | bytes 1105928 | tf_op jit(solution)/shard_map/ppermute | solution.py:25
  149.7 34.9 %collective-permute-start.49 = (bf16[192,960]{1,0:T(8,128)(2,1)S(1)}, bf16[192,960]{1,0:T(8,128)(2,1)S(1)}, u32[]{:S(2)}, u32[]{:S(2)}) collective-permute-start(bf16[192,960]{1,0:T(8,128)(2,1)S(1)} %get-tuple-element.172), channel_id=1, source_target_pairs={{0,3},{1,0},{2,1},{3,2},{4,7},{5,4},{6,5},{7,6},{8,11},{9,8},{10,9... | collective-permute-start | bytes 1105928 | tf_op jit(solution)/shard_map/ppermute | solution.py:25
  156.7 28.7 %collective-permute-start.48 = (bf16[256,768]{1,0:T(8,128)(2,1)S(1)}, bf16[256,768]{1,0:T(8,128)(2,1)S(1)}, u32[]{:S(2)}, u32[]{:S(2)}) collective-permute-start(bf16[256,768]{1,0:T(8,128)(2,1)S(1)} %collective-permute-done.47.refs_2_), channel_id=1, source_target_pairs={{0,4},{4,0},{8,12},{12,8},{1,5},{5,1},{9,13},{13,9},{2,6},{6,2},{1... | collective-permute-start | bytes 1179656 | tf_op jit(solution)/shard_map/ppermute | solution.py:29
  (66 other events, 563.7 us)

commit v7 on v5

--- a/solution.py
+++ b/solution.py
@@ -299,7 +299,7 @@
         pace = () if k == 1 else (down_ring[k - 1],)
         proj_ring.append(shift(after(proj_ring[-1], *pace), "gcol", 1))
     down_tables = [spread(part, far[0]) for part in down_ring]
-    active_even = {1: spread(after(active[1], down_tables[0][last]))}
+    active_even = {1: spread(after(active[1], down_ring[1]))}
     proj_own = jnp.roll(jnp.concatenate(proj_ring[::-1], 1), (gcol + 1) * columns, 1)
     proj_even = spread(proj_own)
     proj_pair = jnp.concatenate([proj_even[j] for j in evens], 0)

time: 187 us -> 187 us (level)
  no operation moved by 1% of the time
where the time goes in v7:
time: 187 us
  waiting for transfers between devices  78.2 us (42%)
  starting transfers between devices  59.6 us (32%)
  local copies, waits for them, and re-layouts  16.3 us (9%)
  Pallas kernels  15.9 us (9%)
  matrix products  9.66 us (5%)
  other arithmetic  4.88 us (3%)
  between operations  2.2 us (1%)
    ppermute x35, waiting for transfers between devices, swap(): lax.ppermute(value, axis, [(i, i ^ bit) for i in range(lax.axis_size(axis...  41.9 us
    ppermute x35, starting transfers between devices, swap(): lax.ppermute(value, axis, [(i, i ^ bit) for i in range(lax.axis_size(axis...  38.5 us
    ppermute x13, waiting for transfers between devices, shift(): lax.ppermute(value, axis, [(i, (i + step) % count) for i in range(count)])  27.9 us
    pallas_call x7, Pallas kernels, call(): pl.pallas_call(kernel, out_shape=[jax.ShapeDtypeStruct(shape, dtype) for...  15.9 us
    ppermute x13, starting transfers between devices, shift(): lax.ppermute(value, axis, [(i, (i + step) % count) for i in range(count)])  11.7 us
    unnamed x104, local copies, waits for them, and re-layouts  10.5 us
    all_to_all x1, starting transfers between devices, body(): lse_all = lax.all_to_all(lse, ('tower', 'grow', 'gcol'), 0, 0)  6.26 us
    dot_general x3, matrix products, dot_nn(): return jnp.dot(left, right, preferred_element_type=F32)  5.06 us
  transfers between devices with their start and end apart: 53, of which 25 were waited for; matrix products, arithmetic and copies ran while one was open for 11% of the time, Pallas kernels for 6%

profile of v7, /device:TPU:9, one launch (start us, length us, event | category | flops | bytes accessed | tf_op | source)
XLA Modules:
  0.0 186.8 jit_solution(6057959390404878920)
XLA Ops:
  4.7 1.6 activate.1
  8.9 2.1 %dynamic-slice_bitcast_fusion.3 = (bf16[256,192]{1,0:T(8,128)(2,1)}, bf16[256,192]{1,0:T(8,128)(2,1)}, bf16[256,192]{1,0:T(8,128)(2,1)S(1)}, bf16[256,192]{1,0:T(8,128)(2,1)S(1)}) fusion(bf16[1,256,768]{2,1,0:T(8,128)(2,1)} %param.5, s32[]{:T(128)S(6)} %select_n.25, s32[]{:T(128)S(6)} %select_n.26, s32[]{:T(128)S(6)} %select_n.28, s32[]{:T(128)S(6)} %select_n.27), kind=kLoop, calls=%fused_computation.52 | loop fusion | bytes 786448 | tf_op jit(solution)/shard_map/dynamic_slice | solution.py:311
  15.5 2.4 %collective-permute-start.1 = (bf16[256,768]{1,0:T(8,128)(2,1)S(1)}, bf16[256,768]{1,0:T(8,128)(2,1)S(1)}, u32[]{:S(2)}, u32[]{:S(2)}) collective-permute-start(bf16[256,768]{1,0:T(8,128)(2,1)S(1)} %get-tuple-element.164.refs_4_), channel_id=1, source_target_pairs={{0,4},{4,0},{8,12},{12,8},{1,5},{5,1},{9,13},{13,9},{2,6},{6,2},{1... | collective-permute-start | bytes 1179656 | tf_op jit(solution)/shard_map/ppermute | solution.py:29
  22.1 2.7 %collective-permute-done.15 = bf16[192,192]{1,0:T(8,128)(2,1)} collective-permute-done((bf16[192,192]{1,0:T(8,128)(2,1)S(1)}, bf16[192,192]{1,0:T(8,128)(2,1)}, u32[]{:S(2)}, u32[]{:S(2)}) %collective-permute-start.15) | collective-permute-done | bytes 73760 | tf_op jit(solution)/shard_map/ppermute | solution.py:25
  27.9 4.3 %collective-permute-start.2 = (bf16[256,768]{1,0:T(8,128)(2,1)}, bf16[256,768]{1,0:T(8,128)(2,1)S(1)}, u32[]{:S(2)}, u32[]{:S(2)}) collective-permute-start(bf16[256,768]{1,0:T(8,128)(2,1)} %get-tuple-element.140.refs_8_), channel_id=1, source_target_pairs={{0,4},{4,0},{8,12},{12,8},{1,5},{5,1},{9,13},{13,9},{2,6},{6,2},{1... | collective-permute-start | bytes 1179656 | tf_op jit(solution)/shard_map/ppermute | solution.py:29
  36.0 4.0 %collective-permute-start.3 = (bf16[256,768]{1,0:T(8,128)(2,1)}, bf16[256,768]{1,0:T(8,128)(2,1)S(1)}, u32[]{:S(2)}, u32[]{:S(2)}) collective-permute-start(bf16[256,768]{1,0:T(8,128)(2,1)} %get-tuple-element.141.refs_12_), channel_id=1, source_target_pairs={{0,4},{4,0},{8,12},{12,8},{1,5},{5,1},{9,13},{13,9},{2,6},{6,2},{1... | collective-permute-start | bytes 1179656 | tf_op jit(solution)/shard_map/ppermute | solution.py:29
  40.2 2.5 %collective-permute-start.17 = (bf16[384,768]{1,0:T(8,128)(2,1)S(1)}, bf16[384,768]{1,0:T(8,128)(2,1)S(1)}, u32[]{:S(2)}, u32[]{:S(2)}) collective-permute-start(bf16[384,768]{1,0:T(8,128)(2,1)S(1)} %pad_maximum_fusion.2.proj_a), channel_id=1, source_target_pairs={{0,4},{4,0},{8,12},{12,8},{1,5},{5,1},{9,13},{13,9},{2,6},{6,2},{1... | collective-permute-start | bytes 1769480 | tf_op jit(solution)/shard_map/ppermute | solution.py:29
  42.7 3.8 %collective-permute-done.11 = bf16[192,768]{1,0:T(8,128)(2,1)S(1)} collective-permute-done((bf16[192,768]{1,0:T(8,128)(2,1)}, bf16[192,768]{1,0:T(8,128)(2,1)S(1)}, u32[]{:S(2)}, u32[]{:S(2)}) %collective-permute-start.11) | collective-permute-done | bytes 294944 | tf_op jit(solution)/shard_map/ppermute | solution.py:29
  46.6 1.8 fusion.16
  49.9 1.6 fusion.20
  59.2 3.6 %collective-permute-done.19 = bf16[128,768]{1,0:T(8,128)(2,1)S(1)} collective-permute-done((bf16[128,768]{1,0:T(8,128)(2,1)S(1)}, bf16[128,768]{1,0:T(8,128)(2,1)S(1)}, u32[]{:S(2)}, u32[]{:S(2)}) %collective-permute-start.19) | collective-permute-done | bytes 196640 | tf_op jit(solution)/shard_map/ppermute | solution.py:47
  68.4 3.9 %collective-permute-done.27 = bf16[256,768]{1,0:T(8,128)(2,1)S(1)} collective-permute-done((bf16[256,768]{1,0:T(8,128)(2,1)S(1)}, bf16[256,768]{1,0:T(8,128)(2,1)S(1)}, u32[]{:S(2)}, u32[]{:S(2)}) %collective-permute-start.27) | collective-permute-done | bytes 393248 | tf_op jit(solution)/shard_map/ppermute | solution.py:29
  74.8 2.2 %collective-permute-start.29 = (bf16[128,768]{1,0:T(8,128)(2,1)S(1)}, bf16[128,768]{1,0:T(8,128)(2,1)S(1)}, u32[]{:S(2)}, u32[]{:S(2)}) collective-permute-start(bf16[128,768]{1,0:T(8,128)(2,1)S(1)} %collective-permute-done.24), channel_id=1, source_target_pairs={{0,1},{1,2},{2,3},{3,0},{4,5},{5,6},{6,7},{7,4},{8,9},{9,10},{10,1... | collective-permute-start | bytes 589832 | tf_op jit(solution)/shard_map/ppermute | solution.py:25
  77.1 3.6 %collective-permute-done.26 = bf16[256,768]{1,0:T(8,128)(2,1)S(1)} collective-permute-done((bf16[256,768]{1,0:T(8,128)(2,1)S(1)}, bf16[256,768]{1,0:T(8,128)(2,1)S(1)}, u32[]{:S(2)}, u32[]{:S(2)}) %collective-permute-start.26) | collective-permute-done | bytes 393248 | tf_op jit(solution)/shard_map/ppermute | solution.py:29
  80.8 1.9 %collective-permute-done.28 = bf16[256,768]{1,0:T(8,128)(2,1)S(1)} collective-permute-done((bf16[256,768]{1,0:T(8,128)(2,1)S(1)}, bf16[256,768]{1,0:T(8,128)(2,1)S(1)}, u32[]{:S(2)}, u32[]{:S(2)}) %collective-permute-start.28) | collective-permute-done | bytes 393248 | tf_op jit(solution)/shard_map/ppermute | solution.py:52
  83.4 1.9 collective-permute-done.29
  85.3 3.8 %collective-permute-start.33 = (bf16[256,768]{1,0:T(8,128)(2,1)S(1)}, bf16[256,768]{1,0:T(8,128)(2,1)S(1)}, u32[]{:S(2)}, u32[]{:S(2)}) collective-permute-start(bf16[256,768]{1,0:T(8,128)(2,1)S(1)} %get-tuple-element.131.mine_ref), channel_id=1, source_target_pairs={{0,4},{4,0},{8,12},{12,8},{1,5},{5,1},{9,13},{13,9},{2,6},{6,2},{1... | collective-permute-start | bytes 1179656 | tf_op jit(solution)/shard_map/ppermute | solution.py:29
  89.2 4.2 %collective-permute-done.31 = bf16[128,768]{1,0:T(8,128)(2,1)S(1)} collective-permute-done((bf16[128,768]{1,0:T(8,128)(2,1)S(1)}, bf16[128,768]{1,0:T(8,128)(2,1)S(1)}, u32[]{:S(2)}, u32[]{:S(2)}) %collective-permute-start.31) | collective-permute-done | bytes 196640 | tf_op jit(solution)/shard_map/ppermute | solution.py:29
  93.4 4.2 %collective-permute-done.32 = bf16[128,768]{1,0:T(8,128)(2,1)S(1)} collective-permute-done((bf16[128,768]{1,0:T(8,128)(2,1)S(1)}, bf16[128,768]{1,0:T(8,128)(2,1)S(1)}, u32[]{:S(2)}, u32[]{:S(2)}) %collective-permute-start.32) | collective-permute-done | bytes 196640 | tf_op jit(solution)/shard_map/ppermute | solution.py:29
  101.5 2.4 %scores.1 = f32[32,1,512]{2,1,0:T(1,128)S(1)} custom-call(f32[1,1]{1,0:T(1,128)} %bitcast.17.scale_ref, bf16[256,768]{1,0:T(8,128)(2,1)S(1)} %get-tuple-element.131.mine_ref, bf16[256,768]{1,0:T(8,128)(2,1)S(1)} %copy-done.6, bf16[2048,768]{1,0:T(8,128)(2,1)S(1)} %constant_dynamic-update-slice_fusion.6.others_ref), custom_call_target="tpu_custom_call" | custom-call | flops 1 | bytes 1 | tf_op jit(solution)/shard_map/scores/pallas_call | solution.py:106
  104.6 6.3 %all-to-all-start = ((f32[32,1,512]{2,1,0:T(1,128)}), f32[32,1,512]{2,1,0:T(1,128)}, u32[]{:S(2)}, u32[]{:S(2)}) async-start(f32[32,1,512]{2,1,0:T(1,128)} %copy-done.31), calls=%async_computation | async-start | bytes 131072 | tf_op jit(solution)/shard_map/all_to_all | solution.py:365
  112.0 1.8 values.1
  116.9 2.0 %all-to-all-done.lse_ref = f32[32,1,512]{2,1,0:T(1,128)} async-done(((f32[32,1,512]{2,1,0:T(1,128)}), f32[32,1,512]{2,1,0:T(1,128)}, u32[]{:S(2)}, u32[]{:S(2)}) %all-to-all-start) | async-done | bytes 65568 | tf_op jit(solution)/shard_map/all_to_all | solution.py:365
  120.1 3.1 %convolution_multiply_fusion.1 = f32[256,768]{1,0:T(8,128)S(1)} fusion(bf16[2048,768]{1,0:T(8,128)(2,1)S(1)} %constant_dynamic-update-slice_fusion.6.others_ref, f32[256,2048]{1,0:T(8,128)} %copy-done.34, f32[2048]{0:T(1024)S(1)} %bitcast.54, f32[256]{0:T(256)S(1)} %get-tuple-element.191, f32[]{:T(128)} %exp.15), kind=kOutput, calls=%fused_computation.4 | convolution fusion | flops 808124416 | bytes 6038532 | tf_op jit(solution)/shard_map/dot_general | solution.py:97
  123.8 2.6 %collective-permute-done.38.refs_11_ = bf16[256,768]{1,0:T(8,128)(2,1)S(1)} collective-permute-done((bf16[256,768]{1,0:T(8,128)(2,1)}, bf16[256,768]{1,0:T(8,128)(2,1)S(1)}, u32[]{:S(2)}, u32[]{:S(2)}) %collective-permute-start.38) | collective-permute-done | bytes 393248 | tf_op jit(solution)/shard_map/ppermute | solution.py:29
  131.2 7.9 %collective-permute-done.45.refs_2_ = bf16[256,768]{1,0:T(8,128)(2,1)S(1)} collective-permute-done((bf16[256,768]{1,0:T(8,128)(2,1)S(1)}, bf16[256,768]{1,0:T(8,128)(2,1)S(1)}, u32[]{:S(2)}, u32[]{:S(2)}) %collective-permute-start.45) | collective-permute-done | bytes 393248 | tf_op jit(solution)/shard_map/ppermute | solution.py:29
  142.2 4.0 %terms.1 = (bf16[192,960]{1,0:T(8,128)(2,1)S(1)}, bf16[192,960]{1,0:T(8,128)(2,1)S(1)}, bf16[192,960]{1,0:T(8,128)(2,1)S(1)}, f32[192,192]{1,0:T(8,128)S(1)}, bf16[192,1024]{1,0:T(8,128)(2,1)S(1)}) custom-call(s32[4]{0:T(128)S(1)} %get-tuple-element.97.places_ref, bf16[192,768]{1,0:T(8,128)(2,1)S(1)} %slice.45.proj_ref, ...), custom_call_target="tpu_custom_call" | custom-call | flops 1 | bytes 1 | tf_op jit(solution)/shard_map/terms/pallas_call | solution.py:106
  147.9 1.7 collective-permute-start.50
  151.0 5.7 %collective-permute-done.47.refs_2_ = bf16[256,768]{1,0:T(8,128)(2,1)S(1)} collective-permute-done((bf16[256,768]{1,0:T(8,128)(2,1)S(1)}, bf16[256,768]{1,0:T(8,128)(2,1)S(1)}, u32[]{:S(2)}, u32[]{:S(2)}) %collective-permute-start.47) | collective-permute-done | bytes 393248 | tf_op jit(solution)/shard_map/ppermute | solution.py:29
  157.9 4.5 %own_gradients.1 = (bf16[256,768]{1,0:T(8,128)(2,1)}, bf16[256,3072]{1,0:T(8,128)(2,1)}) custom-call(s32[4]{0:T(128)S(1)} %get-tuple-element.97.places_ref, s32[4]{0:T(128)S(1)} %get-tuple-element.98.found_ref, bf16[256,3072]{1,0:T(8,128)(2,1)S(1)} %bitcast.53, bf16[256,768]{1,0:T(8,128)(2,1)S(1)} %multiply_convert_fusion.2.refs_0_.embed_ref, ...), custom_call_target="tpu_custom_call" | custom-call | flops 1 | bytes 1 | tf_op jit(solution)/shard_map/own_gradients/pallas_call | solution.py:106
  162.4 18.6 %collective-permute-done.50 = bf16[192,960]{1,0:T(8,128)(2,1)S(1)} collective-permute-done((bf16[192,960]{1,0:T(8,128)(2,1)S(1)}, bf16[192,960]{1,0:T(8,128)(2,1)S(1)}, u32[]{:S(2)}, u32[]{:S(2)}) %collective-permute-start.50) | collective-permute-done | bytes 368672 | tf_op jit(solution)/shard_map/ppermute | solution.py:25
  181.0 3.6 %collective-permute-done.49 = bf16[192,960]{1,0:T(8,128)(2,1)S(1)} collective-permute-done((bf16[192,960]{1,0:T(8,128)(2,1)S(1)}, bf16[192,960]{1,0:T(8,128)(2,1)S(1)}, u32[]{:S(2)}, u32[]{:S(2)}) %collective-permute-start.49) | collective-permute-done | bytes 368672 | tf_op jit(solution)/shard_map/ppermute | solution.py:25
  (217 shorter events, 64.1 us)
Async XLA Ops:
  0.6 10.4 %collective-permute-start.6 = (bf16[192,768]{1,0:T(8,128)(2,1)}, bf16[192,768]{1,0:T(8,128)(2,1)S(1)}, u32[]{:S(2)}, u32[]{:S(2)}) collective-permute-start(bf16[192,768]{1,0:T(8,128)(2,1)} %bitcast.59), channel_id=1, source_target_pairs={{0,1},{1,2},{2,3},{3,0},{4,5},{5,6},{6,7},{7,4},{8,9},{9,10},{10,1... | collective-permute-start | bytes 884744 | tf_op jit(solution)/shard_map/ppermute | solution.py:25
  6.3 9.1 %collective-permute-start = (bf16[256,768]{1,0:T(8,128)(2,1)S(1)}, bf16[256,768]{1,0:T(8,128)(2,1)S(1)}, u32[]{:S(2)}, u32[]{:S(2)}) collective-permute-start(bf16[256,768]{1,0:T(8,128)(2,1)S(1)} %get-tuple-element.186.refs_0_), channel_id=1, source_target_pairs={{0,4},{4,0},{8,12},{12,8},{1,5},{5,1},{9,13},{13,9},{2,6},{6,2},{1... | collective-permute-start | bytes 1179656 | tf_op jit(solution)/shard_map/ppermute | solution.py:29
  13.4 40.9 %collective-permute-start.18 = (bf16[256,768]{1,0:T(8,128)(2,1)S(1)}, bf16[256,768]{1,0:T(8,128)(2,1)}, u32[]{:S(2)}, u32[]{:S(2)}) collective-permute-start(bf16[256,768]{1,0:T(8,128)(2,1)S(1)} %get-tuple-element.164.refs_4_), channel_id=1, source_target_pairs={{0,8},{4,12},{8,0},{12,4},{1,9},{5,13},{9,1},{13,5},{2,10},{6,14},... | collective-permute-start | bytes 1179656 | tf_op jit(solution)/shard_map/ppermute | solution.py:29
  15.5 12.5 %collective-permute-start.1 = (bf16[256,768]{1,0:T(8,128)(2,1)S(1)}, bf16[256,768]{1,0:T(8,128)(2,1)S(1)}, u32[]{:S(2)}, u32[]{:S(2)}) collective-permute-start(bf16[256,768]{1,0:T(8,128)(2,1)S(1)} %get-tuple-element.164.refs_4_), channel_id=1, source_target_pairs={{0,4},{4,0},{8,12},{12,8},{1,5},{5,1},{9,13},{13,9},{2,6},{6,2},{1... | collective-permute-start | bytes 1179656 | tf_op jit(solution)/shard_map/ppermute | solution.py:29
  19.2 14.7 %collective-permute-start.9 = (bf16[192,768]{1,0:T(8,128)(2,1)}, bf16[192,768]{1,0:T(8,128)(2,1)}, u32[]{:S(2)}, u32[]{:S(2)}) collective-permute-start(bf16[192,768]{1,0:T(8,128)(2,1)} %collective-permute-done.8), channel_id=1, source_target_pairs={{0,8},{4,12},{8,0},{12,4},{1,9},{5,13},{9,1},{13,5},{2,10},{6,14},... | collective-permute-start | bytes 884744 | tf_op jit(solution)/shard_map/ppermute | solution.py:29
  20.9 12.0 %collective-permute-start.10 = (bf16[192,768]{1,0:T(8,128)(2,1)}, bf16[192,768]{1,0:T(8,128)(2,1)}, u32[]{:S(2)}, u32[]{:S(2)}) collective-permute-start(bf16[192,768]{1,0:T(8,128)(2,1)} %collective-permute-done.8), channel_id=1, source_target_pairs={{0,1},{1,2},{2,3},{3,0},{4,5},{5,6},{6,7},{7,4},{8,9},{9,10},{10,1... | collective-permute-start | bytes 884744 | tf_op jit(solution)/shard_map/ppermute | solution.py:25
  26.4 13.8 %collective-permute-start.16 = (bf16[192,768]{1,0:T(8,128)(2,1)S(1)}, bf16[192,768]{1,0:T(8,128)(2,1)S(1)}, u32[]{:S(2)}, u32[]{:S(2)}) collective-permute-start(bf16[192,768]{1,0:T(8,128)(2,1)S(1)} %constant_dynamic-slice_fusion), channel_id=1, source_target_pairs={{0,8},{4,12},{8,0},{12,4},{1,9},{5,13},{9,1},{13,5},{2,10},{6,14},... | collective-permute-start | bytes 884744 | tf_op jit(solution)/shard_map/ppermute | solution.py:29
  34.0 12.5 %collective-permute-start.11 = (bf16[192,768]{1,0:T(8,128)(2,1)}, bf16[192,768]{1,0:T(8,128)(2,1)S(1)}, u32[]{:S(2)}, u32[]{:S(2)}) collective-permute-start(bf16[192,768]{1,0:T(8,128)(2,1)} %collective-permute-done.10), channel_id=1, source_target_pairs={{0,8},{4,12},{8,0},{12,4},{1,9},{5,13},{9,1},{13,5},{2,10},{6,14},... | collective-permute-start | bytes 884744 | tf_op jit(solution)/shard_map/ppermute | solution.py:29
  36.0 12.4 %collective-permute-start.3 = (bf16[256,768]{1,0:T(8,128)(2,1)}, bf16[256,768]{1,0:T(8,128)(2,1)S(1)}, u32[]{:S(2)}, u32[]{:S(2)}) collective-permute-start(bf16[256,768]{1,0:T(8,128)(2,1)} %get-tuple-element.141.refs_12_), channel_id=1, source_target_pairs={{0,4},{4,0},{8,12},{12,8},{1,5},{5,1},{9,13},{13,9},{2,6},{6,2},{1... | collective-permute-start | bytes 1179656 | tf_op jit(solution)/shard_map/ppermute | solution.py:29
  40.2 13.0 %collective-permute-start.17 = (bf16[384,768]{1,0:T(8,128)(2,1)S(1)}, bf16[384,768]{1,0:T(8,128)(2,1)S(1)}, u32[]{:S(2)}, u32[]{:S(2)}) collective-permute-start(bf16[384,768]{1,0:T(8,128)(2,1)S(1)} %pad_maximum_fusion.2.proj_a), channel_id=1, source_target_pairs={{0,4},{4,0},{8,12},{12,8},{1,5},{5,1},{9,13},{13,9},{2,6},{6,2},{1... | collective-permute-start | bytes 1769480 | tf_op jit(solution)/shard_map/ppermute | solution.py:29
  57.7 14.6 %collective-permute-start.27 = (bf16[256,768]{1,0:T(8,128)(2,1)S(1)}, bf16[256,768]{1,0:T(8,128)(2,1)S(1)}, u32[]{:S(2)}, u32[]{:S(2)}) collective-permute-start(bf16[256,768]{1,0:T(8,128)(2,1)S(1)} %get-tuple-element.131.mine_ref), channel_id=1, source_target_pairs={{0,8},{4,12},{8,0},{12,4},{1,9},{5,13},{9,1},{13,5},{2,10},{6,14},... | collective-permute-start | bytes 1179656 | tf_op jit(solution)/shard_map/ppermute | solution.py:29
  64.6 10.2 %collective-permute-start.21 = (bf16[256,768]{1,0:T(8,128)(2,1)S(1)}, bf16[256,768]{1,0:T(8,128)(2,1)S(1)}, u32[]{:S(2)}, u32[]{:S(2)}) collective-permute-start(bf16[256,768]{1,0:T(8,128)(2,1)S(1)} %get-tuple-element.131.mine_ref), channel_id=1, source_target_pairs={{0,16},{16,0},{1,17},{17,1},{2,18},{18,2},{3,19},{19,3},{4,20},{20... | collective-permute-start | bytes 1179656 | tf_op jit(solution)/shard_map/ppermute | solution.py:52
  67.4 13.3 %collective-permute-start.26 = (bf16[256,768]{1,0:T(8,128)(2,1)S(1)}, bf16[256,768]{1,0:T(8,128)(2,1)S(1)}, u32[]{:S(2)}, u32[]{:S(2)}) collective-permute-start(bf16[256,768]{1,0:T(8,128)(2,1)S(1)} %pad_maximum_fusion.3), channel_id=1, source_target_pairs={{0,8},{4,12},{8,0},{12,4},{1,9},{5,13},{9,1},{13,5},{2,10},{6,14},... | collective-permute-start | bytes 1179656 | tf_op jit(solution)/shard_map/ppermute | solution.py:29
  72.3 10.3 %collective-permute-start.28 = (bf16[256,768]{1,0:T(8,128)(2,1)S(1)}, bf16[256,768]{1,0:T(8,128)(2,1)S(1)}, u32[]{:S(2)}, u32[]{:S(2)}) collective-permute-start(bf16[256,768]{1,0:T(8,128)(2,1)S(1)} %collective-permute-done.27), channel_id=1, source_target_pairs={{0,16},{16,0},{1,17},{17,1},{2,18},{18,2},{3,19},{19,3},{4,20},{20... | collective-permute-start | bytes 1179656 | tf_op jit(solution)/shard_map/ppermute | solution.py:52
  73.7 15.4 %collective-permute-start.30 = (bf16[256,768]{1,0:T(8,128)(2,1)S(1)}, bf16[256,768]{1,0:T(8,128)(2,1)S(1)}, u32[]{:S(2)}, u32[]{:S(2)}) collective-permute-start(bf16[256,768]{1,0:T(8,128)(2,1)S(1)} %pad_maximum_fusion.4), channel_id=1, source_target_pairs={{0,8},{4,12},{8,0},{12,4},{1,9},{5,13},{9,1},{13,5},{2,10},{6,14},... | collective-permute-start | bytes 1179656 | tf_op jit(solution)/shard_map/ppermute | solution.py:29
  74.8 10.4 %collective-permute-start.29 = (bf16[128,768]{1,0:T(8,128)(2,1)S(1)}, bf16[128,768]{1,0:T(8,128)(2,1)S(1)}, u32[]{:S(2)}, u32[]{:S(2)}) collective-permute-start(bf16[128,768]{1,0:T(8,128)(2,1)S(1)} %collective-permute-done.24), channel_id=1, source_target_pairs={{0,1},{1,2},{2,3},{3,0},{4,5},{5,6},{6,7},{7,4},{8,9},{9,10},{10,1... | collective-permute-start | bytes 589832 | tf_op jit(solution)/shard_map/ppermute | solution.py:25
  82.7 10.7 %collective-permute-start.31 = (bf16[128,768]{1,0:T(8,128)(2,1)S(1)}, bf16[128,768]{1,0:T(8,128)(2,1)S(1)}, u32[]{:S(2)}, u32[]{:S(2)}) collective-permute-start(bf16[128,768]{1,0:T(8,128)(2,1)S(1)} %collective-permute-done.25), channel_id=1, source_target_pairs={{0,8},{4,12},{8,0},{12,4},{1,9},{5,13},{9,1},{13,5},{2,10},{6,14},... | collective-permute-start | bytes 589832 | tf_op jit(solution)/shard_map/ppermute | solution.py:29
  85.3 12.3 %collective-permute-start.32 = (bf16[128,768]{1,0:T(8,128)(2,1)S(1)}, bf16[128,768]{1,0:T(8,128)(2,1)S(1)}, u32[]{:S(2)}, u32[]{:S(2)}) collective-permute-start(bf16[128,768]{1,0:T(8,128)(2,1)S(1)} %collective-permute-done.29), channel_id=1, source_target_pairs={{0,8},{4,12},{8,0},{12,4},{1,9},{5,13},{9,1},{13,5},{2,10},{6,14},... | collective-permute-start | bytes 589832 | tf_op jit(solution)/shard_map/ppermute | solution.py:29
  85.3 12.4 %collective-permute-start.33 = (bf16[256,768]{1,0:T(8,128)(2,1)S(1)}, bf16[256,768]{1,0:T(8,128)(2,1)S(1)}, u32[]{:S(2)}, u32[]{:S(2)}) collective-permute-start(bf16[256,768]{1,0:T(8,128)(2,1)S(1)} %get-tuple-element.131.mine_ref), channel_id=1, source_target_pairs={{0,4},{4,0},{8,12},{12,8},{1,5},{5,1},{9,13},{13,9},{2,6},{6,2},{1... | collective-permute-start | bytes 1179656 | tf_op jit(solution)/shard_map/ppermute | solution.py:29
  98.4 21.7 %collective-permute-start.34 = (bf16[256,768]{1,0:T(8,128)(2,1)}, bf16[256,768]{1,0:T(8,128)(2,1)}, u32[]{:S(2)}, u32[]{:S(2)}) collective-permute-start(bf16[256,768]{1,0:T(8,128)(2,1)} %get-tuple-element.140.refs_8_), channel_id=1, source_target_pairs={{0,8},{4,12},{8,0},{12,4},{1,9},{5,13},{9,1},{13,5},{2,10},{6,14},... | collective-permute-start | bytes 1179656 | tf_op jit(solution)/shard_map/ppermute | solution.py:29
  99.6 20.5 %collective-permute-start.35 = (bf16[256,768]{1,0:T(8,128)(2,1)}, bf16[256,768]{1,0:T(8,128)(2,1)}, u32[]{:S(2)}, u32[]{:S(2)}) collective-permute-start(bf16[256,768]{1,0:T(8,128)(2,1)} %get-tuple-element.141.refs_12_), channel_id=1, source_target_pairs={{0,8},{4,12},{8,0},{12,4},{1,9},{5,13},{9,1},{13,5},{2,10},{6,14},... | collective-permute-start | bytes 1179656 | tf_op jit(solution)/shard_map/ppermute | solution.py:29
  104.6 14.3 %all-to-all-start = ((f32[32,1,512]{2,1,0:T(1,128)}), f32[32,1,512]{2,1,0:T(1,128)}, u32[]{:S(2)}, u32[]{:S(2)}) async-start(f32[32,1,512]{2,1,0:T(1,128)} %copy-done.31), calls=%async_computation | async-start | bytes 131072 | tf_op jit(solution)/shard_map/all_to_all | solution.py:365
  128.5 11.7 %collective-permute-start.40 = (bf16[384,768]{1,0:T(8,128)(2,1)S(1)}, bf16[384,768]{1,0:T(8,128)(2,1)S(1)}, u32[]{:S(2)}, u32[]{:S(2)}) collective-permute-start(bf16[384,768]{1,0:T(8,128)(2,1)S(1)} %copy-done.4), channel_id=1, source_target_pairs={{0,4},{4,0},{8,12},{12,8},{1,5},{5,1},{9,13},{13,9},{2,6},{6,2},{1... | collective-permute-start | bytes 1769480 | tf_op jit(solution)/shard_map/ppermute | solution.py:29
  128.8 10.3 %collective-permute-start.45 = (bf16[256,768]{1,0:T(8,128)(2,1)S(1)}, bf16[256,768]{1,0:T(8,128)(2,1)S(1)}, u32[]{:S(2)}, u32[]{:S(2)}) collective-permute-start(bf16[256,768]{1,0:T(8,128)(2,1)S(1)} %multiply_convert_fusion.2.refs_0_.embed_ref), channel_id=1, source_target_pairs={{0,8},{4,12},{8,0},{12,4},{1,9},{5,13},{9,1},{13,5},{2,10},{6,14},... | collective-permute-start | bytes 1179656 | tf_op jit(solution)/shard_map/ppermute | solution.py:29
  130.0 10.4 %collective-permute-start.41 = (bf16[384,768]{1,0:T(8,128)(2,1)S(1)}, bf16[384,768]{1,0:T(8,128)(2,1)S(1)}, u32[]{:S(2)}, u32[]{:S(2)}) collective-permute-start(bf16[384,768]{1,0:T(8,128)(2,1)S(1)} %copy-done.11), channel_id=1, source_target_pairs={{0,4},{4,0},{8,12},{12,8},{1,5},{5,1},{9,13},{13,9},{2,6},{6,2},{1... | collective-permute-start | bytes 1769480 | tf_op jit(solution)/shard_map/ppermute | solution.py:29
  130.7 9.7 %collective-permute-start.42 = (bf16[384,768]{1,0:T(8,128)(2,1)S(1)}, bf16[384,768]{1,0:T(8,128)(2,1)S(1)}, u32[]{:S(2)}, u32[]{:S(2)}) collective-permute-start(bf16[384,768]{1,0:T(8,128)(2,1)S(1)} %copy-done.9), channel_id=1, source_target_pairs={{0,4},{4,0},{8,12},{12,8},{1,5},{5,1},{9,13},{13,9},{2,6},{6,2},{1... | collective-permute-start | bytes 1769480 | tf_op jit(solution)/shard_map/ppermute | solution.py:29
  130.7 9.6 %collective-permute-start.43 = (bf16[384,768]{1,0:T(8,128)(2,1)S(1)}, bf16[384,768]{1,0:T(8,128)(2,1)S(1)}, u32[]{:S(2)}, u32[]{:S(2)}) collective-permute-start(bf16[384,768]{1,0:T(8,128)(2,1)S(1)} %copy-done.13), channel_id=1, source_target_pairs={{0,4},{4,0},{8,12},{12,8},{1,5},{5,1},{9,13},{13,9},{2,6},{6,2},{1... | collective-permute-start | bytes 1769480 | tf_op jit(solution)/shard_map/ppermute | solution.py:29
  146.3 10.4 %collective-permute-start.47 = (bf16[256,768]{1,0:T(8,128)(2,1)S(1)}, bf16[256,768]{1,0:T(8,128)(2,1)S(1)}, u32[]{:S(2)}, u32[]{:S(2)}) collective-permute-start(bf16[256,768]{1,0:T(8,128)(2,1)S(1)} %copy-done.26), channel_id=1, source_target_pairs={{0,8},{4,12},{8,0},{12,4},{1,9},{5,13},{9,1},{13,5},{2,10},{6,14},... | collective-permute-start | bytes 1179656 | tf_op jit(solution)/shard_map/ppermute | solution.py:29
  147.6 14.8 %collective-permute-start.51 = (bf16[192,960]{1,0:T(8,128)(2,1)S(1)}, bf16[192,960]{1,0:T(8,128)(2,1)S(1)}, u32[]{:S(2)}, u32[]{:S(2)}) collective-permute-start(bf16[192,960]{1,0:T(8,128)(2,1)S(1)} %get-tuple-element.178), channel_id=1, source_target_pairs={{0,1},{1,2},{2,3},{3,0},{4,5},{5,6},{6,7},{7,4},{8,9},{9,10},{10,1... | collective-permute-start | bytes 1105928 | tf_op jit(solution)/shard_map/ppermute | solution.py:25
  147.9 33.1 %collective-permute-start.50 = (bf16[192,960]{1,0:T(8,128)(2,1)S(1)}, bf16[192,960]{1,0:T(8,128)(2,1)S(1)}, u32[]{:S(2)}, u32[]{:S(2)}) collective-permute-start(bf16[192,960]{1,0:T(8,128)(2,1)S(1)} %get-tuple-element.177), channel_id=1, source_target_pairs={{0,2},{1,3},{2,0},{3,1},{4,6},{5,7},{6,4},{7,5},{8,10},{9,11},{10,... | collective-permute-start | bytes 1105928 | tf_op jit(solution)/shard_map/ppermute | solution.py:25
  149.6 34.9 %collective-permute-start.49 = (bf16[192,960]{1,0:T(8,128)(2,1)S(1)}, bf16[192,960]{1,0:T(8,128)(2,1)S(1)}, u32[]{:S(2)}, u32[]{:S(2)}) collective-permute-start(bf16[192,960]{1,0:T(8,128)(2,1)S(1)} %get-tuple-element.176), channel_id=1, source_target_pairs={{0,3},{1,0},{2,1},{3,2},{4,7},{5,4},{6,5},{7,6},{8,11},{9,8},{10,9... | collective-permute-start | bytes 1105928 | tf_op jit(solution)/shard_map/ppermute | solution.py:25
  156.7 28.6 %collective-permute-start.48 = (bf16[256,768]{1,0:T(8,128)(2,1)S(1)}, bf16[256,768]{1,0:T(8,128)(2,1)S(1)}, u32[]{:S(2)}, u32[]{:S(2)}) collective-permute-start(bf16[256,768]{1,0:T(8,128)(2,1)S(1)} %collective-permute-done.47.refs_2_), channel_id=1, source_target_pairs={{0,4},{4,0},{8,12},{12,8},{1,5},{5,1},{9,13},{13,9},{2,6},{6,2},{1... | collective-permute-start | bytes 1179656 | tf_op jit(solution)/shard_map/ppermute | solution.py:29
  (66 other events, 565.7 us)
